TPU v7x, 256 devices: a whole 4x4x8 slice. The times are simulated.
256 devices in a mesh: train: 64 (over z_hi, x, y), layer: 2 (over core), query: 2 (over z_lo).
Axes of the slice: x: 4, y: 4, z: 8 (z_hi: 4, z_lo: 2; z = z_hi * 2 + z_lo), core: 2. Of those that a mesh axis runs over, the one named last changes fastest.
Arguments:
- queries: bfloat16 [2, 512, 2, 16384], P('query', 'train', 'layer'), may hold values from -8 to 8
- train_feats: bfloat16 [24576, 2, 16384], P('train', 'layer'), may hold values from -6 to 6
- train_weight: float32 [24576], P('train'), may hold values from 0.25 to 1
Outputs:
- scores: bfloat16 [2, 512, 24576], P('query', None, 'train')
All inputs are finite; a program needn't handle non-finite values.
Results may differ from a plain program's by a relative error of at most 0.001.
Values may be sent and summed in bfloat16 or wider, within the bound.
No kernel may reach another device: no remote copies, remote signals or barrier semaphores. Data moves between devices by JAX's collectives and lax.ppermute only.
A program may use at most 128 MiB of HBM per device.

v0:
```python
import functools

import jax
import jax.numpy as jnp
from jax import lax
from jax.experimental import pallas as pl
from jax.experimental.pallas import tpu as pltpu
from jax.sharding import Mesh, PartitionSpec as P

RING = 4
LANES = 128
DEPTH = 1024
Z_AXES = ("zh", "query")


def shift(v, axis, by):
    size = lax.axis_size(axis)
    return lax.ppermute(v, axis, [(i, (i + by) % size) for i in range(size)])


def row_product(left, right):
    return lax.dot_general(
        left, right, (((1,), (1,)), ((), ())), preferred_element_type=jnp.float32
    )


def z_planes(own):
    half = own.shape[-1] // 2
    up, down = shift(own, Z_AXES, 1), shift(own, Z_AXES, -1)
    up, down = shift(up, Z_AXES, 1), shift(down, Z_AXES, -1)
    far_up, far_down = shift(up[..., :half], Z_AXES, 1), shift(down[..., half:], Z_AXES, -1)
    far_up, far_down = shift(far_up, Z_AXES, 1), shift(far_down, Z_AXES, -1)
    return own, up, down, far_up, far_down


def ring(v, axis):
    n = v.shape[0] // 2
    left, right = shift(v, axis, 1), shift(v, axis, -1)
    return v, left, right, shift(left[:n], axis, 1), shift(right[n:], axis, -1)


def add_kernel(offsets, n_parts, first, *refs):
    count = len(offsets) * n_parts
    a_refs, b_refs = refs[:count], refs[count : 2 * count]
    a_store, b_store = refs[2 * count : 2 * count + 2]
    out = refs[-1]
    n_out = a_store.shape[0]

    @pl.when(pl.program_id(0) == 0)
    def _():
        if first:
            out[...] = jnp.zeros_like(out)
        else:
            out[...] = refs[2 * count + 2][...]

    def terms(parts, store):
        rows = jnp.concatenate([p[...] for p in parts], 0)
        product = row_product(rows, store[...])
        squares = jnp.zeros((rows.shape[0], LANES), jnp.float32)
        for i in range(0, rows.shape[1], LANES):
            wide = rows[:, i : i + LANES].astype(jnp.float32)
            squares += wide * wide
        return product, squares

    a_product, a_squares = terms(a_refs, a_store)
    b_product, b_squares = terms(b_refs, b_store)
    block = a_product.shape[0] // len(offsets)
    strip = block // RING
    for i, offset in enumerate(offsets):
        rows, source = pl.ds(offset * block, block), slice(i * block, (i + 1) * block)
        out[rows, :n_out] += a_product[source]
        out[rows, n_out:] += a_squares[source]
        for j in range(RING):
            rows = pl.ds(j * block + offset * strip, strip)
            source = slice(i * block + j * strip, i * block + (j + 1) * strip)
            out[rows, :n_out] += b_product[source]
            out[rows, n_out:] += b_squares[source]


def add_blocks(sums, offsets, a_parts, b_parts, store):
    n_out = store.shape[0]
    flat = lambda v: v.reshape(-1, v.shape[-1])
    a_parts, b_parts = [flat(v) for v in a_parts], [flat(v) for v in b_parts]
    steps = a_parts[0].shape[1] // DEPTH
    n_rows = sum(v.shape[0] for v in a_parts)
    shape = (RING * n_rows // len(offsets), n_out + LANES)
    part_specs = [pl.BlockSpec((v.shape[0], DEPTH), lambda k: (0, k)) for v in a_parts + b_parts]
    store_specs = [
        pl.BlockSpec((n_out, DEPTH), lambda k: (0, k)),
        pl.BlockSpec((n_out, DEPTH), lambda k: (0, k + steps)),
    ]
    whole = pl.BlockSpec(shape, lambda k: (0, 0))
    earlier = [] if sums is None else [sums]
    return pl.pallas_call(
        functools.partial(
            add_kernel, offsets, len(a_parts) // len(offsets), sums is None
        ),
        grid=(steps,),
        out_shape=jax.ShapeDtypeStruct(shape, jnp.float32),
        in_specs=part_specs + store_specs + [whole] * len(earlier),
        out_specs=whole,
        compiler_params=pltpu.CompilerParams(vmem_limit_bytes=24 * 1024 * 1024),
        cost_estimate=pl.CostEstimate(
            flops=4 * n_rows * steps * DEPTH * n_out,
            bytes_accessed=2 * steps * DEPTH * (2 * n_out + 2 * n_rows),
            transcendentals=0,
        ),
    )(*a_parts, *b_parts, store, store, *earlier)


def finish_kernel(order, mine, other, weight, out):
    n_out = out.shape[1]

    def body(i, carry):
        halves = []
        for j in range(2):
            rows = pl.ds(pl.multiple_of(order[2 * i + j] * 8, 8), 8)
            both = mine[rows, :] + other[rows, :]
            norm = jnp.sum(both[:, n_out:], axis=1, keepdims=True)
            halves.append(both[:, :n_out] * weight[...] * lax.rsqrt(norm + 1e-06))
        out[pl.ds(pl.multiple_of(i * 16, 16), 16), :] = jnp.concatenate(halves, 0).astype(out.dtype)
        return carry

    lax.fori_loop(0, out.shape[0] // 16, body, 0, unroll=4)


def absolute_order(zh, x, y):
    r = jnp.arange(RING, dtype=jnp.int32)

    def place(at):
        off = (r - at) % RING
        return jnp.where(off == 0, 0, jnp.where(off == 3, 1, off + 1))

    pz, px, py = place(zh), place(x), place(y)
    return (py[None, None, :] * 16 + px[None, :, None] * 4 + pz[:, None, None]).reshape(-1)


def per_device(queries, train_feats, train_weight):
    own = queries[0, :, 0, :][None]
    store = train_feats[:, 0, :]
    half = own.shape[-1] // 2
    z = z_planes(own)
    planes = jnp.concatenate([z[0], z[1], z[2], jnp.concatenate([z[3], z[4]], -1)], 0)
    first = jnp.concatenate(ring(planes[..., :half], "x"), 0)
    second = jnp.concatenate(ring(planes[..., half:], "y"), 0)
    a, b = ring(first, "y"), ring(second, "x")
    sums = add_blocks(None, (0,), a[:1], b[:1], store)
    sums = add_blocks(sums, (1, 2), a[1:3], b[1:3], store)
    sums = add_blocks(sums, (3,), a[3:], b[3:], store)
    other = shift(sums, "layer", 1)
    order = absolute_order(*(lax.axis_index(n) for n in ("zh", "x", "y")))
    vmem = pl.BlockSpec(memory_space=pltpu.VMEM)
    result = pl.pallas_call(
        finish_kernel,
        out_shape=jax.ShapeDtypeStruct((sums.shape[0], store.shape[0]), jnp.bfloat16),
        in_specs=[pl.BlockSpec(memory_space=pltpu.SMEM)] + [vmem] * 3,
        out_specs=vmem,
        compiler_params=pltpu.CompilerParams(vmem_limit_bytes=16 * 1024 * 1024),
    )(order, sums, other, train_weight[None, :])
    return result[None, :, :]


def solution(mesh):
    fine = Mesh(
        mesh.devices.reshape(RING, RING, RING, mesh.shape["layer"], mesh.shape["query"]),
        ("zh", "x", "y", "layer", "query"),
    )
    train = ("zh", "x", "y")
    return jax.shard_map(
        per_device,
        mesh=fine,
        in_specs=(P("query", train, "layer", None), P(train, "layer", None), P(train)),
        out_specs=P("query", None, train),
        check_vma=False,
    )
```

profile of v0, /device:TPU:1, one launch (start us, length us, event | category | flops | bytes accessed | tf_op | source)
XLA Modules:
  0.0 138.3 jit_solution(632879276836426719)
XLA Ops:
  0.0 2.5 %collective-permute-start = (bf16[1,8,16384]{2,1,0:T(8,128)(2,1)}, bf16[1,8,16384]{2,1,0:T(8,128)(2,1)S(1)}, u32[]{:S(2)}, u32[]{:S(2)}) collective-permute-start(bf16[1,8,16384]{2,1,0:T(8,128)(2,1)} %bitcast.29), channel_id=1, source_target_pairs={{0,1},{1,64},{64,65},{65,128},{128,129},{129,192},{192,193},{193,0... | collective-permute-start | bytes 786440 | tf_op jit(solution)/shard_map/ppermute | solution.py:18
  2.5 3.9 %collective-permute-start.2 = (bf16[1,8,16384]{2,1,0:T(8,128)(2,1)}, bf16[1,8,16384]{2,1,0:T(8,128)(2,1)S(1)}, u32[]{:S(2)}, u32[]{:S(2)}) collective-permute-start(bf16[1,8,16384]{2,1,0:T(8,128)(2,1)} %bitcast.30), channel_id=1, source_target_pairs={{0,193},{1,0},{64,1},{65,64},{128,65},{129,128},{192,129},{193,192... | collective-permute-start | bytes 786440 | tf_op jit(solution)/shard_map/ppermute | solution.py:18
  6.4 6.2 %collective-permute-done = bf16[1,8,16384]{2,1,0:T(8,128)(2,1)S(1)} collective-permute-done((bf16[1,8,16384]{2,1,0:T(8,128)(2,1)}, bf16[1,8,16384]{2,1,0:T(8,128)(2,1)S(1)}, u32[]{:S(2)}, u32[]{:S(2)}) %collective-permute-start) | collective-permute-done | bytes 262176 | tf_op jit(solution)/shard_map/ppermute | solution.py:18
  12.7 2.7 %collective-permute-start.3 = (bf16[1,8,16384]{2,1,0:T(8,128)(2,1)S(1)}, bf16[1,8,16384]{2,1,0:T(8,128)(2,1)S(1)}, u32[]{:S(2)}, u32[]{:S(2)}) collective-permute-start(bf16[1,8,16384]{2,1,0:T(8,128)(2,1)S(1)} %collective-permute-done.2), channel_id=1, source_target_pairs={{0,193},{1,0},{64,1},{65,64},{128,65},{129,128},{192,129},{193,192... | collective-permute-start | bytes 786440 | tf_op jit(solution)/shard_map/ppermute | solution.py:18
  15.3 5.1 %collective-permute-done.1 = bf16[1,8,16384]{2,1,0:T(8,128)(2,1)S(1)} collective-permute-done((bf16[1,8,16384]{2,1,0:T(8,128)(2,1)S(1)}, bf16[1,8,16384]{2,1,0:T(8,128)(2,1)S(1)}, u32[]{:S(2)}, u32[]{:S(2)}) %collective-permute-start.1) | collective-permute-done | bytes 262176 | tf_op jit(solution)/shard_map/ppermute | solution.py:18
  20.6 2.7 %collective-permute-start.6 = (bf16[1,8,8192]{2,1,0:T(8,128)(2,1)S(1)}, bf16[1,8,8192]{2,1,0:T(8,128)(2,1)S(1)}, u32[]{:S(2)}, u32[]{:S(2)}) collective-permute-start(bf16[1,8,8192]{2,1,0:T(8,128)(2,1)S(1)} %slice.49), channel_id=1, source_target_pairs={{0,193},{1,0},{64,1},{65,64},{128,65},{129,128},{192,129},{193,192... | collective-permute-start | bytes 393224 | tf_op jit(solution)/shard_map/ppermute | solution.py:18
  23.3 2.3 %collective-permute-done.4 = bf16[1,8,8192]{2,1,0:T(8,128)(2,1)S(1)} collective-permute-done((bf16[1,8,8192]{2,1,0:T(8,128)(2,1)S(1)}, bf16[1,8,8192]{2,1,0:T(8,128)(2,1)S(1)}, u32[]{:S(2)}, u32[]{:S(2)}) %collective-permute-start.4) | collective-permute-done | bytes 131104 | tf_op jit(solution)/shard_map/ppermute | solution.py:18
  25.6 2.8 %collective-permute-start.7 = (bf16[1,8,8192]{2,1,0:T(8,128)(2,1)S(1)}, bf16[1,8,8192]{2,1,0:T(8,128)(2,1)S(1)}, u32[]{:S(2)}, u32[]{:S(2)}) collective-permute-start(bf16[1,8,8192]{2,1,0:T(8,128)(2,1)S(1)} %collective-permute-done.6), channel_id=1, source_target_pairs={{0,193},{1,0},{64,1},{65,64},{128,65},{129,128},{192,129},{193,192... | collective-permute-start | bytes 393224 | tf_op jit(solution)/shard_map/ppermute | solution.py:18
  28.3 2.3 %collective-permute-done.5 = bf16[1,8,8192]{2,1,0:T(8,128)(2,1)S(1)} collective-permute-done((bf16[1,8,8192]{2,1,0:T(8,128)(2,1)S(1)}, bf16[1,8,8192]{2,1,0:T(8,128)(2,1)S(1)}, u32[]{:S(2)}, u32[]{:S(2)}) %collective-permute-start.5) | collective-permute-done | bytes 131104 | tf_op jit(solution)/shard_map/ppermute | solution.py:18
  31.9 1.4 collective-permute-start.16
  33.2 1.5 %collective-permute-start.17 = (bf16[4,8,8192]{2,1,0:T(8,128)(2,1)S(1)}, bf16[4,8,8192]{2,1,0:T(8,128)(2,1)S(1)}, u32[]{:S(2)}, u32[]{:S(2)}) collective-permute-start(bf16[4,8,8192]{2,1,0:T(8,128)(2,1)S(1)} %get-tuple-element.5), channel_id=1, source_target_pairs={{0,12},{4,0},{8,4},{12,8},{1,13},{5,1},{9,5},{13,9},{2,14},{6,2},{... | collective-permute-start | bytes 1572872 | tf_op jit(solution)/shard_map/ppermute | solution.py:18
  36.0 1.5 %collective-permute-start.9 = (bf16[4,8,8192]{2,1,0:T(8,128)(2,1)S(1)}, bf16[4,8,8192]{2,1,0:T(8,128)(2,1)S(1)}, u32[]{:S(2)}, u32[]{:S(2)}) collective-permute-start(bf16[4,8,8192]{2,1,0:T(8,128)(2,1)S(1)} %get-tuple-element.8), channel_id=1, source_target_pairs={{0,48},{16,0},{32,16},{48,32},{1,49},{17,1},{33,17},{49,33},{2,50}... | collective-permute-start | bytes 1572872 | tf_op jit(solution)/shard_map/ppermute | solution.py:18
  37.4 4.8 %collective-permute-done.16 = bf16[4,8,8192]{2,1,0:T(8,128)(2,1)S(1)} collective-permute-done((bf16[4,8,8192]{2,1,0:T(8,128)(2,1)S(1)}, bf16[4,8,8192]{2,1,0:T(8,128)(2,1)S(1)}, u32[]{:S(2)}, u32[]{:S(2)}) %collective-permute-start.16) | collective-permute-done | bytes 524320 | tf_op jit(solution)/shard_map/ppermute | solution.py:18
  42.4 2.7 %collective-permute-start.19 = (bf16[2,8,8192]{2,1,0:T(8,128)(2,1)S(1)}, bf16[2,8,8192]{2,1,0:T(8,128)(2,1)S(1)}, u32[]{:S(2)}, u32[]{:S(2)}) collective-permute-start(bf16[2,8,8192]{2,1,0:T(8,128)(2,1)S(1)} %slice.57), channel_id=1, source_target_pairs={{0,12},{4,0},{8,4},{12,8},{1,13},{5,1},{9,5},{13,9},{2,14},{6,2},{... | collective-permute-start | bytes 786440 | tf_op jit(solution)/shard_map/ppermute | solution.py:18
  45.1 1.3 collective-permute-start.10
  46.5 1.7 %collective-permute-start.11 = (bf16[2,8,8192]{2,1,0:T(8,128)(2,1)S(1)}, bf16[2,8,8192]{2,1,0:T(8,128)(2,1)S(1)}, u32[]{:S(2)}, u32[]{:S(2)}) collective-permute-start(bf16[2,8,8192]{2,1,0:T(8,128)(2,1)S(1)} %slice.52), channel_id=1, source_target_pairs={{0,48},{16,0},{32,16},{48,32},{1,49},{17,1},{33,17},{49,33},{2,50}... | collective-permute-start | bytes 786440 | tf_op jit(solution)/shard_map/ppermute | solution.py:18
  48.4 1.6 %collective-permute-done.18 = bf16[2,8,8192]{2,1,0:T(8,128)(2,1)S(1)} collective-permute-done((bf16[2,8,8192]{2,1,0:T(8,128)(2,1)S(1)}, bf16[2,8,8192]{2,1,0:T(8,128)(2,1)S(1)}, u32[]{:S(2)}, u32[]{:S(2)}) %collective-permute-start.18) | collective-permute-done | bytes 262176 | tf_op jit(solution)/shard_map/ppermute | solution.py:18
  50.0 1.3 collective-permute-start.20
  51.3 1.5 %collective-permute-start.22 = (bf16[16,8,8192]{2,1,0:T(8,128)(2,1)S(1)}, bf16[16,8,8192]{2,1,0:T(8,128)(2,1)S(1)}, u32[]{:S(2)}, u32[]{:S(2)}) collective-permute-start(bf16[16,8,8192]{2,1,0:T(8,128)(2,1)S(1)} %constant_dynamic-update-slice_fusion.5), channel_id=1, source_target_pairs={{0,48},{16,0},{32,16},{48,32},{1,49},{17,1},{33,17},{49,33},{2,50}... | collective-permute-start | bytes 6291464 | tf_op jit(solution)/shard_map/ppermute | solution.py:18
  52.8 1.4 collective-permute-start.12
  54.2 1.5 %collective-permute-start.14 = (bf16[16,8,8192]{2,1,0:T(8,128)(2,1)S(1)}, bf16[16,8,8192]{2,1,0:T(8,128)(2,1)S(1)}, u32[]{:S(2)}, u32[]{:S(2)}) collective-permute-start(bf16[16,8,8192]{2,1,0:T(8,128)(2,1)S(1)} %constant_dynamic-update-slice_fusion), channel_id=1, source_target_pairs={{0,12},{4,0},{8,4},{12,8},{1,13},{5,1},{9,5},{13,9},{2,14},{6,2},{... | collective-permute-start | bytes 6291464 | tf_op jit(solution)/shard_map/ppermute | solution.py:18
  55.7 40.9 %collective-permute-done.20 = bf16[16,8,8192]{2,1,0:T(8,128)(2,1)S(1)} collective-permute-done((bf16[16,8,8192]{2,1,0:T(8,128)(2,1)S(1)}, bf16[16,8,8192]{2,1,0:T(8,128)(2,1)S(1)}, u32[]{:S(2)}, u32[]{:S(2)}) %collective-permute-start.20) | collective-permute-done | bytes 2097184 | tf_op jit(solution)/shard_map/ppermute | solution.py:18
  96.9 2.7 %collective-permute-start.23 = (bf16[8,8,8192]{2,1,0:T(8,128)(2,1)S(1)}, bf16[8,8,8192]{2,1,0:T(8,128)(2,1)S(1)}, u32[]{:S(2)}, u32[]{:S(2)}) collective-permute-start(bf16[8,8,8192]{2,1,0:T(8,128)(2,1)S(1)} %slice.59), channel_id=1, source_target_pairs={{0,48},{16,0},{32,16},{48,32},{1,49},{17,1},{33,17},{49,33},{2,50}... | collective-permute-start | bytes 3145736 | tf_op jit(solution)/shard_map/ppermute | solution.py:18
  99.7 2.2 %collective-permute-start.13 = (bf16[8,8,8192]{2,1,0:T(8,128)(2,1)S(1)}, bf16[8,8,8192]{2,1,0:T(8,128)(2,1)S(1)}, u32[]{:S(2)}, u32[]{:S(2)}) collective-permute-start(bf16[8,8,8192]{2,1,0:T(8,128)(2,1)S(1)} %slice.53), channel_id=1, source_target_pairs={{0,4},{4,8},{8,12},{12,0},{1,5},{5,9},{9,13},{13,1},{2,6},{6,10},{... | collective-permute-start | bytes 3145736 | tf_op jit(solution)/shard_map/ppermute | solution.py:18
  101.9 1.8 %collective-permute-start.15 = (bf16[8,8,8192]{2,1,0:T(8,128)(2,1)S(1)}, bf16[8,8,8192]{2,1,0:T(8,128)(2,1)S(1)}, u32[]{:S(2)}, u32[]{:S(2)}) collective-permute-start(bf16[8,8,8192]{2,1,0:T(8,128)(2,1)S(1)} %slice.54), channel_id=1, source_target_pairs={{0,12},{4,0},{8,4},{12,8},{1,13},{5,1},{9,5},{13,9},{2,14},{6,2},{... | collective-permute-start | bytes 3145736 | tf_op jit(solution)/shard_map/ppermute | solution.py:18
  103.7 6.2 %shard_map.37.refs_6_ = f32[512,512]{1,0:T(8,128)S(1)} custom-call(bf16[128,8192]{1,0:T(8,128)(2,1)S(1)} %bitcast.23, bf16[128,8192]{1,0:T(8,128)(2,1)S(1)} %bitcast.24, bf16[384,16384]{1,0:T(8,128)(2,1)S(1)} %bitcast.13, bf16[384,16384]{1,0:T(8,128)(2,1)S(1)} %bitcast.14), custom_call_target="tpu_custom_call" | custom-call | flops 1610612736 | bytes 16777216 | tf_op jit(solution)/shard_map/pallas_call | solution.py:94
  109.9 7.6 %shard_map.38.refs_6_ = f32[512,512]{1,0:T(8,128)S(1)} custom-call(bf16[128,8192]{1,0:T(8,128)(2,1)S(1)} %bitcast.21, bf16[128,8192]{1,0:T(8,128)(2,1)S(1)} %bitcast.22, bf16[128,8192]{1,0:T(8,128)(2,1)S(1)} %bitcast.19, bf16[128,8192]{1,0:T(8,128)(2,1)S(1)} %bitcast.20, bf16[384,16384]{1,0:T(8,128)(2,1)S(1)} %bitcast.15, bf16[384,16384]{1,0:T(8,128)(2,1)S(1)} %bitcast.16, ...), custom_call_target="tpu_custom_call" | custom-call | flops 3221225472 | bytes 20971520 | tf_op jit(solution)/shard_map/pallas_call | solution.py:94
  118.2 2.4 %collective-permute-done.13 = bf16[8,8,8192]{2,1,0:T(8,128)(2,1)S(1)} collective-permute-done((bf16[8,8,8192]{2,1,0:T(8,128)(2,1)S(1)}, bf16[8,8,8192]{2,1,0:T(8,128)(2,1)S(1)}, u32[]{:S(2)}, u32[]{:S(2)}) %collective-permute-start.13) | collective-permute-done | bytes 1048608 | tf_op jit(solution)/shard_map/ppermute | solution.py:18
  120.8 6.2 %shard_map.39.mine = f32[512,512]{1,0:T(8,128)S(1)} custom-call(bf16[64,8192]{1,0:T(8,128)(2,1)S(1)} %bitcast.27, bf16[64,8192]{1,0:T(8,128)(2,1)S(1)} %bitcast.28, bf16[64,8192]{1,0:T(8,128)(2,1)S(1)} %bitcast.25, bf16[64,8192]{1,0:T(8,128)(2,1)S(1)} %bitcast.26, bf16[384,16384]{1,0:T(8,128)(2,1)S(1)} %bitcast.17, bf16[384,16384]{1,0:T(8,128)(2,1)S(1)} %bitcast.18, ...), custom_call_target="tpu_custom_call" | custom-call | flops 1610612736 | bytes 16777216 | tf_op jit(solution)/shard_map/pallas_call | solution.py:94
  127.1 6.9 %collective-permute-start.24 = (f32[512,512]{1,0:T(8,128)S(1)}, f32[512,512]{1,0:T(8,128)S(1)}, u32[]{:S(2)}, u32[]{:S(2)}) collective-permute-start(f32[512,512]{1,0:T(8,128)S(1)} %shard_map.39.mine), channel_id=1, source_target_pairs={{0,2},{2,0},{1,3},{3,1},{4,6},{6,4},{5,7},{7,5},{8,10},{10,8},{9,1... | collective-permute-start | bytes 3145736 | tf_op jit(solution)/shard_map/ppermute | solution.py:18
  134.2 2.0 %collective-permute-done.24.other = f32[512,512]{1,0:T(8,128)S(1)} collective-permute-done((f32[512,512]{1,0:T(8,128)S(1)}, f32[512,512]{1,0:T(8,128)S(1)}, u32[]{:S(2)}, u32[]{:S(2)}) %collective-permute-start.24) | collective-permute-done | bytes 1048608 | tf_op jit(solution)/shard_map/ppermute | solution.py:18
  136.2 2.1 %shard_map.40 = bf16[512,384]{1,0:T(8,128)(2,1)} custom-call(s32[64]{0:T(128)S(1)} %add.94.order, f32[512,512]{1,0:T(8,128)S(1)} %shard_map.39.mine, f32[512,512]{1,0:T(8,128)S(1)} %collective-permute-done.24.other, f32[1,384]{1,0:T(1,128)S(1)} %broadcast_in_dim.19.weight), custom_call_target="tpu_custom_call" | custom-call | tf_op jit(solution)/shard_map/pallas_call | solution.py:153
  (52 shorter events, 4.5 us)
Async XLA Ops:
  0.0 12.6 %collective-permute-start = (bf16[1,8,16384]{2,1,0:T(8,128)(2,1)}, bf16[1,8,16384]{2,1,0:T(8,128)(2,1)S(1)}, u32[]{:S(2)}, u32[]{:S(2)}) collective-permute-start(bf16[1,8,16384]{2,1,0:T(8,128)(2,1)} %bitcast.29), channel_id=1, source_target_pairs={{0,1},{1,64},{64,65},{65,128},{128,129},{129,192},{192,193},{193,0... | collective-permute-start | bytes 786440 | tf_op jit(solution)/shard_map/ppermute | solution.py:18
  2.5 10.2 %collective-permute-start.2 = (bf16[1,8,16384]{2,1,0:T(8,128)(2,1)}, bf16[1,8,16384]{2,1,0:T(8,128)(2,1)S(1)}, u32[]{:S(2)}, u32[]{:S(2)}) collective-permute-start(bf16[1,8,16384]{2,1,0:T(8,128)(2,1)} %bitcast.30), channel_id=1, source_target_pairs={{0,193},{1,0},{64,1},{65,64},{128,65},{129,128},{192,129},{193,192... | collective-permute-start | bytes 786440 | tf_op jit(solution)/shard_map/ppermute | solution.py:18
  12.6 7.8 %collective-permute-start.1 = (bf16[1,8,16384]{2,1,0:T(8,128)(2,1)S(1)}, bf16[1,8,16384]{2,1,0:T(8,128)(2,1)S(1)}, u32[]{:S(2)}, u32[]{:S(2)}) collective-permute-start(bf16[1,8,16384]{2,1,0:T(8,128)(2,1)S(1)} %collective-permute-done), channel_id=1, source_target_pairs={{0,1},{1,64},{64,65},{65,128},{128,129},{129,192},{192,193},{193,0... | collective-permute-start | bytes 786440 | tf_op jit(solution)/shard_map/ppermute | solution.py:18
  12.7 7.9 %collective-permute-start.3 = (bf16[1,8,16384]{2,1,0:T(8,128)(2,1)S(1)}, bf16[1,8,16384]{2,1,0:T(8,128)(2,1)S(1)}, u32[]{:S(2)}, u32[]{:S(2)}) collective-permute-start(bf16[1,8,16384]{2,1,0:T(8,128)(2,1)S(1)} %collective-permute-done.2), channel_id=1, source_target_pairs={{0,193},{1,0},{64,1},{65,64},{128,65},{129,128},{192,129},{193,192... | collective-permute-start | bytes 786440 | tf_op jit(solution)/shard_map/ppermute | solution.py:18
  20.4 5.1 %collective-permute-start.4 = (bf16[1,8,8192]{2,1,0:T(8,128)(2,1)S(1)}, bf16[1,8,8192]{2,1,0:T(8,128)(2,1)S(1)}, u32[]{:S(2)}, u32[]{:S(2)}) collective-permute-start(bf16[1,8,8192]{2,1,0:T(8,128)(2,1)S(1)} %slice.48), channel_id=1, source_target_pairs={{0,1},{1,64},{64,65},{65,128},{128,129},{129,192},{192,193},{193,0... | collective-permute-start | bytes 393224 | tf_op jit(solution)/shard_map/ppermute | solution.py:18
  20.6 5.0 %collective-permute-start.6 = (bf16[1,8,8192]{2,1,0:T(8,128)(2,1)S(1)}, bf16[1,8,8192]{2,1,0:T(8,128)(2,1)S(1)}, u32[]{:S(2)}, u32[]{:S(2)}) collective-permute-start(bf16[1,8,8192]{2,1,0:T(8,128)(2,1)S(1)} %slice.49), channel_id=1, source_target_pairs={{0,193},{1,0},{64,1},{65,64},{128,65},{129,128},{192,129},{193,192... | collective-permute-start | bytes 393224 | tf_op jit(solution)/shard_map/ppermute | solution.py:18
  25.5 5.0 %collective-permute-start.5 = (bf16[1,8,8192]{2,1,0:T(8,128)(2,1)S(1)}, bf16[1,8,8192]{2,1,0:T(8,128)(2,1)S(1)}, u32[]{:S(2)}, u32[]{:S(2)}) collective-permute-start(bf16[1,8,8192]{2,1,0:T(8,128)(2,1)S(1)} %collective-permute-done.4), channel_id=1, source_target_pairs={{0,1},{1,64},{64,65},{65,128},{128,129},{129,192},{192,193},{193,0... | collective-permute-start | bytes 393224 | tf_op jit(solution)/shard_map/ppermute | solution.py:18
  25.6 5.0 %collective-permute-start.7 = (bf16[1,8,8192]{2,1,0:T(8,128)(2,1)S(1)}, bf16[1,8,8192]{2,1,0:T(8,128)(2,1)S(1)}, u32[]{:S(2)}, u32[]{:S(2)}) collective-permute-start(bf16[1,8,8192]{2,1,0:T(8,128)(2,1)S(1)} %collective-permute-done.6), channel_id=1, source_target_pairs={{0,193},{1,0},{64,1},{65,64},{128,65},{129,128},{192,129},{193,192... | collective-permute-start | bytes 393224 | tf_op jit(solution)/shard_map/ppermute | solution.py:18
  31.9 10.4 %collective-permute-start.16 = (bf16[4,8,8192]{2,1,0:T(8,128)(2,1)S(1)}, bf16[4,8,8192]{2,1,0:T(8,128)(2,1)S(1)}, u32[]{:S(2)}, u32[]{:S(2)}) collective-permute-start(bf16[4,8,8192]{2,1,0:T(8,128)(2,1)S(1)} %get-tuple-element.5), channel_id=1, source_target_pairs={{0,4},{4,8},{8,12},{12,0},{1,5},{5,9},{9,13},{13,1},{2,6},{6,10},{... | collective-permute-start | bytes 1572872 | tf_op jit(solution)/shard_map/ppermute | solution.py:18
  33.2 9.1 %collective-permute-start.17 = (bf16[4,8,8192]{2,1,0:T(8,128)(2,1)S(1)}, bf16[4,8,8192]{2,1,0:T(8,128)(2,1)S(1)}, u32[]{:S(2)}, u32[]{:S(2)}) collective-permute-start(bf16[4,8,8192]{2,1,0:T(8,128)(2,1)S(1)} %get-tuple-element.5), channel_id=1, source_target_pairs={{0,12},{4,0},{8,4},{12,8},{1,13},{5,1},{9,5},{13,9},{2,14},{6,2},{... | collective-permute-start | bytes 1572872 | tf_op jit(solution)/shard_map/ppermute | solution.py:18
  34.8 10.4 %collective-permute-start.8 = (bf16[4,8,8192]{2,1,0:T(8,128)(2,1)S(1)}, bf16[4,8,8192]{2,1,0:T(8,128)(2,1)S(1)}, u32[]{:S(2)}, u32[]{:S(2)}) collective-permute-start(bf16[4,8,8192]{2,1,0:T(8,128)(2,1)S(1)} %get-tuple-element.8), channel_id=1, source_target_pairs={{0,16},{16,32},{32,48},{48,0},{1,17},{17,33},{33,49},{49,1},{2,18}... | collective-permute-start | bytes 1572872 | tf_op jit(solution)/shard_map/ppermute | solution.py:18
  36.0 10.5 %collective-permute-start.9 = (bf16[4,8,8192]{2,1,0:T(8,128)(2,1)S(1)}, bf16[4,8,8192]{2,1,0:T(8,128)(2,1)S(1)}, u32[]{:S(2)}, u32[]{:S(2)}) collective-permute-start(bf16[4,8,8192]{2,1,0:T(8,128)(2,1)S(1)} %get-tuple-element.8), channel_id=1, source_target_pairs={{0,48},{16,0},{32,16},{48,32},{1,49},{17,1},{33,17},{49,33},{2,50}... | collective-permute-start | bytes 1572872 | tf_op jit(solution)/shard_map/ppermute | solution.py:18
  42.3 7.7 %collective-permute-start.18 = (bf16[2,8,8192]{2,1,0:T(8,128)(2,1)S(1)}, bf16[2,8,8192]{2,1,0:T(8,128)(2,1)S(1)}, u32[]{:S(2)}, u32[]{:S(2)}) collective-permute-start(bf16[2,8,8192]{2,1,0:T(8,128)(2,1)S(1)} %slice.56), channel_id=1, source_target_pairs={{0,4},{4,8},{8,12},{12,0},{1,5},{5,9},{9,13},{13,1},{2,6},{6,10},{... | collective-permute-start | bytes 786440 | tf_op jit(solution)/shard_map/ppermute | solution.py:18
  42.4 7.6 %collective-permute-start.19 = (bf16[2,8,8192]{2,1,0:T(8,128)(2,1)S(1)}, bf16[2,8,8192]{2,1,0:T(8,128)(2,1)S(1)}, u32[]{:S(2)}, u32[]{:S(2)}) collective-permute-start(bf16[2,8,8192]{2,1,0:T(8,128)(2,1)S(1)} %slice.57), channel_id=1, source_target_pairs={{0,12},{4,0},{8,4},{12,8},{1,13},{5,1},{9,5},{13,9},{2,14},{6,2},{... | collective-permute-start | bytes 786440 | tf_op jit(solution)/shard_map/ppermute | solution.py:18
  45.1 7.6 %collective-permute-start.10 = (bf16[2,8,8192]{2,1,0:T(8,128)(2,1)S(1)}, bf16[2,8,8192]{2,1,0:T(8,128)(2,1)S(1)}, u32[]{:S(2)}, u32[]{:S(2)}) collective-permute-start(bf16[2,8,8192]{2,1,0:T(8,128)(2,1)S(1)} %slice.51), channel_id=1, source_target_pairs={{0,16},{16,32},{32,48},{48,0},{1,17},{17,33},{33,49},{49,1},{2,18}... | collective-permute-start | bytes 786440 | tf_op jit(solution)/shard_map/ppermute | solution.py:18
  46.5 6.3 %collective-permute-start.11 = (bf16[2,8,8192]{2,1,0:T(8,128)(2,1)S(1)}, bf16[2,8,8192]{2,1,0:T(8,128)(2,1)S(1)}, u32[]{:S(2)}, u32[]{:S(2)}) collective-permute-start(bf16[2,8,8192]{2,1,0:T(8,128)(2,1)S(1)} %slice.52), channel_id=1, source_target_pairs={{0,48},{16,0},{32,16},{48,32},{1,49},{17,1},{33,17},{49,33},{2,50}... | collective-permute-start | bytes 786440 | tf_op jit(solution)/shard_map/ppermute | solution.py:18
  48.3 55.4 %copy-start = (bf16[384,1,16384]{2,0,1:T(8,128)(2,1)S(1)}, bf16[384,1,16384]{2,0,1:T(8,128)(2,1)}, u32[]{:S(2)}) copy-start(bf16[384,1,16384]{2,0,1:T(8,128)(2,1)} %param.4) | copy-start | bytes 37748740
  50.0 46.6 %collective-permute-start.20 = (bf16[16,8,8192]{2,1,0:T(8,128)(2,1)S(1)}, bf16[16,8,8192]{2,1,0:T(8,128)(2,1)S(1)}, u32[]{:S(2)}, u32[]{:S(2)}) collective-permute-start(bf16[16,8,8192]{2,1,0:T(8,128)(2,1)S(1)} %constant_dynamic-update-slice_fusion.5), channel_id=1, source_target_pairs={{0,16},{16,32},{32,48},{48,0},{1,17},{17,33},{33,49},{49,1},{2,18}... | collective-permute-start | bytes 6291464 | tf_op jit(solution)/shard_map/ppermute | solution.py:18
  51.3 45.5 %collective-permute-start.22 = (bf16[16,8,8192]{2,1,0:T(8,128)(2,1)S(1)}, bf16[16,8,8192]{2,1,0:T(8,128)(2,1)S(1)}, u32[]{:S(2)}, u32[]{:S(2)}) collective-permute-start(bf16[16,8,8192]{2,1,0:T(8,128)(2,1)S(1)} %constant_dynamic-update-slice_fusion.5), channel_id=1, source_target_pairs={{0,48},{16,0},{32,16},{48,32},{1,49},{17,1},{33,17},{49,33},{2,50}... | collective-permute-start | bytes 6291464 | tf_op jit(solution)/shard_map/ppermute | solution.py:18
  52.8 46.8 %collective-permute-start.12 = (bf16[16,8,8192]{2,1,0:T(8,128)(2,1)S(1)}, bf16[16,8,8192]{2,1,0:T(8,128)(2,1)S(1)}, u32[]{:S(2)}, u32[]{:S(2)}) collective-permute-start(bf16[16,8,8192]{2,1,0:T(8,128)(2,1)S(1)} %constant_dynamic-update-slice_fusion), channel_id=1, source_target_pairs={{0,4},{4,8},{8,12},{12,0},{1,5},{5,9},{9,13},{13,1},{2,6},{6,10},{... | collective-permute-start | bytes 6291464 | tf_op jit(solution)/shard_map/ppermute | solution.py:18
  54.2 47.6 %collective-permute-start.14 = (bf16[16,8,8192]{2,1,0:T(8,128)(2,1)S(1)}, bf16[16,8,8192]{2,1,0:T(8,128)(2,1)S(1)}, u32[]{:S(2)}, u32[]{:S(2)}) collective-permute-start(bf16[16,8,8192]{2,1,0:T(8,128)(2,1)S(1)} %constant_dynamic-update-slice_fusion), channel_id=1, source_target_pairs={{0,12},{4,0},{8,4},{12,8},{1,13},{5,1},{9,5},{13,9},{2,14},{6,2},{... | collective-permute-start | bytes 6291464 | tf_op jit(solution)/shard_map/ppermute | solution.py:18
  96.7 21.5 %collective-permute-start.21 = (bf16[8,8,8192]{2,1,0:T(8,128)(2,1)S(1)}, bf16[8,8,8192]{2,1,0:T(8,128)(2,1)S(1)}, u32[]{:S(2)}, u32[]{:S(2)}) collective-permute-start(bf16[8,8,8192]{2,1,0:T(8,128)(2,1)S(1)} %slice.58), channel_id=1, source_target_pairs={{0,16},{16,32},{32,48},{48,0},{1,17},{17,33},{33,49},{49,1},{2,18}... | collective-permute-start | bytes 3145736 | tf_op jit(solution)/shard_map/ppermute | solution.py:18
  96.9 21.4 %collective-permute-start.23 = (bf16[8,8,8192]{2,1,0:T(8,128)(2,1)S(1)}, bf16[8,8,8192]{2,1,0:T(8,128)(2,1)S(1)}, u32[]{:S(2)}, u32[]{:S(2)}) collective-permute-start(bf16[8,8,8192]{2,1,0:T(8,128)(2,1)S(1)} %slice.59), channel_id=1, source_target_pairs={{0,48},{16,0},{32,16},{48,32},{1,49},{17,1},{33,17},{49,33},{2,50}... | collective-permute-start | bytes 3145736 | tf_op jit(solution)/shard_map/ppermute | solution.py:18
  99.7 21.0 %collective-permute-start.13 = (bf16[8,8,8192]{2,1,0:T(8,128)(2,1)S(1)}, bf16[8,8,8192]{2,1,0:T(8,128)(2,1)S(1)}, u32[]{:S(2)}, u32[]{:S(2)}) collective-permute-start(bf16[8,8,8192]{2,1,0:T(8,128)(2,1)S(1)} %slice.53), channel_id=1, source_target_pairs={{0,4},{4,8},{8,12},{12,0},{1,5},{5,9},{9,13},{13,1},{2,6},{6,10},{... | collective-permute-start | bytes 3145736 | tf_op jit(solution)/shard_map/ppermute | solution.py:18
  101.9 18.9 %collective-permute-start.15 = (bf16[8,8,8192]{2,1,0:T(8,128)(2,1)S(1)}, bf16[8,8,8192]{2,1,0:T(8,128)(2,1)S(1)}, u32[]{:S(2)}, u32[]{:S(2)}) collective-permute-start(bf16[8,8,8192]{2,1,0:T(8,128)(2,1)S(1)} %slice.54), channel_id=1, source_target_pairs={{0,12},{4,0},{8,4},{12,8},{1,13},{5,1},{9,5},{13,9},{2,14},{6,2},{... | collective-permute-start | bytes 3145736 | tf_op jit(solution)/shard_map/ppermute | solution.py:18
  120.8 13.4 %copy-start.1 = (f32[384]{0:T(512)S(1)}, f32[384]{0:T(512)}, u32[]{:S(2)}) copy-start(f32[384]{0:T(512)} %param.5) | copy-start | bytes 4612
  127.1 9.2 %collective-permute-start.24 = (f32[512,512]{1,0:T(8,128)S(1)}, f32[512,512]{1,0:T(8,128)S(1)}, u32[]{:S(2)}, u32[]{:S(2)}) collective-permute-start(f32[512,512]{1,0:T(8,128)S(1)} %shard_map.39.mine), channel_id=1, source_target_pairs={{0,2},{2,0},{1,3},{3,1},{4,6},{6,4},{5,7},{7,5},{8,10},{10,8},{9,1... | collective-permute-start | bytes 3145736 | tf_op jit(solution)/shard_map/ppermute | solution.py:18
where the time goes:
time: 138 us
  waiting for transfers between devices  68.5 us (50%)
  starting transfers between devices  45.4 us (33%)
  Pallas kernels  22.1 us (16%)
    ppermute x25, waiting for transfers between devices, shift(): return lax.ppermute(v, axis, [(i, (i + by) % size) for i in range(size)])  68.5 us
    ppermute x25, starting transfers between devices, shift(): return lax.ppermute(v, axis, [(i, (i + by) % size) for i in range(size)])  45.4 us
    pallas_call x3, Pallas kernels, add_blocks(): pl.pallas_call(functools.partial(add_kernel, offsets, len(a_parts) // len...  20 us
  transfers between devices with their start and end apart: 25, of which 11 were waited for; matrix products, arithmetic and copies ran while one was open for 1% of the time, Pallas kernels for 10%

commit v1 on v0

--- a/solution.py
+++ b/solution.py
@@ -9,7 +9,6 @@
 
 RING = 4
 LANES = 128
-DEPTH = 1024
 Z_AXES = ("zh", "query")
 
 
@@ -18,18 +17,11 @@
     return lax.ppermute(v, axis, [(i, (i + by) % size) for i in range(size)])
 
 
-def row_product(left, right):
-    return lax.dot_general(
-        left, right, (((1,), (1,)), ((), ())), preferred_element_type=jnp.float32
-    )
-
-
 def z_planes(own):
     half = own.shape[-1] // 2
     up, down = shift(own, Z_AXES, 1), shift(own, Z_AXES, -1)
     up, down = shift(up, Z_AXES, 1), shift(down, Z_AXES, -1)
-    far_up, far_down = shift(up[..., :half], Z_AXES, 1), shift(down[..., half:], Z_AXES, -1)
-    far_up, far_down = shift(far_up, Z_AXES, 1), shift(far_down, Z_AXES, -1)
+    far_up, far_down = shift(up[..., :half], "zh", 1), shift(down[..., half:], "zh", -1)
     return own, up, down, far_up, far_down
 
 
@@ -39,12 +31,16 @@
     return v, left, right, shift(left[:n], axis, 1), shift(right[n:], axis, -1)
 
 
-def add_kernel(offsets, n_parts, first, *refs):
+def add_kernel(offsets, n_parts, *refs):
+    first = offsets == (0,)
     count = len(offsets) * n_parts
     a_refs, b_refs = refs[:count], refs[count : 2 * count]
-    a_store, b_store = refs[2 * count : 2 * count + 2]
-    out = refs[-1]
-    n_out = a_store.shape[0]
+    stores = refs[2 * count : 2 * count + 2]
+    if first:
+        out, turned = refs[2 * count + 2], refs[2 * count + 3 :]
+        n_out = turned[0].shape[1]
+    else:
+        out, n_out = refs[-1], stores[0].shape[1]
 
     @pl.when(pl.program_id(0) == 0)
     def _():
@@ -53,17 +49,21 @@
         else:
             out[...] = refs[2 * count + 2][...]
 
-    def terms(parts, store):
+    def terms(which, parts):
+        store = stores[which][...]
+        if first:
+            store = store.T
+            turned[which][...] = store
         rows = jnp.concatenate([p[...] for p in parts], 0)
-        product = row_product(rows, store[...])
+        product = jnp.dot(rows, store, preferred_element_type=jnp.float32)
         squares = jnp.zeros((rows.shape[0], LANES), jnp.float32)
         for i in range(0, rows.shape[1], LANES):
             wide = rows[:, i : i + LANES].astype(jnp.float32)
             squares += wide * wide
         return product, squares
 
-    a_product, a_squares = terms(a_refs, a_store)
-    b_product, b_squares = terms(b_refs, b_store)
+    a_product, a_squares = terms(0, a_refs)
+    b_product, b_squares = terms(1, b_refs)
     block = a_product.shape[0] // len(offsets)
     strip = block // RING
     for i, offset in enumerate(offsets):
@@ -77,35 +77,41 @@
             out[rows, n_out:] += b_squares[source]
 
 
-def add_blocks(sums, offsets, a_parts, b_parts, store):
-    n_out = store.shape[0]
+def add_blocks(sums, offsets, a_parts, b_parts, stores, n_out, depth):
     flat = lambda v: v.reshape(-1, v.shape[-1])
     a_parts, b_parts = [flat(v) for v in a_parts], [flat(v) for v in b_parts]
-    steps = a_parts[0].shape[1] // DEPTH
+    half = a_parts[0].shape[1]
+    steps = half // depth
     n_rows = sum(v.shape[0] for v in a_parts)
     shape = (RING * n_rows // len(offsets), n_out + LANES)
-    part_specs = [pl.BlockSpec((v.shape[0], DEPTH), lambda k: (0, k)) for v in a_parts + b_parts]
-    store_specs = [
-        pl.BlockSpec((n_out, DEPTH), lambda k: (0, k)),
-        pl.BlockSpec((n_out, DEPTH), lambda k: (0, k + steps)),
-    ]
+    part_specs = [pl.BlockSpec((v.shape[0], depth), lambda k: (0, k)) for v in a_parts + b_parts]
+    turned_spec = pl.BlockSpec((depth, n_out), lambda k: (k, 0))
     whole = pl.BlockSpec(shape, lambda k: (0, 0))
-    earlier = [] if sums is None else [sums]
+    out_shape, out_specs = jax.ShapeDtypeStruct(shape, jnp.float32), whole
+    if sums is None:
+        store_specs = [
+            pl.BlockSpec((n_out, depth), lambda k: (0, k)),
+            pl.BlockSpec((n_out, depth), lambda k: (0, k + steps)),
+        ]
+        turned = jax.ShapeDtypeStruct((half, n_out), stores[0].dtype)
+        out_shape, out_specs = (out_shape, turned, turned), (whole, turned_spec, turned_spec)
+        earlier = []
+    else:
+        store_specs = [turned_spec] * 2
+        earlier = [sums]
     return pl.pallas_call(
-        functools.partial(
-            add_kernel, offsets, len(a_parts) // len(offsets), sums is None
-        ),
+        functools.partial(add_kernel, offsets, len(a_parts) // len(offsets)),
         grid=(steps,),
-        out_shape=jax.ShapeDtypeStruct(shape, jnp.float32),
+        out_shape=out_shape,
         in_specs=part_specs + store_specs + [whole] * len(earlier),
-        out_specs=whole,
-        compiler_params=pltpu.CompilerParams(vmem_limit_bytes=24 * 1024 * 1024),
+        out_specs=out_specs,
+        compiler_params=pltpu.CompilerParams(vmem_limit_bytes=26 * 1024 * 1024),
         cost_estimate=pl.CostEstimate(
-            flops=4 * n_rows * steps * DEPTH * n_out,
-            bytes_accessed=2 * steps * DEPTH * (2 * n_out + 2 * n_rows),
+            flops=4 * n_rows * half * n_out,
+            bytes_accessed=4 * half * (n_out + n_rows),
             transcendentals=0,
         ),
-    )(*a_parts, *b_parts, store, store, *earlier)
+    )(*a_parts, *b_parts, *stores, *earlier)
 
 
 def finish_kernel(order, mine, other, weight, out):
@@ -140,19 +146,21 @@
     store = train_feats[:, 0, :]
     half = own.shape[-1] // 2
     z = z_planes(own)
-    planes = jnp.concatenate([z[0], z[1], z[2], jnp.concatenate([z[3], z[4]], -1)], 0)
-    first = jnp.concatenate(ring(planes[..., :half], "x"), 0)
-    second = jnp.concatenate(ring(planes[..., half:], "y"), 0)
+    a_planes = jnp.concatenate([v[..., :half] for v in z[:3]] + [z[3]], 0)
+    b_planes = jnp.concatenate([v[..., half:] for v in z[:3]] + [z[4]], 0)
+    first = jnp.concatenate(ring(a_planes, "x"), 0)
+    second = jnp.concatenate(ring(b_planes, "y"), 0)
     a, b = ring(first, "y"), ring(second, "x")
-    sums = add_blocks(None, (0,), a[:1], b[:1], store)
-    sums = add_blocks(sums, (1, 2), a[1:3], b[1:3], store)
-    sums = add_blocks(sums, (3,), a[3:], b[3:], store)
+    n_out = store.shape[0]
+    sums, *turned = add_blocks(None, (0,), a[:1], b[:1], (store, store), n_out, 1024)
+    sums = add_blocks(sums, (1, 2), a[1:3], b[1:3], turned, n_out, 2048)
+    sums = add_blocks(sums, (3,), a[3:], b[3:], turned, n_out, 4096)
     other = shift(sums, "layer", 1)
     order = absolute_order(*(lax.axis_index(n) for n in ("zh", "x", "y")))
     vmem = pl.BlockSpec(memory_space=pltpu.VMEM)
     result = pl.pallas_call(
         finish_kernel,
-        out_shape=jax.ShapeDtypeStruct((sums.shape[0], store.shape[0]), jnp.bfloat16),
+        out_shape=jax.ShapeDtypeStruct((sums.shape[0], n_out), jnp.bfloat16),
         in_specs=[pl.BlockSpec(memory_space=pltpu.SMEM)] + [vmem] * 3,
         out_specs=vmem,
         compiler_params=pltpu.CompilerParams(vmem_limit_bytes=16 * 1024 * 1024),

time: 138 us -> 132 us (0.957)
  the two profiles are of different devices: /device:TPU:1 before, /device:TPU:57 now
where the time goes in v1:
time: 132 us
  waiting for transfers between devices  74.6 us (57%)
  starting transfers between devices  34.8 us (26%)
  Pallas kernels  20.3 us (15%)
  local copies, waits for them, and re-layouts  1.76 us (1%)
    ppermute x23, waiting for transfers between devices, shift(): return lax.ppermute(v, axis, [(i, (i + by) % size) for i in range(size)])  74.6 us
    ppermute x23, starting transfers between devices, shift(): return lax.ppermute(v, axis, [(i, (i + by) % size) for i in range(size)])  34.8 us
    pallas_call x3, Pallas kernels, add_blocks(): pl.pallas_call(functools.partial(add_kernel, offsets, len(a_parts) // len...  18.2 us
  transfers between devices with their start and end apart: 23, of which 14 were waited for; matrix products, arithmetic and copies ran while one was open for 2% of the time, Pallas kernels for 12%

profile of v1, /device:TPU:57, one launch (start us, length us, event | category | flops | bytes accessed | tf_op | source)
XLA Modules:
  0.0 132.0 jit_solution(11432912056831115576)
XLA Ops:
  0.0 1.6 %collective-permute-start = (bf16[1,8,16384]{2,1,0:T(8,128)(2,1)}, bf16[1,8,16384]{2,1,0:T(8,128)(2,1)S(1)}, u32[]{:S(2)}, u32[]{:S(2)}) collective-permute-start(bf16[1,8,16384]{2,1,0:T(8,128)(2,1)} %bitcast.25), channel_id=1, source_target_pairs={{0,1},{1,64},{64,65},{65,128},{128,129},{129,192},{192,193},{193,0... | collective-permute-start | bytes 786440 | tf_op jit(solution)/shard_map/ppermute | solution.py:17
  1.6 5.7 %collective-permute-done = bf16[1,8,16384]{2,1,0:T(8,128)(2,1)S(1)} collective-permute-done((bf16[1,8,16384]{2,1,0:T(8,128)(2,1)}, bf16[1,8,16384]{2,1,0:T(8,128)(2,1)S(1)}, u32[]{:S(2)}, u32[]{:S(2)}) %collective-permute-start) | collective-permute-done | bytes 262176 | tf_op jit(solution)/shard_map/ppermute | solution.py:17
  7.4 1.6 %collective-permute-start.1 = (bf16[1,8,16384]{2,1,0:T(8,128)(2,1)S(1)}, bf16[1,8,16384]{2,1,0:T(8,128)(2,1)S(1)}, u32[]{:S(2)}, u32[]{:S(2)}) collective-permute-start(bf16[1,8,16384]{2,1,0:T(8,128)(2,1)S(1)} %collective-permute-done), channel_id=1, source_target_pairs={{0,1},{1,64},{64,65},{65,128},{128,129},{129,192},{192,193},{193,0... | collective-permute-start | bytes 786440 | tf_op jit(solution)/shard_map/ppermute | solution.py:17
  9.0 1.0 fusion.5
  10.0 2.7 %collective-permute-start.3 = (bf16[1,8,16384]{2,1,0:T(8,128)(2,1)S(1)}, bf16[1,8,16384]{2,1,0:T(8,128)(2,1)S(1)}, u32[]{:S(2)}, u32[]{:S(2)}) collective-permute-start(bf16[1,8,16384]{2,1,0:T(8,128)(2,1)S(1)} %collective-permute-done.2), channel_id=1, source_target_pairs={{0,193},{1,0},{64,1},{65,64},{128,65},{129,128},{192,129},{193,192... | collective-permute-start | bytes 786440 | tf_op jit(solution)/shard_map/ppermute | solution.py:17
  12.7 4.3 %collective-permute-done.1 = bf16[1,8,16384]{2,1,0:T(8,128)(2,1)S(1)} collective-permute-done((bf16[1,8,16384]{2,1,0:T(8,128)(2,1)S(1)}, bf16[1,8,16384]{2,1,0:T(8,128)(2,1)S(1)}, u32[]{:S(2)}, u32[]{:S(2)}) %collective-permute-start.1) | collective-permute-done | bytes 262176 | tf_op jit(solution)/shard_map/ppermute | solution.py:17
  17.3 5.4 %collective-permute-start.13 = (bf16[1,8,8192]{2,1,0:T(8,128)(2,1)S(1)}, bf16[1,8,8192]{2,1,0:T(8,128)(2,1)S(1)}, u32[]{:S(2)}, u32[]{:S(2)}) collective-permute-start(bf16[1,8,8192]{2,1,0:T(8,128)(2,1)S(1)} %get-tuple-element.19), channel_id=1, source_target_pairs={{0,192},{64,0},{128,64},{192,128},{1,193},{65,1},{129,65},{193,129... | collective-permute-start | bytes 393224 | tf_op jit(solution)/shard_map/ppermute | solution.py:17
  22.9 3.7 %collective-permute-done.13 = bf16[1,8,8192]{2,1,0:T(8,128)(2,1)S(1)} collective-permute-done((bf16[1,8,8192]{2,1,0:T(8,128)(2,1)S(1)}, bf16[1,8,8192]{2,1,0:T(8,128)(2,1)S(1)}, u32[]{:S(2)}, u32[]{:S(2)}) %collective-permute-start.13) | collective-permute-done | bytes 131104 | tf_op jit(solution)/shard_map/ppermute | solution.py:17
  26.8 1.5 %collective-permute-start.15 = (bf16[4,8,8192]{2,1,0:T(8,128)(2,1)S(1)}, bf16[4,8,8192]{2,1,0:T(8,128)(2,1)S(1)}, u32[]{:S(2)}, u32[]{:S(2)}) collective-permute-start(bf16[4,8,8192]{2,1,0:T(8,128)(2,1)S(1)} %pad_maximum_fusion.1), channel_id=1, source_target_pairs={{0,12},{4,0},{8,4},{12,8},{1,13},{5,1},{9,5},{13,9},{2,14},{6,2},{... | collective-permute-start | bytes 1572872 | tf_op jit(solution)/shard_map/ppermute | solution.py:17
  28.8 1.3 collective-permute-start.5
  30.1 1.5 %collective-permute-start.6 = (bf16[4,8,8192]{2,1,0:T(8,128)(2,1)S(1)}, bf16[4,8,8192]{2,1,0:T(8,128)(2,1)S(1)}, u32[]{:S(2)}, u32[]{:S(2)}) collective-permute-start(bf16[4,8,8192]{2,1,0:T(8,128)(2,1)S(1)} %pad_maximum_fusion), channel_id=1, source_target_pairs={{0,48},{16,0},{32,16},{48,32},{1,49},{17,1},{33,17},{49,33},{2,50}... | collective-permute-start | bytes 1572872 | tf_op jit(solution)/shard_map/ppermute | solution.py:17
  31.6 6.4 %collective-permute-done.14 = bf16[4,8,8192]{2,1,0:T(8,128)(2,1)S(1)} collective-permute-done((bf16[4,8,8192]{2,1,0:T(8,128)(2,1)S(1)}, bf16[4,8,8192]{2,1,0:T(8,128)(2,1)S(1)}, u32[]{:S(2)}, u32[]{:S(2)}) %collective-permute-start.14) | collective-permute-done | bytes 524320 | tf_op jit(solution)/shard_map/ppermute | solution.py:17
  38.0 1.4 %collective-permute-start.16 = (bf16[2,8,8192]{2,1,0:T(8,128)(2,1)S(1)}, bf16[2,8,8192]{2,1,0:T(8,128)(2,1)S(1)}, u32[]{:S(2)}, u32[]{:S(2)}) collective-permute-start(bf16[2,8,8192]{2,1,0:T(8,128)(2,1)S(1)} %slice.68), channel_id=1, source_target_pairs={{0,4},{4,8},{8,12},{12,0},{1,5},{5,9},{9,13},{13,1},{2,6},{6,10},{... | collective-permute-start | bytes 786440 | tf_op jit(solution)/shard_map/ppermute | solution.py:17
  39.8 1.2 collective-permute-start.7
  41.0 1.7 %collective-permute-start.8 = (bf16[2,8,8192]{2,1,0:T(8,128)(2,1)S(1)}, bf16[2,8,8192]{2,1,0:T(8,128)(2,1)S(1)}, u32[]{:S(2)}, u32[]{:S(2)}) collective-permute-start(bf16[2,8,8192]{2,1,0:T(8,128)(2,1)S(1)} %slice.62), channel_id=1, source_target_pairs={{0,48},{16,0},{32,16},{48,32},{1,49},{17,1},{33,17},{49,33},{2,50}... | collective-permute-start | bytes 786440 | tf_op jit(solution)/shard_map/ppermute | solution.py:17
  42.8 0.8 collective-permute-done.16
  43.6 2.3 %collective-permute-done.17 = bf16[2,8,8192]{2,1,0:T(8,128)(2,1)S(1)} collective-permute-done((bf16[2,8,8192]{2,1,0:T(8,128)(2,1)S(1)}, bf16[2,8,8192]{2,1,0:T(8,128)(2,1)S(1)}, u32[]{:S(2)}, u32[]{:S(2)}) %collective-permute-start.17) | collective-permute-done | bytes 262176 | tf_op jit(solution)/shard_map/ppermute | solution.py:17
  45.9 1.3 collective-permute-start.18
  47.2 1.5 %collective-permute-start.20 = (bf16[16,8,8192]{2,1,0:T(8,128)(2,1)S(1)}, bf16[16,8,8192]{2,1,0:T(8,128)(2,1)S(1)}, u32[]{:S(2)}, u32[]{:S(2)}) collective-permute-start(bf16[16,8,8192]{2,1,0:T(8,128)(2,1)S(1)} %constant_dynamic-update-slice_fusion.8), channel_id=1, source_target_pairs={{0,48},{16,0},{32,16},{48,32},{1,49},{17,1},{33,17},{49,33},{2,50}... | collective-permute-start | bytes 6291464 | tf_op jit(solution)/shard_map/ppermute | solution.py:17
  49.2 1.2 collective-permute-start.11
  50.4 43.5 %collective-permute-done.18 = bf16[16,8,8192]{2,1,0:T(8,128)(2,1)S(1)} collective-permute-done((bf16[16,8,8192]{2,1,0:T(8,128)(2,1)S(1)}, bf16[16,8,8192]{2,1,0:T(8,128)(2,1)S(1)}, u32[]{:S(2)}, u32[]{:S(2)}) %collective-permute-start.18) | collective-permute-done | bytes 2097184 | tf_op jit(solution)/shard_map/ppermute | solution.py:17
  94.2 3.1 %collective-permute-start.21 = (bf16[8,8,8192]{2,1,0:T(8,128)(2,1)S(1)}, bf16[8,8,8192]{2,1,0:T(8,128)(2,1)S(1)}, u32[]{:S(2)}, u32[]{:S(2)}) collective-permute-start(bf16[8,8,8192]{2,1,0:T(8,128)(2,1)S(1)} %slice.71), channel_id=1, source_target_pairs={{0,48},{16,0},{32,16},{48,32},{1,49},{17,1},{33,17},{49,33},{2,50}... | collective-permute-start | bytes 3145736 | tf_op jit(solution)/shard_map/ppermute | solution.py:17
  97.7 1.3 collective-permute-start.12
  99.0 9.5 %shard_map.37 = (f32[512,512]{1,0:T(8,128)S(1)}, bf16[8192,384]{1,0:T(8,128)(2,1)S(1)}, bf16[8192,384]{1,0:T(8,128)(2,1)S(1)}) custom-call(bf16[128,8192]{1,0:T(8,128)(2,1)S(1)} %bitcast.17, bf16[128,8192]{1,0:T(8,128)(2,1)S(1)} %bitcast.18, bf16[384,16384]{1,0:T(8,128)(2,1)} %bitcast.23, bf16[384,16384]{1,0:T(8,128)(2,1)} %bitcast.24), custom_call_target="tpu_custom_call" | custom-call | flops 1610612736 | bytes 16777216 | tf_op jit(solution)/shard_map/pallas_call | solution.py:102
  108.6 5.8 %shard_map.38.refs_6_ = f32[512,512]{1,0:T(8,128)S(1)} custom-call(bf16[128,8192]{1,0:T(8,128)(2,1)S(1)} %bitcast.15, bf16[128,8192]{1,0:T(8,128)(2,1)S(1)} %bitcast.16, bf16[128,8192]{1,0:T(8,128)(2,1)S(1)} %bitcast.13, bf16[128,8192]{1,0:T(8,128)(2,1)S(1)} %bitcast.14, bf16[8192,384]{1,0:T(8,128)(2,1)S(1)} %get-tuple-element.8.refs_4_, ...), custom_call_target="tpu_custom_call" | custom-call | flops 3221225472 | bytes 20971520 | tf_op jit(solution)/shard_map/pallas_call | solution.py:102
  114.3 2.2 %collective-permute-done.19 = bf16[8,8,8192]{2,1,0:T(8,128)(2,1)S(1)} collective-permute-done((bf16[8,8,8192]{2,1,0:T(8,128)(2,1)S(1)}, bf16[8,8,8192]{2,1,0:T(8,128)(2,1)S(1)}, u32[]{:S(2)}, u32[]{:S(2)}) %collective-permute-start.19) | collective-permute-done | bytes 1048608 | tf_op jit(solution)/shard_map/ppermute | solution.py:17
  116.6 1.9 %collective-permute-done.10 = bf16[8,8,8192]{2,1,0:T(8,128)(2,1)S(1)} collective-permute-done((bf16[8,8,8192]{2,1,0:T(8,128)(2,1)S(1)}, bf16[8,8,8192]{2,1,0:T(8,128)(2,1)S(1)}, u32[]{:S(2)}, u32[]{:S(2)}) %collective-permute-start.10) | collective-permute-done | bytes 1048608 | tf_op jit(solution)/shard_map/ppermute | solution.py:17
  118.4 0.9 collective-permute-done.12
  119.3 2.9 %shard_map.39.mine = f32[512,512]{1,0:T(8,128)S(1)} custom-call(bf16[64,8192]{1,0:T(8,128)(2,1)S(1)} %bitcast.21, bf16[64,8192]{1,0:T(8,128)(2,1)S(1)} %bitcast.22, bf16[64,8192]{1,0:T(8,128)(2,1)S(1)} %bitcast.19, bf16[64,8192]{1,0:T(8,128)(2,1)S(1)} %bitcast.20, bf16[8192,384]{1,0:T(8,128)(2,1)S(1)} %get-tuple-element.8.refs_4_, ...), custom_call_target="tpu_custom_call" | custom-call | flops 1610612736 | bytes 16777216 | tf_op jit(solution)/shard_map/pallas_call | solution.py:102
  122.3 5.3 %collective-permute-start.22 = (f32[512,512]{1,0:T(8,128)S(1)}, f32[512,512]{1,0:T(8,128)S(1)}, u32[]{:S(2)}, u32[]{:S(2)}) collective-permute-start(f32[512,512]{1,0:T(8,128)S(1)} %shard_map.39.mine), channel_id=1, source_target_pairs={{0,2},{2,0},{1,3},{3,1},{4,6},{6,4},{5,7},{7,5},{8,10},{10,8},{9,1... | collective-permute-start | bytes 3145736 | tf_op jit(solution)/shard_map/ppermute | solution.py:17
  127.9 2.0 %collective-permute-done.22.other = f32[512,512]{1,0:T(8,128)S(1)} collective-permute-done((f32[512,512]{1,0:T(8,128)S(1)}, f32[512,512]{1,0:T(8,128)S(1)}, u32[]{:S(2)}, u32[]{:S(2)}) %collective-permute-start.22) | collective-permute-done | bytes 1048608 | tf_op jit(solution)/shard_map/ppermute | solution.py:17
  129.9 2.1 %shard_map.40 = bf16[512,384]{1,0:T(8,128)(2,1)} custom-call(s32[64]{0:T(128)S(1)} %add.94.order, f32[512,512]{1,0:T(8,128)S(1)} %shard_map.39.mine, f32[512,512]{1,0:T(8,128)S(1)} %collective-permute-done.22.other, f32[1,384]{1,0:T(1,128)S(1)} %broadcast_in_dim.19.weight), custom_call_target="tpu_custom_call" | custom-call | tf_op jit(solution)/shard_map/pallas_call | solution.py:161
  (49 shorter events, 3.3 us)
Async XLA Ops:
  0.0 7.4 %collective-permute-start = (bf16[1,8,16384]{2,1,0:T(8,128)(2,1)}, bf16[1,8,16384]{2,1,0:T(8,128)(2,1)S(1)}, u32[]{:S(2)}, u32[]{:S(2)}) collective-permute-start(bf16[1,8,16384]{2,1,0:T(8,128)(2,1)} %bitcast.25), channel_id=1, source_target_pairs={{0,1},{1,64},{64,65},{65,128},{128,129},{129,192},{192,193},{193,0... | collective-permute-start | bytes 786440 | tf_op jit(solution)/shard_map/ppermute | solution.py:17
  1.6 8.4 %collective-permute-start.2 = (bf16[1,8,16384]{2,1,0:T(8,128)(2,1)}, bf16[1,8,16384]{2,1,0:T(8,128)(2,1)S(1)}, u32[]{:S(2)}, u32[]{:S(2)}) collective-permute-start(bf16[1,8,16384]{2,1,0:T(8,128)(2,1)} %bitcast.26), channel_id=1, source_target_pairs={{0,193},{1,0},{64,1},{65,64},{128,65},{129,128},{192,129},{193,192... | collective-permute-start | bytes 786440 | tf_op jit(solution)/shard_map/ppermute | solution.py:17
  7.4 9.7 %collective-permute-start.1 = (bf16[1,8,16384]{2,1,0:T(8,128)(2,1)S(1)}, bf16[1,8,16384]{2,1,0:T(8,128)(2,1)S(1)}, u32[]{:S(2)}, u32[]{:S(2)}) collective-permute-start(bf16[1,8,16384]{2,1,0:T(8,128)(2,1)S(1)} %collective-permute-done), channel_id=1, source_target_pairs={{0,1},{1,64},{64,65},{65,128},{128,129},{129,192},{192,193},{193,0... | collective-permute-start | bytes 786440 | tf_op jit(solution)/shard_map/ppermute | solution.py:17
  10.0 7.3 %collective-permute-start.3 = (bf16[1,8,16384]{2,1,0:T(8,128)(2,1)S(1)}, bf16[1,8,16384]{2,1,0:T(8,128)(2,1)S(1)}, u32[]{:S(2)}, u32[]{:S(2)}) collective-permute-start(bf16[1,8,16384]{2,1,0:T(8,128)(2,1)S(1)} %collective-permute-done.2), channel_id=1, source_target_pairs={{0,193},{1,0},{64,1},{65,64},{128,65},{129,128},{192,129},{193,192... | collective-permute-start | bytes 786440 | tf_op jit(solution)/shard_map/ppermute | solution.py:17
  17.3 9.3 %collective-permute-start.13 = (bf16[1,8,8192]{2,1,0:T(8,128)(2,1)S(1)}, bf16[1,8,8192]{2,1,0:T(8,128)(2,1)S(1)}, u32[]{:S(2)}, u32[]{:S(2)}) collective-permute-start(bf16[1,8,8192]{2,1,0:T(8,128)(2,1)S(1)} %get-tuple-element.19), channel_id=1, source_target_pairs={{0,192},{64,0},{128,64},{192,128},{1,193},{65,1},{129,65},{193,129... | collective-permute-start | bytes 393224 | tf_op jit(solution)/shard_map/ppermute | solution.py:17
  22.7 6.0 %collective-permute-start.4 = (bf16[1,8,8192]{2,1,0:T(8,128)(2,1)S(1)}, bf16[1,8,8192]{2,1,0:T(8,128)(2,1)S(1)}, u32[]{:S(2)}, u32[]{:S(2)}) collective-permute-start(bf16[1,8,8192]{2,1,0:T(8,128)(2,1)S(1)} %get-tuple-element.18), channel_id=1, source_target_pairs={{0,64},{64,128},{128,192},{192,0},{1,65},{65,129},{129,193},{193,1... | collective-permute-start | bytes 393224 | tf_op jit(solution)/shard_map/ppermute | solution.py:17
  26.7 11.3 %collective-permute-start.14 = (bf16[4,8,8192]{2,1,0:T(8,128)(2,1)S(1)}, bf16[4,8,8192]{2,1,0:T(8,128)(2,1)S(1)}, u32[]{:S(2)}, u32[]{:S(2)}) collective-permute-start(bf16[4,8,8192]{2,1,0:T(8,128)(2,1)S(1)} %pad_maximum_fusion.1), channel_id=1, source_target_pairs={{0,4},{4,8},{8,12},{12,0},{1,5},{5,9},{9,13},{13,1},{2,6},{6,10},{... | collective-permute-start | bytes 1572872 | tf_op jit(solution)/shard_map/ppermute | solution.py:17
  26.8 12.6 %collective-permute-start.15 = (bf16[4,8,8192]{2,1,0:T(8,128)(2,1)S(1)}, bf16[4,8,8192]{2,1,0:T(8,128)(2,1)S(1)}, u32[]{:S(2)}, u32[]{:S(2)}) collective-permute-start(bf16[4,8,8192]{2,1,0:T(8,128)(2,1)S(1)} %pad_maximum_fusion.1), channel_id=1, source_target_pairs={{0,12},{4,0},{8,4},{12,8},{1,13},{5,1},{9,5},{13,9},{2,14},{6,2},{... | collective-permute-start | bytes 1572872 | tf_op jit(solution)/shard_map/ppermute | solution.py:17
  28.8 10.9 %collective-permute-start.5 = (bf16[4,8,8192]{2,1,0:T(8,128)(2,1)S(1)}, bf16[4,8,8192]{2,1,0:T(8,128)(2,1)S(1)}, u32[]{:S(2)}, u32[]{:S(2)}) collective-permute-start(bf16[4,8,8192]{2,1,0:T(8,128)(2,1)S(1)} %pad_maximum_fusion), channel_id=1, source_target_pairs={{0,16},{16,32},{32,48},{48,0},{1,17},{17,33},{33,49},{49,1},{2,18}... | collective-permute-start | bytes 1572872 | tf_op jit(solution)/shard_map/ppermute | solution.py:17
  30.1 10.9 %collective-permute-start.6 = (bf16[4,8,8192]{2,1,0:T(8,128)(2,1)S(1)}, bf16[4,8,8192]{2,1,0:T(8,128)(2,1)S(1)}, u32[]{:S(2)}, u32[]{:S(2)}) collective-permute-start(bf16[4,8,8192]{2,1,0:T(8,128)(2,1)S(1)} %pad_maximum_fusion), channel_id=1, source_target_pairs={{0,48},{16,0},{32,16},{48,32},{1,49},{17,1},{33,17},{49,33},{2,50}... | collective-permute-start | bytes 1572872 | tf_op jit(solution)/shard_map/ppermute | solution.py:17
  38.0 5.6 %collective-permute-start.16 = (bf16[2,8,8192]{2,1,0:T(8,128)(2,1)S(1)}, bf16[2,8,8192]{2,1,0:T(8,128)(2,1)S(1)}, u32[]{:S(2)}, u32[]{:S(2)}) collective-permute-start(bf16[2,8,8192]{2,1,0:T(8,128)(2,1)S(1)} %slice.68), channel_id=1, source_target_pairs={{0,4},{4,8},{8,12},{12,0},{1,5},{5,9},{9,13},{13,1},{2,6},{6,10},{... | collective-permute-start | bytes 786440 | tf_op jit(solution)/shard_map/ppermute | solution.py:17
  39.4 6.5 %collective-permute-start.17 = (bf16[2,8,8192]{2,1,0:T(8,128)(2,1)S(1)}, bf16[2,8,8192]{2,1,0:T(8,128)(2,1)S(1)}, u32[]{:S(2)}, u32[]{:S(2)}) collective-permute-start(bf16[2,8,8192]{2,1,0:T(8,128)(2,1)S(1)} %slice.69), channel_id=1, source_target_pairs={{0,12},{4,0},{8,4},{12,8},{1,13},{5,1},{9,5},{13,9},{2,14},{6,2},{... | collective-permute-start | bytes 786440 | tf_op jit(solution)/shard_map/ppermute | solution.py:17
  39.8 9.0 %collective-permute-start.7 = (bf16[2,8,8192]{2,1,0:T(8,128)(2,1)S(1)}, bf16[2,8,8192]{2,1,0:T(8,128)(2,1)S(1)}, u32[]{:S(2)}, u32[]{:S(2)}) collective-permute-start(bf16[2,8,8192]{2,1,0:T(8,128)(2,1)S(1)} %slice.61), channel_id=1, source_target_pairs={{0,16},{16,32},{32,48},{48,0},{1,17},{17,33},{33,49},{49,1},{2,18}... | collective-permute-start | bytes 786440 | tf_op jit(solution)/shard_map/ppermute | solution.py:17
  41.0 7.8 %collective-permute-start.8 = (bf16[2,8,8192]{2,1,0:T(8,128)(2,1)S(1)}, bf16[2,8,8192]{2,1,0:T(8,128)(2,1)S(1)}, u32[]{:S(2)}, u32[]{:S(2)}) collective-permute-start(bf16[2,8,8192]{2,1,0:T(8,128)(2,1)S(1)} %slice.62), channel_id=1, source_target_pairs={{0,48},{16,0},{32,16},{48,32},{1,49},{17,1},{33,17},{49,33},{2,50}... | collective-permute-start | bytes 786440 | tf_op jit(solution)/shard_map/ppermute | solution.py:17
  45.9 48.0 %collective-permute-start.18 = (bf16[16,8,8192]{2,1,0:T(8,128)(2,1)S(1)}, bf16[16,8,8192]{2,1,0:T(8,128)(2,1)S(1)}, u32[]{:S(2)}, u32[]{:S(2)}) collective-permute-start(bf16[16,8,8192]{2,1,0:T(8,128)(2,1)S(1)} %constant_dynamic-update-slice_fusion.8), channel_id=1, source_target_pairs={{0,16},{16,32},{32,48},{48,0},{1,17},{17,33},{33,49},{49,1},{2,18}... | collective-permute-start | bytes 6291464 | tf_op jit(solution)/shard_map/ppermute | solution.py:17
  47.2 46.9 %collective-permute-start.20 = (bf16[16,8,8192]{2,1,0:T(8,128)(2,1)S(1)}, bf16[16,8,8192]{2,1,0:T(8,128)(2,1)S(1)}, u32[]{:S(2)}, u32[]{:S(2)}) collective-permute-start(bf16[16,8,8192]{2,1,0:T(8,128)(2,1)S(1)} %constant_dynamic-update-slice_fusion.8), channel_id=1, source_target_pairs={{0,48},{16,0},{32,16},{48,32},{1,49},{17,1},{33,17},{49,33},{2,50}... | collective-permute-start | bytes 6291464 | tf_op jit(solution)/shard_map/ppermute | solution.py:17
  48.8 48.4 %collective-permute-start.9 = (bf16[16,8,8192]{2,1,0:T(8,128)(2,1)S(1)}, bf16[16,8,8192]{2,1,0:T(8,128)(2,1)S(1)}, u32[]{:S(2)}, u32[]{:S(2)}) collective-permute-start(bf16[16,8,8192]{2,1,0:T(8,128)(2,1)S(1)} %constant_dynamic-update-slice_fusion), channel_id=1, source_target_pairs={{0,4},{4,8},{8,12},{12,0},{1,5},{5,9},{9,13},{13,1},{2,6},{6,10},{... | collective-permute-start | bytes 6291464 | tf_op jit(solution)/shard_map/ppermute | solution.py:17
  49.2 48.5 %collective-permute-start.11 = (bf16[16,8,8192]{2,1,0:T(8,128)(2,1)S(1)}, bf16[16,8,8192]{2,1,0:T(8,128)(2,1)S(1)}, u32[]{:S(2)}, u32[]{:S(2)}) collective-permute-start(bf16[16,8,8192]{2,1,0:T(8,128)(2,1)S(1)} %constant_dynamic-update-slice_fusion), channel_id=1, source_target_pairs={{0,12},{4,0},{8,4},{12,8},{1,13},{5,1},{9,5},{13,9},{2,14},{6,2},{... | collective-permute-start | bytes 6291464 | tf_op jit(solution)/shard_map/ppermute | solution.py:17
  94.0 22.6 %collective-permute-start.19 = (bf16[8,8,8192]{2,1,0:T(8,128)(2,1)S(1)}, bf16[8,8,8192]{2,1,0:T(8,128)(2,1)S(1)}, u32[]{:S(2)}, u32[]{:S(2)}) collective-permute-start(bf16[8,8,8192]{2,1,0:T(8,128)(2,1)S(1)} %slice.70), channel_id=1, source_target_pairs={{0,16},{16,32},{32,48},{48,0},{1,17},{17,33},{33,49},{49,1},{2,18}... | collective-permute-start | bytes 3145736 | tf_op jit(solution)/shard_map/ppermute | solution.py:17
  94.2 22.4 %collective-permute-start.21 = (bf16[8,8,8192]{2,1,0:T(8,128)(2,1)S(1)}, bf16[8,8,8192]{2,1,0:T(8,128)(2,1)S(1)}, u32[]{:S(2)}, u32[]{:S(2)}) collective-permute-start(bf16[8,8,8192]{2,1,0:T(8,128)(2,1)S(1)} %slice.71), channel_id=1, source_target_pairs={{0,48},{16,0},{32,16},{48,32},{1,49},{17,1},{33,17},{49,33},{2,50}... | collective-permute-start | bytes 3145736 | tf_op jit(solution)/shard_map/ppermute | solution.py:17
  97.3 21.1 %collective-permute-start.10 = (bf16[8,8,8192]{2,1,0:T(8,128)(2,1)S(1)}, bf16[8,8,8192]{2,1,0:T(8,128)(2,1)S(1)}, u32[]{:S(2)}, u32[]{:S(2)}) collective-permute-start(bf16[8,8,8192]{2,1,0:T(8,128)(2,1)S(1)} %slice.63), channel_id=1, source_target_pairs={{0,4},{4,8},{8,12},{12,0},{1,5},{5,9},{9,13},{13,1},{2,6},{6,10},{... | collective-permute-start | bytes 3145736 | tf_op jit(solution)/shard_map/ppermute | solution.py:17
  97.7 21.6 %collective-permute-start.12 = (bf16[8,8,8192]{2,1,0:T(8,128)(2,1)S(1)}, bf16[8,8,8192]{2,1,0:T(8,128)(2,1)S(1)}, u32[]{:S(2)}, u32[]{:S(2)}) collective-permute-start(bf16[8,8,8192]{2,1,0:T(8,128)(2,1)S(1)} %slice.64), channel_id=1, source_target_pairs={{0,12},{4,0},{8,4},{12,8},{1,13},{5,1},{9,5},{13,9},{2,14},{6,2},{... | collective-permute-start | bytes 3145736 | tf_op jit(solution)/shard_map/ppermute | solution.py:17
  119.3 8.6 %copy-start = (f32[384]{0:T(512)S(1)}, f32[384]{0:T(512)}, u32[]{:S(2)}) copy-start(f32[384]{0:T(512)} %param.5) | copy-start | bytes 4612
  122.3 7.6 %collective-permute-start.22 = (f32[512,512]{1,0:T(8,128)S(1)}, f32[512,512]{1,0:T(8,128)S(1)}, u32[]{:S(2)}, u32[]{:S(2)}) collective-permute-start(f32[512,512]{1,0:T(8,128)S(1)} %shard_map.39.mine), channel_id=1, source_target_pairs={{0,2},{2,0},{1,3},{3,1},{4,6},{6,4},{5,7},{7,5},{8,10},{10,8},{9,1... | collective-permute-start | bytes 3145736 | tf_op jit(solution)/shard_map/ppermute | solution.py:17

commit v2 on v1

--- a/solution.py
+++ b/solution.py
@@ -17,12 +17,13 @@
     return lax.ppermute(v, axis, [(i, (i + by) % size) for i in range(size)])
 
 
-def z_planes(own):
-    half = own.shape[-1] // 2
-    up, down = shift(own, Z_AXES, 1), shift(own, Z_AXES, -1)
-    up, down = shift(up, Z_AXES, 1), shift(down, Z_AXES, -1)
-    far_up, far_down = shift(up[..., :half], "zh", 1), shift(down[..., half:], "zh", -1)
-    return own, up, down, far_up, far_down
+def z_planes(a_own, b_own):
+    def twice(v, by):
+        return shift(shift(v, Z_AXES, by), Z_AXES, by)
+
+    a_up, b_down = twice(a_own, 1), twice(b_own, -1)
+    a_far, b_far = shift(a_up, "zh", 1), shift(b_down, "zh", -1)
+    return (a_own, a_up, twice(a_own, -1), a_far), (b_own, twice(b_own, 1), b_down, b_far)
 
 
 def ring(v, axis):
@@ -114,20 +115,16 @@
     )(*a_parts, *b_parts, *stores, *earlier)
 
 
-def finish_kernel(order, mine, other, weight, out):
+def finish_kernel(order, mine, other, weight, out, scaled):
     n_out = out.shape[1]
-
-    def body(i, carry):
-        halves = []
-        for j in range(2):
-            rows = pl.ds(pl.multiple_of(order[2 * i + j] * 8, 8), 8)
-            both = mine[rows, :] + other[rows, :]
-            norm = jnp.sum(both[:, n_out:], axis=1, keepdims=True)
-            halves.append(both[:, :n_out] * weight[...] * lax.rsqrt(norm + 1e-06))
-        out[pl.ds(pl.multiple_of(i * 16, 16), 16), :] = jnp.concatenate(halves, 0).astype(out.dtype)
-        return carry
-
-    lax.fori_loop(0, out.shape[0] // 16, body, 0, unroll=4)
+    for i in range(0, out.shape[0], 64):
+        rows = slice(i, i + 64)
+        both = mine[rows, :] + other[rows, :]
+        norm = jnp.sum(both[:, n_out:], axis=1, keepdims=True)
+        scaled[rows, :] = both[:, :n_out] * weight[...] * lax.rsqrt(norm + 1e-06)
+    for i in range(0, out.shape[0], 16):
+        pair = [scaled[pl.ds(pl.multiple_of(order[i // 8 + j] * 8, 8), 8), :] for j in range(2)]
+        out[i : i + 16, :] = jnp.concatenate(pair, 0).astype(out.dtype)
 
 
 def absolute_order(zh, x, y):
@@ -145,9 +142,9 @@
     own = queries[0, :, 0, :][None]
     store = train_feats[:, 0, :]
     half = own.shape[-1] // 2
-    z = z_planes(own)
-    a_planes = jnp.concatenate([v[..., :half] for v in z[:3]] + [z[3]], 0)
-    b_planes = jnp.concatenate([v[..., half:] for v in z[:3]] + [z[4]], 0)
+    a_planes, b_planes = (
+        jnp.concatenate(v, 0) for v in z_planes(own[..., :half], own[..., half:])
+    )
     first = jnp.concatenate(ring(a_planes, "x"), 0)
     second = jnp.concatenate(ring(b_planes, "y"), 0)
     a, b = ring(first, "y"), ring(second, "x")
@@ -163,6 +160,7 @@
         out_shape=jax.ShapeDtypeStruct((sums.shape[0], n_out), jnp.bfloat16),
         in_specs=[pl.BlockSpec(memory_space=pltpu.SMEM)] + [vmem] * 3,
         out_specs=vmem,
+        scratch_shapes=[pltpu.VMEM((sums.shape[0], n_out), jnp.float32)],
         compiler_params=pltpu.CompilerParams(vmem_limit_bytes=16 * 1024 * 1024),
     )(order, sums, other, train_weight[None, :])
     return result[None, :, :]

time: 132 us -> 126 us (0.955)
  the two profiles are of different devices: /device:TPU:57 before, /device:TPU:1 now
where the time goes in v2:
time: 126 us; the launch traced here: 125 us
  waiting for transfers between devices  57.1 us (45%)
  starting transfers between devices  46 us (37%)
  Pallas kernels  19.7 us (16%)
  local copies, waits for them, and re-layouts  1.73 us (1%)
    ppermute x27, waiting for transfers between devices, shift(): return lax.ppermute(v, axis, [(i, (i + by) % size) for i in range(size)])  57.1 us
    ppermute x27, starting transfers between devices, shift(): return lax.ppermute(v, axis, [(i, (i + by) % size) for i in range(size)])  46 us
    pallas_call x3, Pallas kernels, add_blocks(): pl.pallas_call(functools.partial(add_kernel, offsets, len(a_parts) // len...  18.2 us
  transfers between devices with their start and end apart: 27, of which 12 were waited for; matrix products, arithmetic and copies ran while one was open for 1% of the time, Pallas kernels for 12%

profile of v2, /device:TPU:1, one launch (start us, length us, event | category | flops | bytes accessed | tf_op | source)
XLA Modules:
  0.0 125.2 jit_solution(6670889420033169384)
XLA Ops:
  0.0 1.0 fusion.5
  1.0 6.5 %collective-permute-start.15 = (bf16[1,8,8192]{2,1,0:T(8,128)(2,1)S(1)}, bf16[1,8,8192]{2,1,0:T(8,128)(2,1)S(1)}, u32[]{:S(2)}, u32[]{:S(2)}) collective-permute-start(bf16[1,8,8192]{2,1,0:T(8,128)(2,1)S(1)} %get-tuple-element.11), channel_id=1, source_target_pairs={{0,193},{1,0},{64,1},{65,64},{128,65},{129,128},{192,129},{193,192... | collective-permute-start | bytes 393224 | tf_op jit(solution)/shard_map/ppermute | solution.py:17
  7.5 2.7 %collective-permute-start.2 = (bf16[1,8,8192]{2,1,0:T(8,128)(2,1)S(1)}, bf16[1,8,8192]{2,1,0:T(8,128)(2,1)S(1)}, u32[]{:S(2)}, u32[]{:S(2)}) collective-permute-start(bf16[1,8,8192]{2,1,0:T(8,128)(2,1)S(1)} %get-tuple-element.14), channel_id=1, source_target_pairs={{0,193},{1,0},{64,1},{65,64},{128,65},{129,128},{192,129},{193,192... | collective-permute-start | bytes 393224 | tf_op jit(solution)/shard_map/ppermute | solution.py:17
  10.2 2.9 %collective-permute-start.16 = (bf16[1,8,8192]{2,1,0:T(8,128)(2,1)S(1)}, bf16[1,8,8192]{2,1,0:T(8,128)(2,1)S(1)}, u32[]{:S(2)}, u32[]{:S(2)}) collective-permute-start(bf16[1,8,8192]{2,1,0:T(8,128)(2,1)S(1)} %collective-permute-done.15), channel_id=1, source_target_pairs={{0,193},{1,0},{64,1},{65,64},{128,65},{129,128},{192,129},{193,192... | collective-permute-start | bytes 393224 | tf_op jit(solution)/shard_map/ppermute | solution.py:17
  13.1 2.5 %collective-permute-done = bf16[1,8,8192]{2,1,0:T(8,128)(2,1)S(1)} collective-permute-done((bf16[1,8,8192]{2,1,0:T(8,128)(2,1)S(1)}, bf16[1,8,8192]{2,1,0:T(8,128)(2,1)S(1)}, u32[]{:S(2)}, u32[]{:S(2)}) %collective-permute-start) | collective-permute-done | bytes 131104 | tf_op jit(solution)/shard_map/ppermute | solution.py:17
  15.6 2.7 %collective-permute-start.3 = (bf16[1,8,8192]{2,1,0:T(8,128)(2,1)S(1)}, bf16[1,8,8192]{2,1,0:T(8,128)(2,1)S(1)}, u32[]{:S(2)}, u32[]{:S(2)}) collective-permute-start(bf16[1,8,8192]{2,1,0:T(8,128)(2,1)S(1)} %collective-permute-done.2), channel_id=1, source_target_pairs={{0,193},{1,0},{64,1},{65,64},{128,65},{129,128},{192,129},{193,192... | collective-permute-start | bytes 393224 | tf_op jit(solution)/shard_map/ppermute | solution.py:17
  18.3 3.1 %collective-permute-done.1 = bf16[1,8,8192]{2,1,0:T(8,128)(2,1)S(1)} collective-permute-done((bf16[1,8,8192]{2,1,0:T(8,128)(2,1)S(1)}, bf16[1,8,8192]{2,1,0:T(8,128)(2,1)S(1)}, u32[]{:S(2)}, u32[]{:S(2)}) %collective-permute-start.1) | collective-permute-done | bytes 131104 | tf_op jit(solution)/shard_map/ppermute | solution.py:17
  21.4 2.4 %collective-permute-done.17 = bf16[1,8,8192]{2,1,0:T(8,128)(2,1)S(1)} collective-permute-done((bf16[1,8,8192]{2,1,0:T(8,128)(2,1)S(1)}, bf16[1,8,8192]{2,1,0:T(8,128)(2,1)S(1)}, u32[]{:S(2)}, u32[]{:S(2)}) %collective-permute-start.17) | collective-permute-done | bytes 131104 | tf_op jit(solution)/shard_map/ppermute | solution.py:17
  23.9 1.4 %collective-permute-start.18 = (bf16[4,8,8192]{2,1,0:T(8,128)(2,1)S(1)}, bf16[4,8,8192]{2,1,0:T(8,128)(2,1)S(1)}, u32[]{:S(2)}, u32[]{:S(2)}) collective-permute-start(bf16[4,8,8192]{2,1,0:T(8,128)(2,1)S(1)} %pad_maximum_fusion.1), channel_id=1, source_target_pairs={{0,4},{4,8},{8,12},{12,0},{1,5},{5,9},{9,13},{13,1},{2,6},{6,10},{... | collective-permute-start | bytes 1572872 | tf_op jit(solution)/shard_map/ppermute | solution.py:17
  25.2 1.5 %collective-permute-start.19 = (bf16[4,8,8192]{2,1,0:T(8,128)(2,1)S(1)}, bf16[4,8,8192]{2,1,0:T(8,128)(2,1)S(1)}, u32[]{:S(2)}, u32[]{:S(2)}) collective-permute-start(bf16[4,8,8192]{2,1,0:T(8,128)(2,1)S(1)} %pad_maximum_fusion.1), channel_id=1, source_target_pairs={{0,12},{4,0},{8,4},{12,8},{1,13},{5,1},{9,5},{13,9},{2,14},{6,2},{... | collective-permute-start | bytes 1572872 | tf_op jit(solution)/shard_map/ppermute | solution.py:17
  26.8 1.2 collective-permute-done.4
  28.1 1.3 %collective-permute-start.5 = (bf16[4,8,8192]{2,1,0:T(8,128)(2,1)S(1)}, bf16[4,8,8192]{2,1,0:T(8,128)(2,1)S(1)}, u32[]{:S(2)}, u32[]{:S(2)}) collective-permute-start(bf16[4,8,8192]{2,1,0:T(8,128)(2,1)S(1)} %pad_maximum_fusion), channel_id=1, source_target_pairs={{0,16},{16,32},{32,48},{48,0},{1,17},{17,33},{33,49},{49,1},{2,18}... | collective-permute-start | bytes 1572872 | tf_op jit(solution)/shard_map/ppermute | solution.py:17
  29.4 1.5 %collective-permute-start.6 = (bf16[4,8,8192]{2,1,0:T(8,128)(2,1)S(1)}, bf16[4,8,8192]{2,1,0:T(8,128)(2,1)S(1)}, u32[]{:S(2)}, u32[]{:S(2)}) collective-permute-start(bf16[4,8,8192]{2,1,0:T(8,128)(2,1)S(1)} %pad_maximum_fusion), channel_id=1, source_target_pairs={{0,48},{16,0},{32,16},{48,32},{1,49},{17,1},{33,17},{49,33},{2,50}... | collective-permute-start | bytes 1572872 | tf_op jit(solution)/shard_map/ppermute | solution.py:17
  30.9 4.0 %collective-permute-done.18 = bf16[4,8,8192]{2,1,0:T(8,128)(2,1)S(1)} collective-permute-done((bf16[4,8,8192]{2,1,0:T(8,128)(2,1)S(1)}, bf16[4,8,8192]{2,1,0:T(8,128)(2,1)S(1)}, u32[]{:S(2)}, u32[]{:S(2)}) %collective-permute-start.18) | collective-permute-done | bytes 524320 | tf_op jit(solution)/shard_map/ppermute | solution.py:17
  35.0 2.9 %collective-permute-start.21 = (bf16[2,8,8192]{2,1,0:T(8,128)(2,1)S(1)}, bf16[2,8,8192]{2,1,0:T(8,128)(2,1)S(1)}, u32[]{:S(2)}, u32[]{:S(2)}) collective-permute-start(bf16[2,8,8192]{2,1,0:T(8,128)(2,1)S(1)} %slice.47), channel_id=1, source_target_pairs={{0,12},{4,0},{8,4},{12,8},{1,13},{5,1},{9,5},{13,9},{2,14},{6,2},{... | collective-permute-start | bytes 786440 | tf_op jit(solution)/shard_map/ppermute | solution.py:17
  39.3 2.0 %collective-permute-start.8 = (bf16[2,8,8192]{2,1,0:T(8,128)(2,1)S(1)}, bf16[2,8,8192]{2,1,0:T(8,128)(2,1)S(1)}, u32[]{:S(2)}, u32[]{:S(2)}) collective-permute-start(bf16[2,8,8192]{2,1,0:T(8,128)(2,1)S(1)} %slice.42), channel_id=1, source_target_pairs={{0,48},{16,0},{32,16},{48,32},{1,49},{17,1},{33,17},{49,33},{2,50}... | collective-permute-start | bytes 786440 | tf_op jit(solution)/shard_map/ppermute | solution.py:17
  42.0 1.3 %collective-permute-start.22 = (bf16[16,8,8192]{2,1,0:T(8,128)(2,1)S(1)}, bf16[16,8,8192]{2,1,0:T(8,128)(2,1)S(1)}, u32[]{:S(2)}, u32[]{:S(2)}) collective-permute-start(bf16[16,8,8192]{2,1,0:T(8,128)(2,1)S(1)} %constant_dynamic-update-slice_fusion.8), channel_id=1, source_target_pairs={{0,16},{16,32},{32,48},{48,0},{1,17},{17,33},{33,49},{49,1},{2,18}... | collective-permute-start | bytes 6291464 | tf_op jit(solution)/shard_map/ppermute | solution.py:17
  43.3 1.5 %collective-permute-start.24 = (bf16[16,8,8192]{2,1,0:T(8,128)(2,1)S(1)}, bf16[16,8,8192]{2,1,0:T(8,128)(2,1)S(1)}, u32[]{:S(2)}, u32[]{:S(2)}) collective-permute-start(bf16[16,8,8192]{2,1,0:T(8,128)(2,1)S(1)} %constant_dynamic-update-slice_fusion.8), channel_id=1, source_target_pairs={{0,48},{16,0},{32,16},{48,32},{1,49},{17,1},{33,17},{49,33},{2,50}... | collective-permute-start | bytes 6291464 | tf_op jit(solution)/shard_map/ppermute | solution.py:17
  44.8 1.3 %collective-permute-done.7 = bf16[2,8,8192]{2,1,0:T(8,128)(2,1)S(1)} collective-permute-done((bf16[2,8,8192]{2,1,0:T(8,128)(2,1)S(1)}, bf16[2,8,8192]{2,1,0:T(8,128)(2,1)S(1)}, u32[]{:S(2)}, u32[]{:S(2)}) %collective-permute-start.7) | collective-permute-done | bytes 262176 | tf_op jit(solution)/shard_map/ppermute | solution.py:17
  46.2 1.3 %collective-permute-start.9 = (bf16[16,8,8192]{2,1,0:T(8,128)(2,1)S(1)}, bf16[16,8,8192]{2,1,0:T(8,128)(2,1)S(1)}, u32[]{:S(2)}, u32[]{:S(2)}) collective-permute-start(bf16[16,8,8192]{2,1,0:T(8,128)(2,1)S(1)} %constant_dynamic-update-slice_fusion), channel_id=1, source_target_pairs={{0,4},{4,8},{8,12},{12,0},{1,5},{5,9},{9,13},{13,1},{2,6},{6,10},{... | collective-permute-start | bytes 6291464 | tf_op jit(solution)/shard_map/ppermute | solution.py:17
  47.5 1.6 %collective-permute-start.11 = (bf16[16,8,8192]{2,1,0:T(8,128)(2,1)S(1)}, bf16[16,8,8192]{2,1,0:T(8,128)(2,1)S(1)}, u32[]{:S(2)}, u32[]{:S(2)}) collective-permute-start(bf16[16,8,8192]{2,1,0:T(8,128)(2,1)S(1)} %constant_dynamic-update-slice_fusion), channel_id=1, source_target_pairs={{0,12},{4,0},{8,4},{12,8},{1,13},{5,1},{9,5},{13,9},{2,14},{6,2},{... | collective-permute-start | bytes 6291464 | tf_op jit(solution)/shard_map/ppermute | solution.py:17
  49.1 39.0 %collective-permute-done.22 = bf16[16,8,8192]{2,1,0:T(8,128)(2,1)S(1)} collective-permute-done((bf16[16,8,8192]{2,1,0:T(8,128)(2,1)S(1)}, bf16[16,8,8192]{2,1,0:T(8,128)(2,1)S(1)}, u32[]{:S(2)}, u32[]{:S(2)}) %collective-permute-start.22) | collective-permute-done | bytes 2097184 | tf_op jit(solution)/shard_map/ppermute | solution.py:17
  88.2 0.8 collective-permute-start.23
  89.1 2.0 %collective-permute-start.25 = (bf16[8,8,8192]{2,1,0:T(8,128)(2,1)S(1)}, bf16[8,8,8192]{2,1,0:T(8,128)(2,1)S(1)}, u32[]{:S(2)}, u32[]{:S(2)}) collective-permute-start(bf16[8,8,8192]{2,1,0:T(8,128)(2,1)S(1)} %slice.49), channel_id=1, source_target_pairs={{0,48},{16,0},{32,16},{48,32},{1,49},{17,1},{33,17},{49,33},{2,50}... | collective-permute-start | bytes 3145736 | tf_op jit(solution)/shard_map/ppermute | solution.py:17
  91.2 1.4 %collective-permute-start.10 = (bf16[8,8,8192]{2,1,0:T(8,128)(2,1)S(1)}, bf16[8,8,8192]{2,1,0:T(8,128)(2,1)S(1)}, u32[]{:S(2)}, u32[]{:S(2)}) collective-permute-start(bf16[8,8,8192]{2,1,0:T(8,128)(2,1)S(1)} %slice.43), channel_id=1, source_target_pairs={{0,4},{4,8},{8,12},{12,0},{1,5},{5,9},{9,13},{13,1},{2,6},{6,10},{... | collective-permute-start | bytes 3145736 | tf_op jit(solution)/shard_map/ppermute | solution.py:17
  92.6 1.6 %collective-permute-start.12 = (bf16[8,8,8192]{2,1,0:T(8,128)(2,1)S(1)}, bf16[8,8,8192]{2,1,0:T(8,128)(2,1)S(1)}, u32[]{:S(2)}, u32[]{:S(2)}) collective-permute-start(bf16[8,8,8192]{2,1,0:T(8,128)(2,1)S(1)} %slice.44), channel_id=1, source_target_pairs={{0,12},{4,0},{8,4},{12,8},{1,13},{5,1},{9,5},{13,9},{2,14},{6,2},{... | collective-permute-start | bytes 3145736 | tf_op jit(solution)/shard_map/ppermute | solution.py:17
  94.2 9.5 %shard_map.37 = (f32[512,512]{1,0:T(8,128)S(1)}, bf16[8192,384]{1,0:T(8,128)(2,1)S(1)}, bf16[8192,384]{1,0:T(8,128)(2,1)S(1)}) custom-call(bf16[128,8192]{1,0:T(8,128)(2,1)S(1)} %bitcast.17, bf16[128,8192]{1,0:T(8,128)(2,1)S(1)} %bitcast.18, bf16[384,16384]{1,0:T(8,128)(2,1)} %bitcast.23, bf16[384,16384]{1,0:T(8,128)(2,1)} %bitcast.24), custom_call_target="tpu_custom_call" | custom-call | flops 1610612736 | bytes 16777216 | tf_op jit(solution)/shard_map/pallas_call | solution.py:103
  103.7 5.8 %shard_map.38.refs_6_ = f32[512,512]{1,0:T(8,128)S(1)} custom-call(bf16[128,8192]{1,0:T(8,128)(2,1)S(1)} %bitcast.15, bf16[128,8192]{1,0:T(8,128)(2,1)S(1)} %bitcast.16, bf16[128,8192]{1,0:T(8,128)(2,1)S(1)} %bitcast.13, bf16[128,8192]{1,0:T(8,128)(2,1)S(1)} %bitcast.14, bf16[8192,384]{1,0:T(8,128)(2,1)S(1)} %get-tuple-element.8.refs_4_, ...), custom_call_target="tpu_custom_call" | custom-call | flops 3221225472 | bytes 20971520 | tf_op jit(solution)/shard_map/pallas_call | solution.py:103
  110.1 2.9 %shard_map.39.mine = f32[512,512]{1,0:T(8,128)S(1)} custom-call(bf16[64,8192]{1,0:T(8,128)(2,1)S(1)} %bitcast.21, bf16[64,8192]{1,0:T(8,128)(2,1)S(1)} %bitcast.22, bf16[64,8192]{1,0:T(8,128)(2,1)S(1)} %bitcast.19, bf16[64,8192]{1,0:T(8,128)(2,1)S(1)} %bitcast.20, bf16[8192,384]{1,0:T(8,128)(2,1)S(1)} %get-tuple-element.8.refs_4_, ...), custom_call_target="tpu_custom_call" | custom-call | flops 1610612736 | bytes 16777216 | tf_op jit(solution)/shard_map/pallas_call | solution.py:103
  113.0 8.4 %collective-permute-start.26 = (f32[512,512]{1,0:T(8,128)S(1)}, f32[512,512]{1,0:T(8,128)S(1)}, u32[]{:S(2)}, u32[]{:S(2)}) collective-permute-start(f32[512,512]{1,0:T(8,128)S(1)} %shard_map.39.mine), channel_id=1, source_target_pairs={{0,2},{2,0},{1,3},{3,1},{4,6},{6,4},{5,7},{7,5},{8,10},{10,8},{9,1... | collective-permute-start | bytes 3145736 | tf_op jit(solution)/shard_map/ppermute | solution.py:17
  121.7 2.0 %collective-permute-done.26.other = f32[512,512]{1,0:T(8,128)S(1)} collective-permute-done((f32[512,512]{1,0:T(8,128)S(1)}, f32[512,512]{1,0:T(8,128)S(1)}, u32[]{:S(2)}, u32[]{:S(2)}) %collective-permute-start.26) | collective-permute-done | bytes 1048608 | tf_op jit(solution)/shard_map/ppermute | solution.py:17
  123.6 1.5 %shard_map.40 = bf16[512,384]{1,0:T(8,128)(2,1)} custom-call(s32[64]{0:T(128)S(1)} %add.94.order, f32[512,512]{1,0:T(8,128)S(1)} %shard_map.39.mine, f32[512,512]{1,0:T(8,128)S(1)} %collective-permute-done.26.other, f32[1,384]{1,0:T(1,128)S(1)} %broadcast_in_dim.19.weight), custom_call_target="tpu_custom_call" | custom-call | tf_op jit(solution)/shard_map/pallas_call | solution.py:158
  (59 shorter events, 3.5 us)
Async XLA Ops:
  1.0 9.2 %collective-permute-start.15 = (bf16[1,8,8192]{2,1,0:T(8,128)(2,1)S(1)}, bf16[1,8,8192]{2,1,0:T(8,128)(2,1)S(1)}, u32[]{:S(2)}, u32[]{:S(2)}) collective-permute-start(bf16[1,8,8192]{2,1,0:T(8,128)(2,1)S(1)} %get-tuple-element.11), channel_id=1, source_target_pairs={{0,193},{1,0},{64,1},{65,64},{128,65},{129,128},{192,129},{193,192... | collective-permute-start | bytes 393224 | tf_op jit(solution)/shard_map/ppermute | solution.py:17
  7.5 5.6 %collective-permute-start.13 = (bf16[1,8,8192]{2,1,0:T(8,128)(2,1)S(1)}, bf16[1,8,8192]{2,1,0:T(8,128)(2,1)S(1)}, u32[]{:S(2)}, u32[]{:S(2)}) collective-permute-start(bf16[1,8,8192]{2,1,0:T(8,128)(2,1)S(1)} %get-tuple-element.11), channel_id=1, source_target_pairs={{0,1},{1,64},{64,65},{65,128},{128,129},{129,192},{192,193},{193,0... | collective-permute-start | bytes 393224 | tf_op jit(solution)/shard_map/ppermute | solution.py:17
  7.5 8.1 %collective-permute-start = (bf16[1,8,8192]{2,1,0:T(8,128)(2,1)S(1)}, bf16[1,8,8192]{2,1,0:T(8,128)(2,1)S(1)}, u32[]{:S(2)}, u32[]{:S(2)}) collective-permute-start(bf16[1,8,8192]{2,1,0:T(8,128)(2,1)S(1)} %get-tuple-element.14), channel_id=1, source_target_pairs={{0,1},{1,64},{64,65},{65,128},{128,129},{129,192},{192,193},{193,0... | collective-permute-start | bytes 393224 | tf_op jit(solution)/shard_map/ppermute | solution.py:17
  7.5 8.1 %collective-permute-start.2 = (bf16[1,8,8192]{2,1,0:T(8,128)(2,1)S(1)}, bf16[1,8,8192]{2,1,0:T(8,128)(2,1)S(1)}, u32[]{:S(2)}, u32[]{:S(2)}) collective-permute-start(bf16[1,8,8192]{2,1,0:T(8,128)(2,1)S(1)} %get-tuple-element.14), channel_id=1, source_target_pairs={{0,193},{1,0},{64,1},{65,64},{128,65},{129,128},{192,129},{193,192... | collective-permute-start | bytes 393224 | tf_op jit(solution)/shard_map/ppermute | solution.py:17
  10.2 8.0 %collective-permute-start.16 = (bf16[1,8,8192]{2,1,0:T(8,128)(2,1)S(1)}, bf16[1,8,8192]{2,1,0:T(8,128)(2,1)S(1)}, u32[]{:S(2)}, u32[]{:S(2)}) collective-permute-start(bf16[1,8,8192]{2,1,0:T(8,128)(2,1)S(1)} %collective-permute-done.15), channel_id=1, source_target_pairs={{0,193},{1,0},{64,1},{65,64},{128,65},{129,128},{192,129},{193,192... | collective-permute-start | bytes 393224 | tf_op jit(solution)/shard_map/ppermute | solution.py:17
  13.1 5.2 %collective-permute-start.14 = (bf16[1,8,8192]{2,1,0:T(8,128)(2,1)S(1)}, bf16[1,8,8192]{2,1,0:T(8,128)(2,1)S(1)}, u32[]{:S(2)}, u32[]{:S(2)}) collective-permute-start(bf16[1,8,8192]{2,1,0:T(8,128)(2,1)S(1)} %collective-permute-done.13), channel_id=1, source_target_pairs={{0,1},{1,64},{64,65},{65,128},{128,129},{129,192},{192,193},{193,0... | collective-permute-start | bytes 393224 | tf_op jit(solution)/shard_map/ppermute | solution.py:17
  15.6 5.8 %collective-permute-start.1 = (bf16[1,8,8192]{2,1,0:T(8,128)(2,1)S(1)}, bf16[1,8,8192]{2,1,0:T(8,128)(2,1)S(1)}, u32[]{:S(2)}, u32[]{:S(2)}) collective-permute-start(bf16[1,8,8192]{2,1,0:T(8,128)(2,1)S(1)} %collective-permute-done), channel_id=1, source_target_pairs={{0,1},{1,64},{64,65},{65,128},{128,129},{129,192},{192,193},{193,0... | collective-permute-start | bytes 393224 | tf_op jit(solution)/shard_map/ppermute | solution.py:17
  15.6 5.8 %collective-permute-start.3 = (bf16[1,8,8192]{2,1,0:T(8,128)(2,1)S(1)}, bf16[1,8,8192]{2,1,0:T(8,128)(2,1)S(1)}, u32[]{:S(2)}, u32[]{:S(2)}) collective-permute-start(bf16[1,8,8192]{2,1,0:T(8,128)(2,1)S(1)} %collective-permute-done.2), channel_id=1, source_target_pairs={{0,193},{1,0},{64,1},{65,64},{128,65},{129,128},{192,129},{193,192... | collective-permute-start | bytes 393224 | tf_op jit(solution)/shard_map/ppermute | solution.py:17
  18.2 5.5 %collective-permute-start.17 = (bf16[1,8,8192]{2,1,0:T(8,128)(2,1)S(1)}, bf16[1,8,8192]{2,1,0:T(8,128)(2,1)S(1)}, u32[]{:S(2)}, u32[]{:S(2)}) collective-permute-start(bf16[1,8,8192]{2,1,0:T(8,128)(2,1)S(1)} %collective-permute-done.16), channel_id=1, source_target_pairs={{0,192},{64,0},{128,64},{192,128},{1,193},{65,1},{129,65},{193,129... | collective-permute-start | bytes 393224 | tf_op jit(solution)/shard_map/ppermute | solution.py:17
  21.4 6.6 %collective-permute-start.4 = (bf16[1,8,8192]{2,1,0:T(8,128)(2,1)S(1)}, bf16[1,8,8192]{2,1,0:T(8,128)(2,1)S(1)}, u32[]{:S(2)}, u32[]{:S(2)}) collective-permute-start(bf16[1,8,8192]{2,1,0:T(8,128)(2,1)S(1)} %collective-permute-done.1), channel_id=1, source_target_pairs={{0,64},{64,128},{128,192},{192,0},{1,65},{65,129},{129,193},{193,1... | collective-permute-start | bytes 393224 | tf_op jit(solution)/shard_map/ppermute | solution.py:17
  23.9 11.0 %collective-permute-start.18 = (bf16[4,8,8192]{2,1,0:T(8,128)(2,1)S(1)}, bf16[4,8,8192]{2,1,0:T(8,128)(2,1)S(1)}, u32[]{:S(2)}, u32[]{:S(2)}) collective-permute-start(bf16[4,8,8192]{2,1,0:T(8,128)(2,1)S(1)} %pad_maximum_fusion.1), channel_id=1, source_target_pairs={{0,4},{4,8},{8,12},{12,0},{1,5},{5,9},{9,13},{13,1},{2,6},{6,10},{... | collective-permute-start | bytes 1572872 | tf_op jit(solution)/shard_map/ppermute | solution.py:17
  25.2 9.8 %collective-permute-start.19 = (bf16[4,8,8192]{2,1,0:T(8,128)(2,1)S(1)}, bf16[4,8,8192]{2,1,0:T(8,128)(2,1)S(1)}, u32[]{:S(2)}, u32[]{:S(2)}) collective-permute-start(bf16[4,8,8192]{2,1,0:T(8,128)(2,1)S(1)} %pad_maximum_fusion.1), channel_id=1, source_target_pairs={{0,12},{4,0},{8,4},{12,8},{1,13},{5,1},{9,5},{13,9},{2,14},{6,2},{... | collective-permute-start | bytes 1572872 | tf_op jit(solution)/shard_map/ppermute | solution.py:17
  28.1 10.3 %collective-permute-start.5 = (bf16[4,8,8192]{2,1,0:T(8,128)(2,1)S(1)}, bf16[4,8,8192]{2,1,0:T(8,128)(2,1)S(1)}, u32[]{:S(2)}, u32[]{:S(2)}) collective-permute-start(bf16[4,8,8192]{2,1,0:T(8,128)(2,1)S(1)} %pad_maximum_fusion), channel_id=1, source_target_pairs={{0,16},{16,32},{32,48},{48,0},{1,17},{17,33},{33,49},{49,1},{2,18}... | collective-permute-start | bytes 1572872 | tf_op jit(solution)/shard_map/ppermute | solution.py:17
  29.4 9.9 %collective-permute-start.6 = (bf16[4,8,8192]{2,1,0:T(8,128)(2,1)S(1)}, bf16[4,8,8192]{2,1,0:T(8,128)(2,1)S(1)}, u32[]{:S(2)}, u32[]{:S(2)}) collective-permute-start(bf16[4,8,8192]{2,1,0:T(8,128)(2,1)S(1)} %pad_maximum_fusion), channel_id=1, source_target_pairs={{0,48},{16,0},{32,16},{48,32},{1,49},{17,1},{33,17},{49,33},{2,50}... | collective-permute-start | bytes 1572872 | tf_op jit(solution)/shard_map/ppermute | solution.py:17
  34.9 7.1 %collective-permute-start.20 = (bf16[2,8,8192]{2,1,0:T(8,128)(2,1)S(1)}, bf16[2,8,8192]{2,1,0:T(8,128)(2,1)S(1)}, u32[]{:S(2)}, u32[]{:S(2)}) collective-permute-start(bf16[2,8,8192]{2,1,0:T(8,128)(2,1)S(1)} %slice.46), channel_id=1, source_target_pairs={{0,4},{4,8},{8,12},{12,0},{1,5},{5,9},{9,13},{13,1},{2,6},{6,10},{... | collective-permute-start | bytes 786440 | tf_op jit(solution)/shard_map/ppermute | solution.py:17
  35.0 7.0 %collective-permute-start.21 = (bf16[2,8,8192]{2,1,0:T(8,128)(2,1)S(1)}, bf16[2,8,8192]{2,1,0:T(8,128)(2,1)S(1)}, u32[]{:S(2)}, u32[]{:S(2)}) collective-permute-start(bf16[2,8,8192]{2,1,0:T(8,128)(2,1)S(1)} %slice.47), channel_id=1, source_target_pairs={{0,12},{4,0},{8,4},{12,8},{1,13},{5,1},{9,5},{13,9},{2,14},{6,2},{... | collective-permute-start | bytes 786440 | tf_op jit(solution)/shard_map/ppermute | solution.py:17
  38.4 7.7 %collective-permute-start.7 = (bf16[2,8,8192]{2,1,0:T(8,128)(2,1)S(1)}, bf16[2,8,8192]{2,1,0:T(8,128)(2,1)S(1)}, u32[]{:S(2)}, u32[]{:S(2)}) collective-permute-start(bf16[2,8,8192]{2,1,0:T(8,128)(2,1)S(1)} %slice.41), channel_id=1, source_target_pairs={{0,16},{16,32},{32,48},{48,0},{1,17},{17,33},{33,49},{49,1},{2,18}... | collective-permute-start | bytes 786440 | tf_op jit(solution)/shard_map/ppermute | solution.py:17
  39.3 6.9 %collective-permute-start.8 = (bf16[2,8,8192]{2,1,0:T(8,128)(2,1)S(1)}, bf16[2,8,8192]{2,1,0:T(8,128)(2,1)S(1)}, u32[]{:S(2)}, u32[]{:S(2)}) collective-permute-start(bf16[2,8,8192]{2,1,0:T(8,128)(2,1)S(1)} %slice.42), channel_id=1, source_target_pairs={{0,48},{16,0},{32,16},{48,32},{1,49},{17,1},{33,17},{49,33},{2,50}... | collective-permute-start | bytes 786440 | tf_op jit(solution)/shard_map/ppermute | solution.py:17
  42.0 46.1 %collective-permute-start.22 = (bf16[16,8,8192]{2,1,0:T(8,128)(2,1)S(1)}, bf16[16,8,8192]{2,1,0:T(8,128)(2,1)S(1)}, u32[]{:S(2)}, u32[]{:S(2)}) collective-permute-start(bf16[16,8,8192]{2,1,0:T(8,128)(2,1)S(1)} %constant_dynamic-update-slice_fusion.8), channel_id=1, source_target_pairs={{0,16},{16,32},{32,48},{48,0},{1,17},{17,33},{33,49},{49,1},{2,18}... | collective-permute-start | bytes 6291464 | tf_op jit(solution)/shard_map/ppermute | solution.py:17
  43.3 45.7 %collective-permute-start.24 = (bf16[16,8,8192]{2,1,0:T(8,128)(2,1)S(1)}, bf16[16,8,8192]{2,1,0:T(8,128)(2,1)S(1)}, u32[]{:S(2)}, u32[]{:S(2)}) collective-permute-start(bf16[16,8,8192]{2,1,0:T(8,128)(2,1)S(1)} %constant_dynamic-update-slice_fusion.8), channel_id=1, source_target_pairs={{0,48},{16,0},{32,16},{48,32},{1,49},{17,1},{33,17},{49,33},{2,50}... | collective-permute-start | bytes 6291464 | tf_op jit(solution)/shard_map/ppermute | solution.py:17
  46.2 44.9 %collective-permute-start.9 = (bf16[16,8,8192]{2,1,0:T(8,128)(2,1)S(1)}, bf16[16,8,8192]{2,1,0:T(8,128)(2,1)S(1)}, u32[]{:S(2)}, u32[]{:S(2)}) collective-permute-start(bf16[16,8,8192]{2,1,0:T(8,128)(2,1)S(1)} %constant_dynamic-update-slice_fusion), channel_id=1, source_target_pairs={{0,4},{4,8},{8,12},{12,0},{1,5},{5,9},{9,13},{13,1},{2,6},{6,10},{... | collective-permute-start | bytes 6291464 | tf_op jit(solution)/shard_map/ppermute | solution.py:17
  47.5 45.0 %collective-permute-start.11 = (bf16[16,8,8192]{2,1,0:T(8,128)(2,1)S(1)}, bf16[16,8,8192]{2,1,0:T(8,128)(2,1)S(1)}, u32[]{:S(2)}, u32[]{:S(2)}) collective-permute-start(bf16[16,8,8192]{2,1,0:T(8,128)(2,1)S(1)} %constant_dynamic-update-slice_fusion), channel_id=1, source_target_pairs={{0,12},{4,0},{8,4},{12,8},{1,13},{5,1},{9,5},{13,9},{2,14},{6,2},{... | collective-permute-start | bytes 6291464 | tf_op jit(solution)/shard_map/ppermute | solution.py:17
  88.2 21.5 %collective-permute-start.23 = (bf16[8,8,8192]{2,1,0:T(8,128)(2,1)S(1)}, bf16[8,8,8192]{2,1,0:T(8,128)(2,1)S(1)}, u32[]{:S(2)}, u32[]{:S(2)}) collective-permute-start(bf16[8,8,8192]{2,1,0:T(8,128)(2,1)S(1)} %slice.48), channel_id=1, source_target_pairs={{0,16},{16,32},{32,48},{48,0},{1,17},{17,33},{33,49},{49,1},{2,18}... | collective-permute-start | bytes 3145736 | tf_op jit(solution)/shard_map/ppermute | solution.py:17
  89.1 21.0 %collective-permute-start.25 = (bf16[8,8,8192]{2,1,0:T(8,128)(2,1)S(1)}, bf16[8,8,8192]{2,1,0:T(8,128)(2,1)S(1)}, u32[]{:S(2)}, u32[]{:S(2)}) collective-permute-start(bf16[8,8,8192]{2,1,0:T(8,128)(2,1)S(1)} %slice.49), channel_id=1, source_target_pairs={{0,48},{16,0},{32,16},{48,32},{1,49},{17,1},{33,17},{49,33},{2,50}... | collective-permute-start | bytes 3145736 | tf_op jit(solution)/shard_map/ppermute | solution.py:17
  91.2 18.9 %collective-permute-start.10 = (bf16[8,8,8192]{2,1,0:T(8,128)(2,1)S(1)}, bf16[8,8,8192]{2,1,0:T(8,128)(2,1)S(1)}, u32[]{:S(2)}, u32[]{:S(2)}) collective-permute-start(bf16[8,8,8192]{2,1,0:T(8,128)(2,1)S(1)} %slice.43), channel_id=1, source_target_pairs={{0,4},{4,8},{8,12},{12,0},{1,5},{5,9},{9,13},{13,1},{2,6},{6,10},{... | collective-permute-start | bytes 3145736 | tf_op jit(solution)/shard_map/ppermute | solution.py:17
  92.6 17.4 %collective-permute-start.12 = (bf16[8,8,8192]{2,1,0:T(8,128)(2,1)S(1)}, bf16[8,8,8192]{2,1,0:T(8,128)(2,1)S(1)}, u32[]{:S(2)}, u32[]{:S(2)}) collective-permute-start(bf16[8,8,8192]{2,1,0:T(8,128)(2,1)S(1)} %slice.44), channel_id=1, source_target_pairs={{0,12},{4,0},{8,4},{12,8},{1,13},{5,1},{9,5},{13,9},{2,14},{6,2},{... | collective-permute-start | bytes 3145736 | tf_op jit(solution)/shard_map/ppermute | solution.py:17
  110.0 11.6 %copy-start = (f32[384]{0:T(512)S(1)}, f32[384]{0:T(512)}, u32[]{:S(2)}) copy-start(f32[384]{0:T(512)} %param.5) | copy-start | bytes 4612
  113.0 10.6 %collective-permute-start.26 = (f32[512,512]{1,0:T(8,128)S(1)}, f32[512,512]{1,0:T(8,128)S(1)}, u32[]{:S(2)}, u32[]{:S(2)}) collective-permute-start(f32[512,512]{1,0:T(8,128)S(1)} %shard_map.39.mine), channel_id=1, source_target_pairs={{0,2},{2,0},{1,3},{3,1},{4,6},{6,4},{5,7},{7,5},{8,10},{10,8},{9,1... | collective-permute-start | bytes 3145736 | tf_op jit(solution)/shard_map/ppermute | solution.py:17

commit v3 on v2

--- a/solution.py
+++ b/solution.py
@@ -32,39 +32,16 @@
     return v, left, right, shift(left[:n], axis, 1), shift(right[n:], axis, -1)
 
 
-def add_kernel(offsets, n_parts, *refs):
-    first = offsets == (0,)
-    count = len(offsets) * n_parts
-    a_refs, b_refs = refs[:count], refs[count : 2 * count]
-    stores = refs[2 * count : 2 * count + 2]
-    if first:
-        out, turned = refs[2 * count + 2], refs[2 * count + 3 :]
-        n_out = turned[0].shape[1]
-    else:
-        out, n_out = refs[-1], stores[0].shape[1]
-
-    @pl.when(pl.program_id(0) == 0)
-    def _():
-        if first:
-            out[...] = jnp.zeros_like(out)
-        else:
-            out[...] = refs[2 * count + 2][...]
-
-    def terms(which, parts):
-        store = stores[which][...]
-        if first:
-            store = store.T
-            turned[which][...] = store
-        rows = jnp.concatenate([p[...] for p in parts], 0)
-        product = jnp.dot(rows, store, preferred_element_type=jnp.float32)
-        squares = jnp.zeros((rows.shape[0], LANES), jnp.float32)
-        for i in range(0, rows.shape[1], LANES):
-            wide = rows[:, i : i + LANES].astype(jnp.float32)
-            squares += wide * wide
-        return product, squares
-
-    a_product, a_squares = terms(0, a_refs)
-    b_product, b_squares = terms(1, b_refs)
+def lane_squares(rows):
+    squares = jnp.zeros((rows.shape[0], LANES), jnp.float32)
+    for i in range(0, rows.shape[1], LANES):
+        wide = rows[:, i : i + LANES].astype(jnp.float32)
+        squares += wide * wide
+    return squares
+
+
+def add_rows(out, n_out, offsets, a_terms, b_terms):
+    (a_product, a_squares), (b_product, b_squares) = a_terms, b_terms
     block = a_product.shape[0] // len(offsets)
     strip = block // RING
     for i, offset in enumerate(offsets):
@@ -76,6 +53,52 @@
             source = slice(i * block + j * strip, i * block + (j + 1) * strip)
             out[rows, :n_out] += b_product[source]
             out[rows, n_out:] += b_squares[source]
+
+
+def last_kernel(offset, depth, *refs):
+    count = (len(refs) - 4) // 2
+    a_refs, b_refs = refs[:count], refs[count : 2 * count]
+    a_store, b_store, _, out = refs[2 * count :]
+    n_out = a_store.shape[1]
+
+    def terms(parts, store):
+        product, squares = 0.0, 0.0
+        for k in range(0, store.shape[0], depth):
+            rows = jnp.concatenate([p[:, k : k + depth] for p in parts], 0)
+            product += jnp.dot(rows, store[k : k + depth, :], preferred_element_type=jnp.float32)
+            squares += lane_squares(rows)
+        return product, squares
+
+    add_rows(out, n_out, (offset,), terms(a_refs, a_store), terms(b_refs, b_store))
+
+
+def add_kernel(offsets, n_parts, *refs):
+    first = offsets == (0,)
+    count = len(offsets) * n_parts
+    a_refs, b_refs = refs[:count], refs[count : 2 * count]
+    stores = refs[2 * count : 2 * count + 2]
+    if first:
+        out, turned = refs[2 * count + 2], refs[2 * count + 3 :]
+        n_out = turned[0].shape[1]
+    else:
+        out, n_out = refs[-1], stores[0].shape[1]
+
+    @pl.when(pl.program_id(0) == 0)
+    def _():
+        if first:
+            out[...] = jnp.zeros_like(out)
+        else:
+            out[...] = refs[2 * count + 2][...]
+
+    def terms(which, parts):
+        store = stores[which][...]
+        if first:
+            store = store.T
+            turned[which][...] = store
+        rows = jnp.concatenate([p[...] for p in parts], 0)
+        return jnp.dot(rows, store, preferred_element_type=jnp.float32), lane_squares(rows)
+
+    add_rows(out, n_out, offsets, terms(0, a_refs), terms(1, b_refs))
 
 
 def add_blocks(sums, offsets, a_parts, b_parts, stores, n_out, depth):
@@ -115,6 +138,20 @@
     )(*a_parts, *b_parts, *stores, *earlier)
 
 
+def add_last(sums, offset, a_parts, b_parts, turned, depth):
+    flat = lambda v: v.reshape(-1, v.shape[-1])
+    operands = [flat(v) for v in (*a_parts, *b_parts)] + [*turned, sums]
+    vmem = pl.BlockSpec(memory_space=pltpu.VMEM)
+    return pl.pallas_call(
+        functools.partial(last_kernel, offset, depth),
+        out_shape=jax.ShapeDtypeStruct(sums.shape, sums.dtype),
+        in_specs=[vmem] * len(operands),
+        out_specs=vmem,
+        input_output_aliases={len(operands) - 1: 0},
+        compiler_params=pltpu.CompilerParams(vmem_limit_bytes=26 * 1024 * 1024),
+    )(*operands)
+
+
 def finish_kernel(order, mine, other, weight, out, scaled):
     n_out = out.shape[1]
     for i in range(0, out.shape[0], 64):
@@ -151,7 +188,7 @@
     n_out = store.shape[0]
     sums, *turned = add_blocks(None, (0,), a[:1], b[:1], (store, store), n_out, 1024)
     sums = add_blocks(sums, (1, 2), a[1:3], b[1:3], turned, n_out, 2048)
-    sums = add_blocks(sums, (3,), a[3:], b[3:], turned, n_out, 4096)
+    sums = add_last(sums, 3, a[3:], b[3:], turned, 2048)
     other = shift(sums, "layer", 1)
     order = absolute_order(*(lax.axis_index(n) for n in ("zh", "x", "y")))
     vmem = pl.BlockSpec(memory_space=pltpu.VMEM)

time: 126 us -> 126 us (level)
    pallas_call x3 -> x2, Pallas kernels: 18.2 us -> 15.3 us  [add_blocks(): pl.pallas_call(functools.partial(add_kernel, offsets, len(a_parts) // len...]
    pallas_call x0 -> x1, Pallas kernels: none -> 2.36 us  [add_last(): pl.pallas_call(functools.partial(last_kernel, offset, depth), out_shape=j...]
  transfers between devices with their start and end apart: 27 -> 27, of which waited for: 12 -> 11; matrix products, arithmetic and copies ran while one was open for 1% -> 1% of each run, Pallas kernels for 12% -> 12%
where the time goes in v3:
time: 126 us; the launch traced here: 125 us
  waiting for transfers between devices  56.8 us (45%)
  starting transfers between devices  46.5 us (37%)
  Pallas kernels  19.2 us (15%)
  local copies, waits for them, and re-layouts  1.73 us (1%)
    ppermute x27, waiting for transfers between devices, shift(): return lax.ppermute(v, axis, [(i, (i + by) % size) for i in range(size)])  56.8 us
    ppermute x27, starting transfers between devices, shift(): return lax.ppermute(v, axis, [(i, (i + by) % size) for i in range(size)])  46.5 us
    pallas_call x2, Pallas kernels, add_blocks(): pl.pallas_call(functools.partial(add_kernel, offsets, len(a_parts) // len...  15.3 us
  transfers between devices with their start and end apart: 27, of which 11 were waited for; matrix products, arithmetic and copies ran while one was open for 1% of the time, Pallas kernels for 12%

profile of v3, /device:TPU:1, one launch (start us, length us, event | category | flops | bytes accessed | tf_op | source)
XLA Modules:
  0.0 124.8 jit_solution(1085788156848225922)
XLA Ops:
  0.0 1.0 fusion.5
  1.0 6.5 %collective-permute-start.15 = (bf16[1,8,8192]{2,1,0:T(8,128)(2,1)S(1)}, bf16[1,8,8192]{2,1,0:T(8,128)(2,1)S(1)}, u32[]{:S(2)}, u32[]{:S(2)}) collective-permute-start(bf16[1,8,8192]{2,1,0:T(8,128)(2,1)S(1)} %get-tuple-element.11), channel_id=1, source_target_pairs={{0,193},{1,0},{64,1},{65,64},{128,65},{129,128},{192,129},{193,192... | collective-permute-start | bytes 393224 | tf_op jit(solution)/shard_map/ppermute | solution.py:17
  7.5 2.7 %collective-permute-start.2 = (bf16[1,8,8192]{2,1,0:T(8,128)(2,1)S(1)}, bf16[1,8,8192]{2,1,0:T(8,128)(2,1)S(1)}, u32[]{:S(2)}, u32[]{:S(2)}) collective-permute-start(bf16[1,8,8192]{2,1,0:T(8,128)(2,1)S(1)} %get-tuple-element.14), channel_id=1, source_target_pairs={{0,193},{1,0},{64,1},{65,64},{128,65},{129,128},{192,129},{193,192... | collective-permute-start | bytes 393224 | tf_op jit(solution)/shard_map/ppermute | solution.py:17
  10.2 2.9 %collective-permute-start.16 = (bf16[1,8,8192]{2,1,0:T(8,128)(2,1)S(1)}, bf16[1,8,8192]{2,1,0:T(8,128)(2,1)S(1)}, u32[]{:S(2)}, u32[]{:S(2)}) collective-permute-start(bf16[1,8,8192]{2,1,0:T(8,128)(2,1)S(1)} %collective-permute-done.15), channel_id=1, source_target_pairs={{0,193},{1,0},{64,1},{65,64},{128,65},{129,128},{192,129},{193,192... | collective-permute-start | bytes 393224 | tf_op jit(solution)/shard_map/ppermute | solution.py:17
  13.1 2.5 %collective-permute-done = bf16[1,8,8192]{2,1,0:T(8,128)(2,1)S(1)} collective-permute-done((bf16[1,8,8192]{2,1,0:T(8,128)(2,1)S(1)}, bf16[1,8,8192]{2,1,0:T(8,128)(2,1)S(1)}, u32[]{:S(2)}, u32[]{:S(2)}) %collective-permute-start) | collective-permute-done | bytes 131104 | tf_op jit(solution)/shard_map/ppermute | solution.py:17
  15.6 2.7 %collective-permute-start.3 = (bf16[1,8,8192]{2,1,0:T(8,128)(2,1)S(1)}, bf16[1,8,8192]{2,1,0:T(8,128)(2,1)S(1)}, u32[]{:S(2)}, u32[]{:S(2)}) collective-permute-start(bf16[1,8,8192]{2,1,0:T(8,128)(2,1)S(1)} %collective-permute-done.2), channel_id=1, source_target_pairs={{0,193},{1,0},{64,1},{65,64},{128,65},{129,128},{192,129},{193,192... | collective-permute-start | bytes 393224 | tf_op jit(solution)/shard_map/ppermute | solution.py:17
  18.3 3.1 %collective-permute-done.1 = bf16[1,8,8192]{2,1,0:T(8,128)(2,1)S(1)} collective-permute-done((bf16[1,8,8192]{2,1,0:T(8,128)(2,1)S(1)}, bf16[1,8,8192]{2,1,0:T(8,128)(2,1)S(1)}, u32[]{:S(2)}, u32[]{:S(2)}) %collective-permute-start.1) | collective-permute-done | bytes 131104 | tf_op jit(solution)/shard_map/ppermute | solution.py:17
  21.4 2.4 %collective-permute-done.17 = bf16[1,8,8192]{2,1,0:T(8,128)(2,1)S(1)} collective-permute-done((bf16[1,8,8192]{2,1,0:T(8,128)(2,1)S(1)}, bf16[1,8,8192]{2,1,0:T(8,128)(2,1)S(1)}, u32[]{:S(2)}, u32[]{:S(2)}) %collective-permute-start.17) | collective-permute-done | bytes 131104 | tf_op jit(solution)/shard_map/ppermute | solution.py:17
  23.9 1.4 %collective-permute-start.18 = (bf16[4,8,8192]{2,1,0:T(8,128)(2,1)S(1)}, bf16[4,8,8192]{2,1,0:T(8,128)(2,1)S(1)}, u32[]{:S(2)}, u32[]{:S(2)}) collective-permute-start(bf16[4,8,8192]{2,1,0:T(8,128)(2,1)S(1)} %pad_maximum_fusion.1), channel_id=1, source_target_pairs={{0,4},{4,8},{8,12},{12,0},{1,5},{5,9},{9,13},{13,1},{2,6},{6,10},{... | collective-permute-start | bytes 1572872 | tf_op jit(solution)/shard_map/ppermute | solution.py:17
  25.2 1.5 %collective-permute-start.19 = (bf16[4,8,8192]{2,1,0:T(8,128)(2,1)S(1)}, bf16[4,8,8192]{2,1,0:T(8,128)(2,1)S(1)}, u32[]{:S(2)}, u32[]{:S(2)}) collective-permute-start(bf16[4,8,8192]{2,1,0:T(8,128)(2,1)S(1)} %pad_maximum_fusion.1), channel_id=1, source_target_pairs={{0,12},{4,0},{8,4},{12,8},{1,13},{5,1},{9,5},{13,9},{2,14},{6,2},{... | collective-permute-start | bytes 1572872 | tf_op jit(solution)/shard_map/ppermute | solution.py:17
  26.8 1.2 collective-permute-done.4
  28.1 1.3 %collective-permute-start.5 = (bf16[4,8,8192]{2,1,0:T(8,128)(2,1)S(1)}, bf16[4,8,8192]{2,1,0:T(8,128)(2,1)S(1)}, u32[]{:S(2)}, u32[]{:S(2)}) collective-permute-start(bf16[4,8,8192]{2,1,0:T(8,128)(2,1)S(1)} %pad_maximum_fusion), channel_id=1, source_target_pairs={{0,16},{16,32},{32,48},{48,0},{1,17},{17,33},{33,49},{49,1},{2,18}... | collective-permute-start | bytes 1572872 | tf_op jit(solution)/shard_map/ppermute | solution.py:17
  29.4 1.5 %collective-permute-start.6 = (bf16[4,8,8192]{2,1,0:T(8,128)(2,1)S(1)}, bf16[4,8,8192]{2,1,0:T(8,128)(2,1)S(1)}, u32[]{:S(2)}, u32[]{:S(2)}) collective-permute-start(bf16[4,8,8192]{2,1,0:T(8,128)(2,1)S(1)} %pad_maximum_fusion), channel_id=1, source_target_pairs={{0,48},{16,0},{32,16},{48,32},{1,49},{17,1},{33,17},{49,33},{2,50}... | collective-permute-start | bytes 1572872 | tf_op jit(solution)/shard_map/ppermute | solution.py:17
  30.9 4.0 %collective-permute-done.18 = bf16[4,8,8192]{2,1,0:T(8,128)(2,1)S(1)} collective-permute-done((bf16[4,8,8192]{2,1,0:T(8,128)(2,1)S(1)}, bf16[4,8,8192]{2,1,0:T(8,128)(2,1)S(1)}, u32[]{:S(2)}, u32[]{:S(2)}) %collective-permute-start.18) | collective-permute-done | bytes 524320 | tf_op jit(solution)/shard_map/ppermute | solution.py:17
  35.0 2.9 %collective-permute-start.21 = (bf16[2,8,8192]{2,1,0:T(8,128)(2,1)S(1)}, bf16[2,8,8192]{2,1,0:T(8,128)(2,1)S(1)}, u32[]{:S(2)}, u32[]{:S(2)}) collective-permute-start(bf16[2,8,8192]{2,1,0:T(8,128)(2,1)S(1)} %slice.47), channel_id=1, source_target_pairs={{0,12},{4,0},{8,4},{12,8},{1,13},{5,1},{9,5},{13,9},{2,14},{6,2},{... | collective-permute-start | bytes 786440 | tf_op jit(solution)/shard_map/ppermute | solution.py:17
  39.3 2.0 %collective-permute-start.8 = (bf16[2,8,8192]{2,1,0:T(8,128)(2,1)S(1)}, bf16[2,8,8192]{2,1,0:T(8,128)(2,1)S(1)}, u32[]{:S(2)}, u32[]{:S(2)}) collective-permute-start(bf16[2,8,8192]{2,1,0:T(8,128)(2,1)S(1)} %slice.42), channel_id=1, source_target_pairs={{0,48},{16,0},{32,16},{48,32},{1,49},{17,1},{33,17},{49,33},{2,50}... | collective-permute-start | bytes 786440 | tf_op jit(solution)/shard_map/ppermute | solution.py:17
  42.0 1.3 %collective-permute-start.22 = (bf16[16,8,8192]{2,1,0:T(8,128)(2,1)S(1)}, bf16[16,8,8192]{2,1,0:T(8,128)(2,1)S(1)}, u32[]{:S(2)}, u32[]{:S(2)}) collective-permute-start(bf16[16,8,8192]{2,1,0:T(8,128)(2,1)S(1)} %constant_dynamic-update-slice_fusion.8), channel_id=1, source_target_pairs={{0,16},{16,32},{32,48},{48,0},{1,17},{17,33},{33,49},{49,1},{2,18}... | collective-permute-start | bytes 6291464 | tf_op jit(solution)/shard_map/ppermute | solution.py:17
  43.3 1.5 %collective-permute-start.24 = (bf16[16,8,8192]{2,1,0:T(8,128)(2,1)S(1)}, bf16[16,8,8192]{2,1,0:T(8,128)(2,1)S(1)}, u32[]{:S(2)}, u32[]{:S(2)}) collective-permute-start(bf16[16,8,8192]{2,1,0:T(8,128)(2,1)S(1)} %constant_dynamic-update-slice_fusion.8), channel_id=1, source_target_pairs={{0,48},{16,0},{32,16},{48,32},{1,49},{17,1},{33,17},{49,33},{2,50}... | collective-permute-start | bytes 6291464 | tf_op jit(solution)/shard_map/ppermute | solution.py:17
  44.8 1.3 %collective-permute-done.7 = bf16[2,8,8192]{2,1,0:T(8,128)(2,1)S(1)} collective-permute-done((bf16[2,8,8192]{2,1,0:T(8,128)(2,1)S(1)}, bf16[2,8,8192]{2,1,0:T(8,128)(2,1)S(1)}, u32[]{:S(2)}, u32[]{:S(2)}) %collective-permute-start.7) | collective-permute-done | bytes 262176 | tf_op jit(solution)/shard_map/ppermute | solution.py:17
  46.2 1.3 %collective-permute-start.9 = (bf16[16,8,8192]{2,1,0:T(8,128)(2,1)S(1)}, bf16[16,8,8192]{2,1,0:T(8,128)(2,1)S(1)}, u32[]{:S(2)}, u32[]{:S(2)}) collective-permute-start(bf16[16,8,8192]{2,1,0:T(8,128)(2,1)S(1)} %constant_dynamic-update-slice_fusion), channel_id=1, source_target_pairs={{0,4},{4,8},{8,12},{12,0},{1,5},{5,9},{9,13},{13,1},{2,6},{6,10},{... | collective-permute-start | bytes 6291464 | tf_op jit(solution)/shard_map/ppermute | solution.py:17
  47.5 1.6 %collective-permute-start.11 = (bf16[16,8,8192]{2,1,0:T(8,128)(2,1)S(1)}, bf16[16,8,8192]{2,1,0:T(8,128)(2,1)S(1)}, u32[]{:S(2)}, u32[]{:S(2)}) collective-permute-start(bf16[16,8,8192]{2,1,0:T(8,128)(2,1)S(1)} %constant_dynamic-update-slice_fusion), channel_id=1, source_target_pairs={{0,12},{4,0},{8,4},{12,8},{1,13},{5,1},{9,5},{13,9},{2,14},{6,2},{... | collective-permute-start | bytes 6291464 | tf_op jit(solution)/shard_map/ppermute | solution.py:17
  49.1 39.0 %collective-permute-done.22 = bf16[16,8,8192]{2,1,0:T(8,128)(2,1)S(1)} collective-permute-done((bf16[16,8,8192]{2,1,0:T(8,128)(2,1)S(1)}, bf16[16,8,8192]{2,1,0:T(8,128)(2,1)S(1)}, u32[]{:S(2)}, u32[]{:S(2)}) %collective-permute-start.22) | collective-permute-done | bytes 2097184 | tf_op jit(solution)/shard_map/ppermute | solution.py:17
  88.2 0.8 collective-permute-start.23
  89.1 2.0 %collective-permute-start.25 = (bf16[8,8,8192]{2,1,0:T(8,128)(2,1)S(1)}, bf16[8,8,8192]{2,1,0:T(8,128)(2,1)S(1)}, u32[]{:S(2)}, u32[]{:S(2)}) collective-permute-start(bf16[8,8,8192]{2,1,0:T(8,128)(2,1)S(1)} %slice.49), channel_id=1, source_target_pairs={{0,48},{16,0},{32,16},{48,32},{1,49},{17,1},{33,17},{49,33},{2,50}... | collective-permute-start | bytes 3145736 | tf_op jit(solution)/shard_map/ppermute | solution.py:17
  91.2 1.4 %collective-permute-start.10 = (bf16[8,8,8192]{2,1,0:T(8,128)(2,1)S(1)}, bf16[8,8,8192]{2,1,0:T(8,128)(2,1)S(1)}, u32[]{:S(2)}, u32[]{:S(2)}) collective-permute-start(bf16[8,8,8192]{2,1,0:T(8,128)(2,1)S(1)} %slice.43), channel_id=1, source_target_pairs={{0,4},{4,8},{8,12},{12,0},{1,5},{5,9},{9,13},{13,1},{2,6},{6,10},{... | collective-permute-start | bytes 3145736 | tf_op jit(solution)/shard_map/ppermute | solution.py:17
  92.6 1.8 %collective-permute-start.12 = (bf16[8,8,8192]{2,1,0:T(8,128)(2,1)S(1)}, bf16[8,8,8192]{2,1,0:T(8,128)(2,1)S(1)}, u32[]{:S(2)}, u32[]{:S(2)}) collective-permute-start(bf16[8,8,8192]{2,1,0:T(8,128)(2,1)S(1)} %slice.44), channel_id=1, source_target_pairs={{0,12},{4,0},{8,4},{12,8},{1,13},{5,1},{9,5},{13,9},{2,14},{6,2},{... | collective-permute-start | bytes 3145736 | tf_op jit(solution)/shard_map/ppermute | solution.py:17
  94.4 9.5 %shard_map.37 = (f32[512,512]{1,0:T(8,128)S(1)}, bf16[8192,384]{1,0:T(8,128)(2,1)S(1)}, bf16[8192,384]{1,0:T(8,128)(2,1)S(1)}) custom-call(bf16[128,8192]{1,0:T(8,128)(2,1)S(1)} %bitcast.17, bf16[128,8192]{1,0:T(8,128)(2,1)S(1)} %bitcast.18, bf16[384,16384]{1,0:T(8,128)(2,1)} %bitcast.23, bf16[384,16384]{1,0:T(8,128)(2,1)} %bitcast.24), custom_call_target="tpu_custom_call" | custom-call | flops 1610612736 | bytes 16777216 | tf_op jit(solution)/shard_map/pallas_call | solution.py:126
  104.0 5.8 %shard_map.38.refs_6_ = f32[512,512]{1,0:T(8,128)S(1)} custom-call(bf16[128,8192]{1,0:T(8,128)(2,1)S(1)} %bitcast.15, bf16[128,8192]{1,0:T(8,128)(2,1)S(1)} %bitcast.16, bf16[128,8192]{1,0:T(8,128)(2,1)S(1)} %bitcast.13, bf16[128,8192]{1,0:T(8,128)(2,1)S(1)} %bitcast.14, bf16[8192,384]{1,0:T(8,128)(2,1)S(1)} %get-tuple-element.8.refs_4_, ...), custom_call_target="tpu_custom_call" | custom-call | flops 3221225472 | bytes 20971520 | tf_op jit(solution)/shard_map/pallas_call | solution.py:126
  110.1 2.4 %shard_map.39.mine = f32[512,512]{1,0:T(8,128)S(1)} custom-call(bf16[64,8192]{1,0:T(8,128)(2,1)S(1)} %bitcast.21, bf16[64,8192]{1,0:T(8,128)(2,1)S(1)} %bitcast.22, bf16[64,8192]{1,0:T(8,128)(2,1)S(1)} %bitcast.19, bf16[64,8192]{1,0:T(8,128)(2,1)S(1)} %bitcast.20, bf16[8192,384]{1,0:T(8,128)(2,1)S(1)} %get-tuple-element.8.refs_4_, ...), custom_call_target="tpu_custom_call", output_to_operand_aliasing={{}: (6, {})} | custom-call | tf_op jit(solution)/shard_map/pallas_call | solution.py:145
  112.4 8.6 %collective-permute-start.26 = (f32[512,512]{1,0:T(8,128)S(1)}, f32[512,512]{1,0:T(8,128)S(1)}, u32[]{:S(2)}, u32[]{:S(2)}) collective-permute-start(f32[512,512]{1,0:T(8,128)S(1)} %shard_map.39.mine), channel_id=1, source_target_pairs={{0,2},{2,0},{1,3},{3,1},{4,6},{6,4},{5,7},{7,5},{8,10},{10,8},{9,1... | collective-permute-start | bytes 3145736 | tf_op jit(solution)/shard_map/ppermute | solution.py:17
  121.3 2.0 %collective-permute-done.26.other = f32[512,512]{1,0:T(8,128)S(1)} collective-permute-done((f32[512,512]{1,0:T(8,128)S(1)}, f32[512,512]{1,0:T(8,128)S(1)}, u32[]{:S(2)}, u32[]{:S(2)}) %collective-permute-start.26) | collective-permute-done | bytes 1048608 | tf_op jit(solution)/shard_map/ppermute | solution.py:17
  123.3 1.5 %shard_map.40 = bf16[512,384]{1,0:T(8,128)(2,1)} custom-call(s32[64]{0:T(128)S(1)} %add.94.order, f32[512,512]{1,0:T(8,128)S(1)} %shard_map.39.mine, f32[512,512]{1,0:T(8,128)S(1)} %collective-permute-done.26.other, f32[1,384]{1,0:T(1,128)S(1)} %broadcast_in_dim.19.weight), custom_call_target="tpu_custom_call" | custom-call | tf_op jit(solution)/shard_map/pallas_call | solution.py:195
  (59 shorter events, 3.3 us)
Async XLA Ops:
  1.0 9.2 %collective-permute-start.15 = (bf16[1,8,8192]{2,1,0:T(8,128)(2,1)S(1)}, bf16[1,8,8192]{2,1,0:T(8,128)(2,1)S(1)}, u32[]{:S(2)}, u32[]{:S(2)}) collective-permute-start(bf16[1,8,8192]{2,1,0:T(8,128)(2,1)S(1)} %get-tuple-element.11), channel_id=1, source_target_pairs={{0,193},{1,0},{64,1},{65,64},{128,65},{129,128},{192,129},{193,192... | collective-permute-start | bytes 393224 | tf_op jit(solution)/shard_map/ppermute | solution.py:17
  7.5 5.6 %collective-permute-start.13 = (bf16[1,8,8192]{2,1,0:T(8,128)(2,1)S(1)}, bf16[1,8,8192]{2,1,0:T(8,128)(2,1)S(1)}, u32[]{:S(2)}, u32[]{:S(2)}) collective-permute-start(bf16[1,8,8192]{2,1,0:T(8,128)(2,1)S(1)} %get-tuple-element.11), channel_id=1, source_target_pairs={{0,1},{1,64},{64,65},{65,128},{128,129},{129,192},{192,193},{193,0... | collective-permute-start | bytes 393224 | tf_op jit(solution)/shard_map/ppermute | solution.py:17
  7.5 8.1 %collective-permute-start = (bf16[1,8,8192]{2,1,0:T(8,128)(2,1)S(1)}, bf16[1,8,8192]{2,1,0:T(8,128)(2,1)S(1)}, u32[]{:S(2)}, u32[]{:S(2)}) collective-permute-start(bf16[1,8,8192]{2,1,0:T(8,128)(2,1)S(1)} %get-tuple-element.14), channel_id=1, source_target_pairs={{0,1},{1,64},{64,65},{65,128},{128,129},{129,192},{192,193},{193,0... | collective-permute-start | bytes 393224 | tf_op jit(solution)/shard_map/ppermute | solution.py:17
  7.5 8.1 %collective-permute-start.2 = (bf16[1,8,8192]{2,1,0:T(8,128)(2,1)S(1)}, bf16[1,8,8192]{2,1,0:T(8,128)(2,1)S(1)}, u32[]{:S(2)}, u32[]{:S(2)}) collective-permute-start(bf16[1,8,8192]{2,1,0:T(8,128)(2,1)S(1)} %get-tuple-element.14), channel_id=1, source_target_pairs={{0,193},{1,0},{64,1},{65,64},{128,65},{129,128},{192,129},{193,192... | collective-permute-start | bytes 393224 | tf_op jit(solution)/shard_map/ppermute | solution.py:17
  10.2 8.0 %collective-permute-start.16 = (bf16[1,8,8192]{2,1,0:T(8,128)(2,1)S(1)}, bf16[1,8,8192]{2,1,0:T(8,128)(2,1)S(1)}, u32[]{:S(2)}, u32[]{:S(2)}) collective-permute-start(bf16[1,8,8192]{2,1,0:T(8,128)(2,1)S(1)} %collective-permute-done.15), channel_id=1, source_target_pairs={{0,193},{1,0},{64,1},{65,64},{128,65},{129,128},{192,129},{193,192... | collective-permute-start | bytes 393224 | tf_op jit(solution)/shard_map/ppermute | solution.py:17
  13.1 5.2 %collective-permute-start.14 = (bf16[1,8,8192]{2,1,0:T(8,128)(2,1)S(1)}, bf16[1,8,8192]{2,1,0:T(8,128)(2,1)S(1)}, u32[]{:S(2)}, u32[]{:S(2)}) collective-permute-start(bf16[1,8,8192]{2,1,0:T(8,128)(2,1)S(1)} %collective-permute-done.13), channel_id=1, source_target_pairs={{0,1},{1,64},{64,65},{65,128},{128,129},{129,192},{192,193},{193,0... | collective-permute-start | bytes 393224 | tf_op jit(solution)/shard_map/ppermute | solution.py:17
  15.6 5.8 %collective-permute-start.1 = (bf16[1,8,8192]{2,1,0:T(8,128)(2,1)S(1)}, bf16[1,8,8192]{2,1,0:T(8,128)(2,1)S(1)}, u32[]{:S(2)}, u32[]{:S(2)}) collective-permute-start(bf16[1,8,8192]{2,1,0:T(8,128)(2,1)S(1)} %collective-permute-done), channel_id=1, source_target_pairs={{0,1},{1,64},{64,65},{65,128},{128,129},{129,192},{192,193},{193,0... | collective-permute-start | bytes 393224 | tf_op jit(solution)/shard_map/ppermute | solution.py:17
  15.6 5.8 %collective-permute-start.3 = (bf16[1,8,8192]{2,1,0:T(8,128)(2,1)S(1)}, bf16[1,8,8192]{2,1,0:T(8,128)(2,1)S(1)}, u32[]{:S(2)}, u32[]{:S(2)}) collective-permute-start(bf16[1,8,8192]{2,1,0:T(8,128)(2,1)S(1)} %collective-permute-done.2), channel_id=1, source_target_pairs={{0,193},{1,0},{64,1},{65,64},{128,65},{129,128},{192,129},{193,192... | collective-permute-start | bytes 393224 | tf_op jit(solution)/shard_map/ppermute | solution.py:17
  18.2 5.5 %collective-permute-start.17 = (bf16[1,8,8192]{2,1,0:T(8,128)(2,1)S(1)}, bf16[1,8,8192]{2,1,0:T(8,128)(2,1)S(1)}, u32[]{:S(2)}, u32[]{:S(2)}) collective-permute-start(bf16[1,8,8192]{2,1,0:T(8,128)(2,1)S(1)} %collective-permute-done.16), channel_id=1, source_target_pairs={{0,192},{64,0},{128,64},{192,128},{1,193},{65,1},{129,65},{193,129... | collective-permute-start | bytes 393224 | tf_op jit(solution)/shard_map/ppermute | solution.py:17
  21.4 6.6 %collective-permute-start.4 = (bf16[1,8,8192]{2,1,0:T(8,128)(2,1)S(1)}, bf16[1,8,8192]{2,1,0:T(8,128)(2,1)S(1)}, u32[]{:S(2)}, u32[]{:S(2)}) collective-permute-start(bf16[1,8,8192]{2,1,0:T(8,128)(2,1)S(1)} %collective-permute-done.1), channel_id=1, source_target_pairs={{0,64},{64,128},{128,192},{192,0},{1,65},{65,129},{129,193},{193,1... | collective-permute-start | bytes 393224 | tf_op jit(solution)/shard_map/ppermute | solution.py:17
  23.9 11.0 %collective-permute-start.18 = (bf16[4,8,8192]{2,1,0:T(8,128)(2,1)S(1)}, bf16[4,8,8192]{2,1,0:T(8,128)(2,1)S(1)}, u32[]{:S(2)}, u32[]{:S(2)}) collective-permute-start(bf16[4,8,8192]{2,1,0:T(8,128)(2,1)S(1)} %pad_maximum_fusion.1), channel_id=1, source_target_pairs={{0,4},{4,8},{8,12},{12,0},{1,5},{5,9},{9,13},{13,1},{2,6},{6,10},{... | collective-permute-start | bytes 1572872 | tf_op jit(solution)/shard_map/ppermute | solution.py:17
  25.2 9.8 %collective-permute-start.19 = (bf16[4,8,8192]{2,1,0:T(8,128)(2,1)S(1)}, bf16[4,8,8192]{2,1,0:T(8,128)(2,1)S(1)}, u32[]{:S(2)}, u32[]{:S(2)}) collective-permute-start(bf16[4,8,8192]{2,1,0:T(8,128)(2,1)S(1)} %pad_maximum_fusion.1), channel_id=1, source_target_pairs={{0,12},{4,0},{8,4},{12,8},{1,13},{5,1},{9,5},{13,9},{2,14},{6,2},{... | collective-permute-start | bytes 1572872 | tf_op jit(solution)/shard_map/ppermute | solution.py:17
  28.1 10.3 %collective-permute-start.5 = (bf16[4,8,8192]{2,1,0:T(8,128)(2,1)S(1)}, bf16[4,8,8192]{2,1,0:T(8,128)(2,1)S(1)}, u32[]{:S(2)}, u32[]{:S(2)}) collective-permute-start(bf16[4,8,8192]{2,1,0:T(8,128)(2,1)S(1)} %pad_maximum_fusion), channel_id=1, source_target_pairs={{0,16},{16,32},{32,48},{48,0},{1,17},{17,33},{33,49},{49,1},{2,18}... | collective-permute-start | bytes 1572872 | tf_op jit(solution)/shard_map/ppermute | solution.py:17
  29.4 9.9 %collective-permute-start.6 = (bf16[4,8,8192]{2,1,0:T(8,128)(2,1)S(1)}, bf16[4,8,8192]{2,1,0:T(8,128)(2,1)S(1)}, u32[]{:S(2)}, u32[]{:S(2)}) collective-permute-start(bf16[4,8,8192]{2,1,0:T(8,128)(2,1)S(1)} %pad_maximum_fusion), channel_id=1, source_target_pairs={{0,48},{16,0},{32,16},{48,32},{1,49},{17,1},{33,17},{49,33},{2,50}... | collective-permute-start | bytes 1572872 | tf_op jit(solution)/shard_map/ppermute | solution.py:17
  34.9 7.1 %collective-permute-start.20 = (bf16[2,8,8192]{2,1,0:T(8,128)(2,1)S(1)}, bf16[2,8,8192]{2,1,0:T(8,128)(2,1)S(1)}, u32[]{:S(2)}, u32[]{:S(2)}) collective-permute-start(bf16[2,8,8192]{2,1,0:T(8,128)(2,1)S(1)} %slice.46), channel_id=1, source_target_pairs={{0,4},{4,8},{8,12},{12,0},{1,5},{5,9},{9,13},{13,1},{2,6},{6,10},{... | collective-permute-start | bytes 786440 | tf_op jit(solution)/shard_map/ppermute | solution.py:17
  35.0 7.0 %collective-permute-start.21 = (bf16[2,8,8192]{2,1,0:T(8,128)(2,1)S(1)}, bf16[2,8,8192]{2,1,0:T(8,128)(2,1)S(1)}, u32[]{:S(2)}, u32[]{:S(2)}) collective-permute-start(bf16[2,8,8192]{2,1,0:T(8,128)(2,1)S(1)} %slice.47), channel_id=1, source_target_pairs={{0,12},{4,0},{8,4},{12,8},{1,13},{5,1},{9,5},{13,9},{2,14},{6,2},{... | collective-permute-start | bytes 786440 | tf_op jit(solution)/shard_map/ppermute | solution.py:17
  38.4 7.7 %collective-permute-start.7 = (bf16[2,8,8192]{2,1,0:T(8,128)(2,1)S(1)}, bf16[2,8,8192]{2,1,0:T(8,128)(2,1)S(1)}, u32[]{:S(2)}, u32[]{:S(2)}) collective-permute-start(bf16[2,8,8192]{2,1,0:T(8,128)(2,1)S(1)} %slice.41), channel_id=1, source_target_pairs={{0,16},{16,32},{32,48},{48,0},{1,17},{17,33},{33,49},{49,1},{2,18}... | collective-permute-start | bytes 786440 | tf_op jit(solution)/shard_map/ppermute | solution.py:17
  39.3 6.9 %collective-permute-start.8 = (bf16[2,8,8192]{2,1,0:T(8,128)(2,1)S(1)}, bf16[2,8,8192]{2,1,0:T(8,128)(2,1)S(1)}, u32[]{:S(2)}, u32[]{:S(2)}) collective-permute-start(bf16[2,8,8192]{2,1,0:T(8,128)(2,1)S(1)} %slice.42), channel_id=1, source_target_pairs={{0,48},{16,0},{32,16},{48,32},{1,49},{17,1},{33,17},{49,33},{2,50}... | collective-permute-start | bytes 786440 | tf_op jit(solution)/shard_map/ppermute | solution.py:17
  42.0 46.1 %collective-permute-start.22 = (bf16[16,8,8192]{2,1,0:T(8,128)(2,1)S(1)}, bf16[16,8,8192]{2,1,0:T(8,128)(2,1)S(1)}, u32[]{:S(2)}, u32[]{:S(2)}) collective-permute-start(bf16[16,8,8192]{2,1,0:T(8,128)(2,1)S(1)} %constant_dynamic-update-slice_fusion.8), channel_id=1, source_target_pairs={{0,16},{16,32},{32,48},{48,0},{1,17},{17,33},{33,49},{49,1},{2,18}... | collective-permute-start | bytes 6291464 | tf_op jit(solution)/shard_map/ppermute | solution.py:17
  43.3 45.7 %collective-permute-start.24 = (bf16[16,8,8192]{2,1,0:T(8,128)(2,1)S(1)}, bf16[16,8,8192]{2,1,0:T(8,128)(2,1)S(1)}, u32[]{:S(2)}, u32[]{:S(2)}) collective-permute-start(bf16[16,8,8192]{2,1,0:T(8,128)(2,1)S(1)} %constant_dynamic-update-slice_fusion.8), channel_id=1, source_target_pairs={{0,48},{16,0},{32,16},{48,32},{1,49},{17,1},{33,17},{49,33},{2,50}... | collective-permute-start | bytes 6291464 | tf_op jit(solution)/shard_map/ppermute | solution.py:17
  46.2 44.9 %collective-permute-start.9 = (bf16[16,8,8192]{2,1,0:T(8,128)(2,1)S(1)}, bf16[16,8,8192]{2,1,0:T(8,128)(2,1)S(1)}, u32[]{:S(2)}, u32[]{:S(2)}) collective-permute-start(bf16[16,8,8192]{2,1,0:T(8,128)(2,1)S(1)} %constant_dynamic-update-slice_fusion), channel_id=1, source_target_pairs={{0,4},{4,8},{8,12},{12,0},{1,5},{5,9},{9,13},{13,1},{2,6},{6,10},{... | collective-permute-start | bytes 6291464 | tf_op jit(solution)/shard_map/ppermute | solution.py:17
  47.5 45.0 %collective-permute-start.11 = (bf16[16,8,8192]{2,1,0:T(8,128)(2,1)S(1)}, bf16[16,8,8192]{2,1,0:T(8,128)(2,1)S(1)}, u32[]{:S(2)}, u32[]{:S(2)}) collective-permute-start(bf16[16,8,8192]{2,1,0:T(8,128)(2,1)S(1)} %constant_dynamic-update-slice_fusion), channel_id=1, source_target_pairs={{0,12},{4,0},{8,4},{12,8},{1,13},{5,1},{9,5},{13,9},{2,14},{6,2},{... | collective-permute-start | bytes 6291464 | tf_op jit(solution)/shard_map/ppermute | solution.py:17
  88.2 21.6 %collective-permute-start.23 = (bf16[8,8,8192]{2,1,0:T(8,128)(2,1)S(1)}, bf16[8,8,8192]{2,1,0:T(8,128)(2,1)S(1)}, u32[]{:S(2)}, u32[]{:S(2)}) collective-permute-start(bf16[8,8,8192]{2,1,0:T(8,128)(2,1)S(1)} %slice.48), channel_id=1, source_target_pairs={{0,16},{16,32},{32,48},{48,0},{1,17},{17,33},{33,49},{49,1},{2,18}... | collective-permute-start | bytes 3145736 | tf_op jit(solution)/shard_map/ppermute | solution.py:17
  89.1 21.0 %collective-permute-start.25 = (bf16[8,8,8192]{2,1,0:T(8,128)(2,1)S(1)}, bf16[8,8,8192]{2,1,0:T(8,128)(2,1)S(1)}, u32[]{:S(2)}, u32[]{:S(2)}) collective-permute-start(bf16[8,8,8192]{2,1,0:T(8,128)(2,1)S(1)} %slice.49), channel_id=1, source_target_pairs={{0,48},{16,0},{32,16},{48,32},{1,49},{17,1},{33,17},{49,33},{2,50}... | collective-permute-start | bytes 3145736 | tf_op jit(solution)/shard_map/ppermute | solution.py:17
  91.2 18.9 %collective-permute-start.10 = (bf16[8,8,8192]{2,1,0:T(8,128)(2,1)S(1)}, bf16[8,8,8192]{2,1,0:T(8,128)(2,1)S(1)}, u32[]{:S(2)}, u32[]{:S(2)}) collective-permute-start(bf16[8,8,8192]{2,1,0:T(8,128)(2,1)S(1)} %slice.43), channel_id=1, source_target_pairs={{0,4},{4,8},{8,12},{12,0},{1,5},{5,9},{9,13},{13,1},{2,6},{6,10},{... | collective-permute-start | bytes 3145736 | tf_op jit(solution)/shard_map/ppermute | solution.py:17
  92.6 17.4 %collective-permute-start.12 = (bf16[8,8,8192]{2,1,0:T(8,128)(2,1)S(1)}, bf16[8,8,8192]{2,1,0:T(8,128)(2,1)S(1)}, u32[]{:S(2)}, u32[]{:S(2)}) collective-permute-start(bf16[8,8,8192]{2,1,0:T(8,128)(2,1)S(1)} %slice.44), channel_id=1, source_target_pairs={{0,12},{4,0},{8,4},{12,8},{1,13},{5,1},{9,5},{13,9},{2,14},{6,2},{... | collective-permute-start | bytes 3145736 | tf_op jit(solution)/shard_map/ppermute | solution.py:17
  110.0 11.2 %copy-start = (f32[384]{0:T(512)S(1)}, f32[384]{0:T(512)}, u32[]{:S(2)}) copy-start(f32[384]{0:T(512)} %param.5) | copy-start | bytes 4612
  112.4 10.9 %collective-permute-start.26 = (f32[512,512]{1,0:T(8,128)S(1)}, f32[512,512]{1,0:T(8,128)S(1)}, u32[]{:S(2)}, u32[]{:S(2)}) collective-permute-start(f32[512,512]{1,0:T(8,128)S(1)} %shard_map.39.mine), channel_id=1, source_target_pairs={{0,2},{2,0},{1,3},{3,1},{4,6},{6,4},{5,7},{7,5},{8,10},{10,8},{9,1... | collective-permute-start | bytes 3145736 | tf_op jit(solution)/shard_map/ppermute | solution.py:17

commit v4 on v3

--- a/solution.py
+++ b/solution.py
@@ -186,7 +186,7 @@
     second = jnp.concatenate(ring(b_planes, "y"), 0)
     a, b = ring(first, "y"), ring(second, "x")
     n_out = store.shape[0]
-    sums, *turned = add_blocks(None, (0,), a[:1], b[:1], (store, store), n_out, 1024)
+    sums, *turned = add_blocks(None, (0,), a[:1], b[:1], (store, store), n_out, 2048)
     sums = add_blocks(sums, (1, 2), a[1:3], b[1:3], turned, n_out, 2048)
     sums = add_last(sums, 3, a[3:], b[3:], turned, 2048)
     other = shift(sums, "layer", 1)

time: 126 us -> 126 us (level)
  waiting for transfers between devices: 56.8 us -> 58.7 us
  Pallas kernels: 19.2 us -> 17.4 us
    ppermute x27, waiting for transfers between devices: 56.8 us -> 58.7 us  [shift(): return lax.ppermute(v, axis, [(i, (i + by) % size) for i in range(size)])]
    pallas_call x2, Pallas kernels: 15.3 us -> 13.5 us  [add_blocks(): pl.pallas_call(functools.partial(add_kernel, offsets, len(a_parts) // len...]
  transfers between devices with their start and end apart: 27 -> 27, of which waited for: 11 -> 12; matrix products, arithmetic and copies ran while one was open for 1% -> 1% of each run, Pallas kernels for 12% -> 11%
where the time goes in v4:
time: 126 us; the launch traced here: 125 us
  waiting for transfers between devices  58.7 us (47%)
  starting transfers between devices  46.4 us (37%)
  Pallas kernels  17.4 us (14%)
  local copies, waits for them, and re-layouts  1.73 us (1%)
    ppermute x27, waiting for transfers between devices, shift(): return lax.ppermute(v, axis, [(i, (i + by) % size) for i in range(size)])  58.7 us
    ppermute x27, starting transfers between devices, shift(): return lax.ppermute(v, axis, [(i, (i + by) % size) for i in range(size)])  46.4 us
    pallas_call x2, Pallas kernels, add_blocks(): pl.pallas_call(functools.partial(add_kernel, offsets, len(a_parts) // len...  13.5 us
  transfers between devices with their start and end apart: 27, of which 12 were waited for; matrix products, arithmetic and copies ran while one was open for 1% of the time, Pallas kernels for 11%

profile of v4, /device:TPU:1, one launch (start us, length us, event | category | flops | bytes accessed | tf_op | source)
XLA Modules:
  0.0 124.7 jit_solution(2118000539465303888)
XLA Ops:
  0.0 1.0 fusion.5
  1.0 6.5 %collective-permute-start.15 = (bf16[1,8,8192]{2,1,0:T(8,128)(2,1)S(1)}, bf16[1,8,8192]{2,1,0:T(8,128)(2,1)S(1)}, u32[]{:S(2)}, u32[]{:S(2)}) collective-permute-start(bf16[1,8,8192]{2,1,0:T(8,128)(2,1)S(1)} %get-tuple-element.11), channel_id=1, source_target_pairs={{0,193},{1,0},{64,1},{65,64},{128,65},{129,128},{192,129},{193,192... | collective-permute-start | bytes 393224 | tf_op jit(solution)/shard_map/ppermute | solution.py:17
  7.5 2.7 %collective-permute-start.2 = (bf16[1,8,8192]{2,1,0:T(8,128)(2,1)S(1)}, bf16[1,8,8192]{2,1,0:T(8,128)(2,1)S(1)}, u32[]{:S(2)}, u32[]{:S(2)}) collective-permute-start(bf16[1,8,8192]{2,1,0:T(8,128)(2,1)S(1)} %get-tuple-element.14), channel_id=1, source_target_pairs={{0,193},{1,0},{64,1},{65,64},{128,65},{129,128},{192,129},{193,192... | collective-permute-start | bytes 393224 | tf_op jit(solution)/shard_map/ppermute | solution.py:17
  10.2 2.9 %collective-permute-start.16 = (bf16[1,8,8192]{2,1,0:T(8,128)(2,1)S(1)}, bf16[1,8,8192]{2,1,0:T(8,128)(2,1)S(1)}, u32[]{:S(2)}, u32[]{:S(2)}) collective-permute-start(bf16[1,8,8192]{2,1,0:T(8,128)(2,1)S(1)} %collective-permute-done.15), channel_id=1, source_target_pairs={{0,193},{1,0},{64,1},{65,64},{128,65},{129,128},{192,129},{193,192... | collective-permute-start | bytes 393224 | tf_op jit(solution)/shard_map/ppermute | solution.py:17
  13.1 2.5 %collective-permute-done = bf16[1,8,8192]{2,1,0:T(8,128)(2,1)S(1)} collective-permute-done((bf16[1,8,8192]{2,1,0:T(8,128)(2,1)S(1)}, bf16[1,8,8192]{2,1,0:T(8,128)(2,1)S(1)}, u32[]{:S(2)}, u32[]{:S(2)}) %collective-permute-start) | collective-permute-done | bytes 131104 | tf_op jit(solution)/shard_map/ppermute | solution.py:17
  15.6 2.7 %collective-permute-start.3 = (bf16[1,8,8192]{2,1,0:T(8,128)(2,1)S(1)}, bf16[1,8,8192]{2,1,0:T(8,128)(2,1)S(1)}, u32[]{:S(2)}, u32[]{:S(2)}) collective-permute-start(bf16[1,8,8192]{2,1,0:T(8,128)(2,1)S(1)} %collective-permute-done.2), channel_id=1, source_target_pairs={{0,193},{1,0},{64,1},{65,64},{128,65},{129,128},{192,129},{193,192... | collective-permute-start | bytes 393224 | tf_op jit(solution)/shard_map/ppermute | solution.py:17
  18.3 3.1 %collective-permute-done.1 = bf16[1,8,8192]{2,1,0:T(8,128)(2,1)S(1)} collective-permute-done((bf16[1,8,8192]{2,1,0:T(8,128)(2,1)S(1)}, bf16[1,8,8192]{2,1,0:T(8,128)(2,1)S(1)}, u32[]{:S(2)}, u32[]{:S(2)}) %collective-permute-start.1) | collective-permute-done | bytes 131104 | tf_op jit(solution)/shard_map/ppermute | solution.py:17
  21.4 2.4 %collective-permute-done.17 = bf16[1,8,8192]{2,1,0:T(8,128)(2,1)S(1)} collective-permute-done((bf16[1,8,8192]{2,1,0:T(8,128)(2,1)S(1)}, bf16[1,8,8192]{2,1,0:T(8,128)(2,1)S(1)}, u32[]{:S(2)}, u32[]{:S(2)}) %collective-permute-start.17) | collective-permute-done | bytes 131104 | tf_op jit(solution)/shard_map/ppermute | solution.py:17
  23.9 1.4 %collective-permute-start.18 = (bf16[4,8,8192]{2,1,0:T(8,128)(2,1)S(1)}, bf16[4,8,8192]{2,1,0:T(8,128)(2,1)S(1)}, u32[]{:S(2)}, u32[]{:S(2)}) collective-permute-start(bf16[4,8,8192]{2,1,0:T(8,128)(2,1)S(1)} %pad_maximum_fusion.1), channel_id=1, source_target_pairs={{0,4},{4,8},{8,12},{12,0},{1,5},{5,9},{9,13},{13,1},{2,6},{6,10},{... | collective-permute-start | bytes 1572872 | tf_op jit(solution)/shard_map/ppermute | solution.py:17
  25.2 1.5 %collective-permute-start.19 = (bf16[4,8,8192]{2,1,0:T(8,128)(2,1)S(1)}, bf16[4,8,8192]{2,1,0:T(8,128)(2,1)S(1)}, u32[]{:S(2)}, u32[]{:S(2)}) collective-permute-start(bf16[4,8,8192]{2,1,0:T(8,128)(2,1)S(1)} %pad_maximum_fusion.1), channel_id=1, source_target_pairs={{0,12},{4,0},{8,4},{12,8},{1,13},{5,1},{9,5},{13,9},{2,14},{6,2},{... | collective-permute-start | bytes 1572872 | tf_op jit(solution)/shard_map/ppermute | solution.py:17
  26.8 1.2 collective-permute-done.4
  28.1 1.3 %collective-permute-start.5 = (bf16[4,8,8192]{2,1,0:T(8,128)(2,1)S(1)}, bf16[4,8,8192]{2,1,0:T(8,128)(2,1)S(1)}, u32[]{:S(2)}, u32[]{:S(2)}) collective-permute-start(bf16[4,8,8192]{2,1,0:T(8,128)(2,1)S(1)} %pad_maximum_fusion), channel_id=1, source_target_pairs={{0,16},{16,32},{32,48},{48,0},{1,17},{17,33},{33,49},{49,1},{2,18}... | collective-permute-start | bytes 1572872 | tf_op jit(solution)/shard_map/ppermute | solution.py:17
  29.4 1.5 %collective-permute-start.6 = (bf16[4,8,8192]{2,1,0:T(8,128)(2,1)S(1)}, bf16[4,8,8192]{2,1,0:T(8,128)(2,1)S(1)}, u32[]{:S(2)}, u32[]{:S(2)}) collective-permute-start(bf16[4,8,8192]{2,1,0:T(8,128)(2,1)S(1)} %pad_maximum_fusion), channel_id=1, source_target_pairs={{0,48},{16,0},{32,16},{48,32},{1,49},{17,1},{33,17},{49,33},{2,50}... | collective-permute-start | bytes 1572872 | tf_op jit(solution)/shard_map/ppermute | solution.py:17
  30.9 4.0 %collective-permute-done.18 = bf16[4,8,8192]{2,1,0:T(8,128)(2,1)S(1)} collective-permute-done((bf16[4,8,8192]{2,1,0:T(8,128)(2,1)S(1)}, bf16[4,8,8192]{2,1,0:T(8,128)(2,1)S(1)}, u32[]{:S(2)}, u32[]{:S(2)}) %collective-permute-start.18) | collective-permute-done | bytes 524320 | tf_op jit(solution)/shard_map/ppermute | solution.py:17
  35.0 2.9 %collective-permute-start.21 = (bf16[2,8,8192]{2,1,0:T(8,128)(2,1)S(1)}, bf16[2,8,8192]{2,1,0:T(8,128)(2,1)S(1)}, u32[]{:S(2)}, u32[]{:S(2)}) collective-permute-start(bf16[2,8,8192]{2,1,0:T(8,128)(2,1)S(1)} %slice.47), channel_id=1, source_target_pairs={{0,12},{4,0},{8,4},{12,8},{1,13},{5,1},{9,5},{13,9},{2,14},{6,2},{... | collective-permute-start | bytes 786440 | tf_op jit(solution)/shard_map/ppermute | solution.py:17
  39.3 2.0 %collective-permute-start.8 = (bf16[2,8,8192]{2,1,0:T(8,128)(2,1)S(1)}, bf16[2,8,8192]{2,1,0:T(8,128)(2,1)S(1)}, u32[]{:S(2)}, u32[]{:S(2)}) collective-permute-start(bf16[2,8,8192]{2,1,0:T(8,128)(2,1)S(1)} %slice.42), channel_id=1, source_target_pairs={{0,48},{16,0},{32,16},{48,32},{1,49},{17,1},{33,17},{49,33},{2,50}... | collective-permute-start | bytes 786440 | tf_op jit(solution)/shard_map/ppermute | solution.py:17
  42.0 1.3 %collective-permute-start.22 = (bf16[16,8,8192]{2,1,0:T(8,128)(2,1)S(1)}, bf16[16,8,8192]{2,1,0:T(8,128)(2,1)S(1)}, u32[]{:S(2)}, u32[]{:S(2)}) collective-permute-start(bf16[16,8,8192]{2,1,0:T(8,128)(2,1)S(1)} %constant_dynamic-update-slice_fusion.8), channel_id=1, source_target_pairs={{0,16},{16,32},{32,48},{48,0},{1,17},{17,33},{33,49},{49,1},{2,18}... | collective-permute-start | bytes 6291464 | tf_op jit(solution)/shard_map/ppermute | solution.py:17
  43.3 1.5 %collective-permute-start.24 = (bf16[16,8,8192]{2,1,0:T(8,128)(2,1)S(1)}, bf16[16,8,8192]{2,1,0:T(8,128)(2,1)S(1)}, u32[]{:S(2)}, u32[]{:S(2)}) collective-permute-start(bf16[16,8,8192]{2,1,0:T(8,128)(2,1)S(1)} %constant_dynamic-update-slice_fusion.8), channel_id=1, source_target_pairs={{0,48},{16,0},{32,16},{48,32},{1,49},{17,1},{33,17},{49,33},{2,50}... | collective-permute-start | bytes 6291464 | tf_op jit(solution)/shard_map/ppermute | solution.py:17
  44.8 1.3 %collective-permute-done.7 = bf16[2,8,8192]{2,1,0:T(8,128)(2,1)S(1)} collective-permute-done((bf16[2,8,8192]{2,1,0:T(8,128)(2,1)S(1)}, bf16[2,8,8192]{2,1,0:T(8,128)(2,1)S(1)}, u32[]{:S(2)}, u32[]{:S(2)}) %collective-permute-start.7) | collective-permute-done | bytes 262176 | tf_op jit(solution)/shard_map/ppermute | solution.py:17
  46.2 1.3 %collective-permute-start.9 = (bf16[16,8,8192]{2,1,0:T(8,128)(2,1)S(1)}, bf16[16,8,8192]{2,1,0:T(8,128)(2,1)S(1)}, u32[]{:S(2)}, u32[]{:S(2)}) collective-permute-start(bf16[16,8,8192]{2,1,0:T(8,128)(2,1)S(1)} %constant_dynamic-update-slice_fusion), channel_id=1, source_target_pairs={{0,4},{4,8},{8,12},{12,0},{1,5},{5,9},{9,13},{13,1},{2,6},{6,10},{... | collective-permute-start | bytes 6291464 | tf_op jit(solution)/shard_map/ppermute | solution.py:17
  47.5 1.6 %collective-permute-start.11 = (bf16[16,8,8192]{2,1,0:T(8,128)(2,1)S(1)}, bf16[16,8,8192]{2,1,0:T(8,128)(2,1)S(1)}, u32[]{:S(2)}, u32[]{:S(2)}) collective-permute-start(bf16[16,8,8192]{2,1,0:T(8,128)(2,1)S(1)} %constant_dynamic-update-slice_fusion), channel_id=1, source_target_pairs={{0,12},{4,0},{8,4},{12,8},{1,13},{5,1},{9,5},{13,9},{2,14},{6,2},{... | collective-permute-start | bytes 6291464 | tf_op jit(solution)/shard_map/ppermute | solution.py:17
  49.1 39.0 %collective-permute-done.22 = bf16[16,8,8192]{2,1,0:T(8,128)(2,1)S(1)} collective-permute-done((bf16[16,8,8192]{2,1,0:T(8,128)(2,1)S(1)}, bf16[16,8,8192]{2,1,0:T(8,128)(2,1)S(1)}, u32[]{:S(2)}, u32[]{:S(2)}) %collective-permute-start.22) | collective-permute-done | bytes 2097184 | tf_op jit(solution)/shard_map/ppermute | solution.py:17
  89.1 2.0 %collective-permute-start.25 = (bf16[8,8,8192]{2,1,0:T(8,128)(2,1)S(1)}, bf16[8,8,8192]{2,1,0:T(8,128)(2,1)S(1)}, u32[]{:S(2)}, u32[]{:S(2)}) collective-permute-start(bf16[8,8,8192]{2,1,0:T(8,128)(2,1)S(1)} %slice.49), channel_id=1, source_target_pairs={{0,48},{16,0},{32,16},{48,32},{1,49},{17,1},{33,17},{49,33},{2,50}... | collective-permute-start | bytes 3145736 | tf_op jit(solution)/shard_map/ppermute | solution.py:17
  91.2 1.4 %collective-permute-start.10 = (bf16[8,8,8192]{2,1,0:T(8,128)(2,1)S(1)}, bf16[8,8,8192]{2,1,0:T(8,128)(2,1)S(1)}, u32[]{:S(2)}, u32[]{:S(2)}) collective-permute-start(bf16[8,8,8192]{2,1,0:T(8,128)(2,1)S(1)} %slice.43), channel_id=1, source_target_pairs={{0,4},{4,8},{8,12},{12,0},{1,5},{5,9},{9,13},{13,1},{2,6},{6,10},{... | collective-permute-start | bytes 3145736 | tf_op jit(solution)/shard_map/ppermute | solution.py:17
  92.6 1.8 %collective-permute-start.12 = (bf16[8,8,8192]{2,1,0:T(8,128)(2,1)S(1)}, bf16[8,8,8192]{2,1,0:T(8,128)(2,1)S(1)}, u32[]{:S(2)}, u32[]{:S(2)}) collective-permute-start(bf16[8,8,8192]{2,1,0:T(8,128)(2,1)S(1)} %slice.44), channel_id=1, source_target_pairs={{0,12},{4,0},{8,4},{12,8},{1,13},{5,1},{9,5},{13,9},{2,14},{6,2},{... | collective-permute-start | bytes 3145736 | tf_op jit(solution)/shard_map/ppermute | solution.py:17
  94.4 7.7 %shard_map.37 = (f32[512,512]{1,0:T(8,128)S(1)}, bf16[8192,384]{1,0:T(8,128)(2,1)S(1)}, bf16[8192,384]{1,0:T(8,128)(2,1)S(1)}) custom-call(bf16[128,8192]{1,0:T(8,128)(2,1)S(1)} %bitcast.17, bf16[128,8192]{1,0:T(8,128)(2,1)S(1)} %bitcast.18, bf16[384,16384]{1,0:T(8,128)(2,1)} %bitcast.23, bf16[384,16384]{1,0:T(8,128)(2,1)} %bitcast.24), custom_call_target="tpu_custom_call" | custom-call | flops 1610612736 | bytes 16777216 | tf_op jit(solution)/shard_map/pallas_call | solution.py:126
  102.2 5.8 %shard_map.38.refs_6_ = f32[512,512]{1,0:T(8,128)S(1)} custom-call(bf16[128,8192]{1,0:T(8,128)(2,1)S(1)} %bitcast.15, bf16[128,8192]{1,0:T(8,128)(2,1)S(1)} %bitcast.16, bf16[128,8192]{1,0:T(8,128)(2,1)S(1)} %bitcast.13, bf16[128,8192]{1,0:T(8,128)(2,1)S(1)} %bitcast.14, bf16[8192,384]{1,0:T(8,128)(2,1)S(1)} %get-tuple-element.8.refs_4_, ...), custom_call_target="tpu_custom_call" | custom-call | flops 3221225472 | bytes 20971520 | tf_op jit(solution)/shard_map/pallas_call | solution.py:126
  107.9 1.8 %collective-permute-done.23 = bf16[8,8,8192]{2,1,0:T(8,128)(2,1)S(1)} collective-permute-done((bf16[8,8,8192]{2,1,0:T(8,128)(2,1)S(1)}, bf16[8,8,8192]{2,1,0:T(8,128)(2,1)S(1)}, u32[]{:S(2)}, u32[]{:S(2)}) %collective-permute-start.23) | collective-permute-done | bytes 1048608 | tf_op jit(solution)/shard_map/ppermute | solution.py:17
  110.1 2.4 %shard_map.39.mine = f32[512,512]{1,0:T(8,128)S(1)} custom-call(bf16[64,8192]{1,0:T(8,128)(2,1)S(1)} %bitcast.21, bf16[64,8192]{1,0:T(8,128)(2,1)S(1)} %bitcast.22, bf16[64,8192]{1,0:T(8,128)(2,1)S(1)} %bitcast.19, bf16[64,8192]{1,0:T(8,128)(2,1)S(1)} %bitcast.20, bf16[8192,384]{1,0:T(8,128)(2,1)S(1)} %get-tuple-element.8.refs_4_, ...), custom_call_target="tpu_custom_call", output_to_operand_aliasing={{}: (6, {})} | custom-call | tf_op jit(solution)/shard_map/pallas_call | solution.py:145
  112.4 8.5 %collective-permute-start.26 = (f32[512,512]{1,0:T(8,128)S(1)}, f32[512,512]{1,0:T(8,128)S(1)}, u32[]{:S(2)}, u32[]{:S(2)}) collective-permute-start(f32[512,512]{1,0:T(8,128)S(1)} %shard_map.39.mine), channel_id=1, source_target_pairs={{0,2},{2,0},{1,3},{3,1},{4,6},{6,4},{5,7},{7,5},{8,10},{10,8},{9,1... | collective-permute-start | bytes 3145736 | tf_op jit(solution)/shard_map/ppermute | solution.py:17
  121.2 2.0 %collective-permute-done.26.other = f32[512,512]{1,0:T(8,128)S(1)} collective-permute-done((f32[512,512]{1,0:T(8,128)S(1)}, f32[512,512]{1,0:T(8,128)S(1)}, u32[]{:S(2)}, u32[]{:S(2)}) %collective-permute-start.26) | collective-permute-done | bytes 1048608 | tf_op jit(solution)/shard_map/ppermute | solution.py:17
  123.2 1.5 %shard_map.40 = bf16[512,384]{1,0:T(8,128)(2,1)} custom-call(s32[64]{0:T(128)S(1)} %add.94.order, f32[512,512]{1,0:T(8,128)S(1)} %shard_map.39.mine, f32[512,512]{1,0:T(8,128)S(1)} %collective-permute-done.26.other, f32[1,384]{1,0:T(1,128)S(1)} %broadcast_in_dim.19.weight), custom_call_target="tpu_custom_call" | custom-call | tf_op jit(solution)/shard_map/pallas_call | solution.py:195
  (59 shorter events, 4.2 us)
Async XLA Ops:
  1.0 9.2 %collective-permute-start.15 = (bf16[1,8,8192]{2,1,0:T(8,128)(2,1)S(1)}, bf16[1,8,8192]{2,1,0:T(8,128)(2,1)S(1)}, u32[]{:S(2)}, u32[]{:S(2)}) collective-permute-start(bf16[1,8,8192]{2,1,0:T(8,128)(2,1)S(1)} %get-tuple-element.11), channel_id=1, source_target_pairs={{0,193},{1,0},{64,1},{65,64},{128,65},{129,128},{192,129},{193,192... | collective-permute-start | bytes 393224 | tf_op jit(solution)/shard_map/ppermute | solution.py:17
  7.5 5.6 %collective-permute-start.13 = (bf16[1,8,8192]{2,1,0:T(8,128)(2,1)S(1)}, bf16[1,8,8192]{2,1,0:T(8,128)(2,1)S(1)}, u32[]{:S(2)}, u32[]{:S(2)}) collective-permute-start(bf16[1,8,8192]{2,1,0:T(8,128)(2,1)S(1)} %get-tuple-element.11), channel_id=1, source_target_pairs={{0,1},{1,64},{64,65},{65,128},{128,129},{129,192},{192,193},{193,0... | collective-permute-start | bytes 393224 | tf_op jit(solution)/shard_map/ppermute | solution.py:17
  7.5 8.1 %collective-permute-start = (bf16[1,8,8192]{2,1,0:T(8,128)(2,1)S(1)}, bf16[1,8,8192]{2,1,0:T(8,128)(2,1)S(1)}, u32[]{:S(2)}, u32[]{:S(2)}) collective-permute-start(bf16[1,8,8192]{2,1,0:T(8,128)(2,1)S(1)} %get-tuple-element.14), channel_id=1, source_target_pairs={{0,1},{1,64},{64,65},{65,128},{128,129},{129,192},{192,193},{193,0... | collective-permute-start | bytes 393224 | tf_op jit(solution)/shard_map/ppermute | solution.py:17
  7.5 8.1 %collective-permute-start.2 = (bf16[1,8,8192]{2,1,0:T(8,128)(2,1)S(1)}, bf16[1,8,8192]{2,1,0:T(8,128)(2,1)S(1)}, u32[]{:S(2)}, u32[]{:S(2)}) collective-permute-start(bf16[1,8,8192]{2,1,0:T(8,128)(2,1)S(1)} %get-tuple-element.14), channel_id=1, source_target_pairs={{0,193},{1,0},{64,1},{65,64},{128,65},{129,128},{192,129},{193,192... | collective-permute-start | bytes 393224 | tf_op jit(solution)/shard_map/ppermute | solution.py:17
  10.2 8.0 %collective-permute-start.16 = (bf16[1,8,8192]{2,1,0:T(8,128)(2,1)S(1)}, bf16[1,8,8192]{2,1,0:T(8,128)(2,1)S(1)}, u32[]{:S(2)}, u32[]{:S(2)}) collective-permute-start(bf16[1,8,8192]{2,1,0:T(8,128)(2,1)S(1)} %collective-permute-done.15), channel_id=1, source_target_pairs={{0,193},{1,0},{64,1},{65,64},{128,65},{129,128},{192,129},{193,192... | collective-permute-start | bytes 393224 | tf_op jit(solution)/shard_map/ppermute | solution.py:17
  13.1 5.2 %collective-permute-start.14 = (bf16[1,8,8192]{2,1,0:T(8,128)(2,1)S(1)}, bf16[1,8,8192]{2,1,0:T(8,128)(2,1)S(1)}, u32[]{:S(2)}, u32[]{:S(2)}) collective-permute-start(bf16[1,8,8192]{2,1,0:T(8,128)(2,1)S(1)} %collective-permute-done.13), channel_id=1, source_target_pairs={{0,1},{1,64},{64,65},{65,128},{128,129},{129,192},{192,193},{193,0... | collective-permute-start | bytes 393224 | tf_op jit(solution)/shard_map/ppermute | solution.py:17
  15.6 5.8 %collective-permute-start.1 = (bf16[1,8,8192]{2,1,0:T(8,128)(2,1)S(1)}, bf16[1,8,8192]{2,1,0:T(8,128)(2,1)S(1)}, u32[]{:S(2)}, u32[]{:S(2)}) collective-permute-start(bf16[1,8,8192]{2,1,0:T(8,128)(2,1)S(1)} %collective-permute-done), channel_id=1, source_target_pairs={{0,1},{1,64},{64,65},{65,128},{128,129},{129,192},{192,193},{193,0... | collective-permute-start | bytes 393224 | tf_op jit(solution)/shard_map/ppermute | solution.py:17
  15.6 5.8 %collective-permute-start.3 = (bf16[1,8,8192]{2,1,0:T(8,128)(2,1)S(1)}, bf16[1,8,8192]{2,1,0:T(8,128)(2,1)S(1)}, u32[]{:S(2)}, u32[]{:S(2)}) collective-permute-start(bf16[1,8,8192]{2,1,0:T(8,128)(2,1)S(1)} %collective-permute-done.2), channel_id=1, source_target_pairs={{0,193},{1,0},{64,1},{65,64},{128,65},{129,128},{192,129},{193,192... | collective-permute-start | bytes 393224 | tf_op jit(solution)/shard_map/ppermute | solution.py:17
  18.2 5.5 %collective-permute-start.17 = (bf16[1,8,8192]{2,1,0:T(8,128)(2,1)S(1)}, bf16[1,8,8192]{2,1,0:T(8,128)(2,1)S(1)}, u32[]{:S(2)}, u32[]{:S(2)}) collective-permute-start(bf16[1,8,8192]{2,1,0:T(8,128)(2,1)S(1)} %collective-permute-done.16), channel_id=1, source_target_pairs={{0,192},{64,0},{128,64},{192,128},{1,193},{65,1},{129,65},{193,129... | collective-permute-start | bytes 393224 | tf_op jit(solution)/shard_map/ppermute | solution.py:17
  21.4 6.6 %collective-permute-start.4 = (bf16[1,8,8192]{2,1,0:T(8,128)(2,1)S(1)}, bf16[1,8,8192]{2,1,0:T(8,128)(2,1)S(1)}, u32[]{:S(2)}, u32[]{:S(2)}) collective-permute-start(bf16[1,8,8192]{2,1,0:T(8,128)(2,1)S(1)} %collective-permute-done.1), channel_id=1, source_target_pairs={{0,64},{64,128},{128,192},{192,0},{1,65},{65,129},{129,193},{193,1... | collective-permute-start | bytes 393224 | tf_op jit(solution)/shard_map/ppermute | solution.py:17
  23.9 11.0 %collective-permute-start.18 = (bf16[4,8,8192]{2,1,0:T(8,128)(2,1)S(1)}, bf16[4,8,8192]{2,1,0:T(8,128)(2,1)S(1)}, u32[]{:S(2)}, u32[]{:S(2)}) collective-permute-start(bf16[4,8,8192]{2,1,0:T(8,128)(2,1)S(1)} %pad_maximum_fusion.1), channel_id=1, source_target_pairs={{0,4},{4,8},{8,12},{12,0},{1,5},{5,9},{9,13},{13,1},{2,6},{6,10},{... | collective-permute-start | bytes 1572872 | tf_op jit(solution)/shard_map/ppermute | solution.py:17
  25.2 9.8 %collective-permute-start.19 = (bf16[4,8,8192]{2,1,0:T(8,128)(2,1)S(1)}, bf16[4,8,8192]{2,1,0:T(8,128)(2,1)S(1)}, u32[]{:S(2)}, u32[]{:S(2)}) collective-permute-start(bf16[4,8,8192]{2,1,0:T(8,128)(2,1)S(1)} %pad_maximum_fusion.1), channel_id=1, source_target_pairs={{0,12},{4,0},{8,4},{12,8},{1,13},{5,1},{9,5},{13,9},{2,14},{6,2},{... | collective-permute-start | bytes 1572872 | tf_op jit(solution)/shard_map/ppermute | solution.py:17
  28.1 10.3 %collective-permute-start.5 = (bf16[4,8,8192]{2,1,0:T(8,128)(2,1)S(1)}, bf16[4,8,8192]{2,1,0:T(8,128)(2,1)S(1)}, u32[]{:S(2)}, u32[]{:S(2)}) collective-permute-start(bf16[4,8,8192]{2,1,0:T(8,128)(2,1)S(1)} %pad_maximum_fusion), channel_id=1, source_target_pairs={{0,16},{16,32},{32,48},{48,0},{1,17},{17,33},{33,49},{49,1},{2,18}... | collective-permute-start | bytes 1572872 | tf_op jit(solution)/shard_map/ppermute | solution.py:17
  29.4 9.9 %collective-permute-start.6 = (bf16[4,8,8192]{2,1,0:T(8,128)(2,1)S(1)}, bf16[4,8,8192]{2,1,0:T(8,128)(2,1)S(1)}, u32[]{:S(2)}, u32[]{:S(2)}) collective-permute-start(bf16[4,8,8192]{2,1,0:T(8,128)(2,1)S(1)} %pad_maximum_fusion), channel_id=1, source_target_pairs={{0,48},{16,0},{32,16},{48,32},{1,49},{17,1},{33,17},{49,33},{2,50}... | collective-permute-start | bytes 1572872 | tf_op jit(solution)/shard_map/ppermute | solution.py:17
  34.9 7.1 %collective-permute-start.20 = (bf16[2,8,8192]{2,1,0:T(8,128)(2,1)S(1)}, bf16[2,8,8192]{2,1,0:T(8,128)(2,1)S(1)}, u32[]{:S(2)}, u32[]{:S(2)}) collective-permute-start(bf16[2,8,8192]{2,1,0:T(8,128)(2,1)S(1)} %slice.46), channel_id=1, source_target_pairs={{0,4},{4,8},{8,12},{12,0},{1,5},{5,9},{9,13},{13,1},{2,6},{6,10},{... | collective-permute-start | bytes 786440 | tf_op jit(solution)/shard_map/ppermute | solution.py:17
  35.0 7.0 %collective-permute-start.21 = (bf16[2,8,8192]{2,1,0:T(8,128)(2,1)S(1)}, bf16[2,8,8192]{2,1,0:T(8,128)(2,1)S(1)}, u32[]{:S(2)}, u32[]{:S(2)}) collective-permute-start(bf16[2,8,8192]{2,1,0:T(8,128)(2,1)S(1)} %slice.47), channel_id=1, source_target_pairs={{0,12},{4,0},{8,4},{12,8},{1,13},{5,1},{9,5},{13,9},{2,14},{6,2},{... | collective-permute-start | bytes 786440 | tf_op jit(solution)/shard_map/ppermute | solution.py:17
  38.4 7.7 %collective-permute-start.7 = (bf16[2,8,8192]{2,1,0:T(8,128)(2,1)S(1)}, bf16[2,8,8192]{2,1,0:T(8,128)(2,1)S(1)}, u32[]{:S(2)}, u32[]{:S(2)}) collective-permute-start(bf16[2,8,8192]{2,1,0:T(8,128)(2,1)S(1)} %slice.41), channel_id=1, source_target_pairs={{0,16},{16,32},{32,48},{48,0},{1,17},{17,33},{33,49},{49,1},{2,18}... | collective-permute-start | bytes 786440 | tf_op jit(solution)/shard_map/ppermute | solution.py:17
  39.3 6.9 %collective-permute-start.8 = (bf16[2,8,8192]{2,1,0:T(8,128)(2,1)S(1)}, bf16[2,8,8192]{2,1,0:T(8,128)(2,1)S(1)}, u32[]{:S(2)}, u32[]{:S(2)}) collective-permute-start(bf16[2,8,8192]{2,1,0:T(8,128)(2,1)S(1)} %slice.42), channel_id=1, source_target_pairs={{0,48},{16,0},{32,16},{48,32},{1,49},{17,1},{33,17},{49,33},{2,50}... | collective-permute-start | bytes 786440 | tf_op jit(solution)/shard_map/ppermute | solution.py:17
  42.0 46.1 %collective-permute-start.22 = (bf16[16,8,8192]{2,1,0:T(8,128)(2,1)S(1)}, bf16[16,8,8192]{2,1,0:T(8,128)(2,1)S(1)}, u32[]{:S(2)}, u32[]{:S(2)}) collective-permute-start(bf16[16,8,8192]{2,1,0:T(8,128)(2,1)S(1)} %constant_dynamic-update-slice_fusion.8), channel_id=1, source_target_pairs={{0,16},{16,32},{32,48},{48,0},{1,17},{17,33},{33,49},{49,1},{2,18}... | collective-permute-start | bytes 6291464 | tf_op jit(solution)/shard_map/ppermute | solution.py:17
  43.3 45.7 %collective-permute-start.24 = (bf16[16,8,8192]{2,1,0:T(8,128)(2,1)S(1)}, bf16[16,8,8192]{2,1,0:T(8,128)(2,1)S(1)}, u32[]{:S(2)}, u32[]{:S(2)}) collective-permute-start(bf16[16,8,8192]{2,1,0:T(8,128)(2,1)S(1)} %constant_dynamic-update-slice_fusion.8), channel_id=1, source_target_pairs={{0,48},{16,0},{32,16},{48,32},{1,49},{17,1},{33,17},{49,33},{2,50}... | collective-permute-start | bytes 6291464 | tf_op jit(solution)/shard_map/ppermute | solution.py:17
  46.2 44.9 %collective-permute-start.9 = (bf16[16,8,8192]{2,1,0:T(8,128)(2,1)S(1)}, bf16[16,8,8192]{2,1,0:T(8,128)(2,1)S(1)}, u32[]{:S(2)}, u32[]{:S(2)}) collective-permute-start(bf16[16,8,8192]{2,1,0:T(8,128)(2,1)S(1)} %constant_dynamic-update-slice_fusion), channel_id=1, source_target_pairs={{0,4},{4,8},{8,12},{12,0},{1,5},{5,9},{9,13},{13,1},{2,6},{6,10},{... | collective-permute-start | bytes 6291464 | tf_op jit(solution)/shard_map/ppermute | solution.py:17
  47.5 45.0 %collective-permute-start.11 = (bf16[16,8,8192]{2,1,0:T(8,128)(2,1)S(1)}, bf16[16,8,8192]{2,1,0:T(8,128)(2,1)S(1)}, u32[]{:S(2)}, u32[]{:S(2)}) collective-permute-start(bf16[16,8,8192]{2,1,0:T(8,128)(2,1)S(1)} %constant_dynamic-update-slice_fusion), channel_id=1, source_target_pairs={{0,12},{4,0},{8,4},{12,8},{1,13},{5,1},{9,5},{13,9},{2,14},{6,2},{... | collective-permute-start | bytes 6291464 | tf_op jit(solution)/shard_map/ppermute | solution.py:17
  88.2 21.5 %collective-permute-start.23 = (bf16[8,8,8192]{2,1,0:T(8,128)(2,1)S(1)}, bf16[8,8,8192]{2,1,0:T(8,128)(2,1)S(1)}, u32[]{:S(2)}, u32[]{:S(2)}) collective-permute-start(bf16[8,8,8192]{2,1,0:T(8,128)(2,1)S(1)} %slice.48), channel_id=1, source_target_pairs={{0,16},{16,32},{32,48},{48,0},{1,17},{17,33},{33,49},{49,1},{2,18}... | collective-permute-start | bytes 3145736 | tf_op jit(solution)/shard_map/ppermute | solution.py:17
  89.1 21.0 %collective-permute-start.25 = (bf16[8,8,8192]{2,1,0:T(8,128)(2,1)S(1)}, bf16[8,8,8192]{2,1,0:T(8,128)(2,1)S(1)}, u32[]{:S(2)}, u32[]{:S(2)}) collective-permute-start(bf16[8,8,8192]{2,1,0:T(8,128)(2,1)S(1)} %slice.49), channel_id=1, source_target_pairs={{0,48},{16,0},{32,16},{48,32},{1,49},{17,1},{33,17},{49,33},{2,50}... | collective-permute-start | bytes 3145736 | tf_op jit(solution)/shard_map/ppermute | solution.py:17
  91.2 18.9 %collective-permute-start.10 = (bf16[8,8,8192]{2,1,0:T(8,128)(2,1)S(1)}, bf16[8,8,8192]{2,1,0:T(8,128)(2,1)S(1)}, u32[]{:S(2)}, u32[]{:S(2)}) collective-permute-start(bf16[8,8,8192]{2,1,0:T(8,128)(2,1)S(1)} %slice.43), channel_id=1, source_target_pairs={{0,4},{4,8},{8,12},{12,0},{1,5},{5,9},{9,13},{13,1},{2,6},{6,10},{... | collective-permute-start | bytes 3145736 | tf_op jit(solution)/shard_map/ppermute | solution.py:17
  92.6 17.4 %collective-permute-start.12 = (bf16[8,8,8192]{2,1,0:T(8,128)(2,1)S(1)}, bf16[8,8,8192]{2,1,0:T(8,128)(2,1)S(1)}, u32[]{:S(2)}, u32[]{:S(2)}) collective-permute-start(bf16[8,8,8192]{2,1,0:T(8,128)(2,1)S(1)} %slice.44), channel_id=1, source_target_pairs={{0,12},{4,0},{8,4},{12,8},{1,13},{5,1},{9,5},{13,9},{2,14},{6,2},{... | collective-permute-start | bytes 3145736 | tf_op jit(solution)/shard_map/ppermute | solution.py:17
  110.0 11.2 %copy-start = (f32[384]{0:T(512)S(1)}, f32[384]{0:T(512)}, u32[]{:S(2)}) copy-start(f32[384]{0:T(512)} %param.5) | copy-start | bytes 4612
  112.4 10.8 %collective-permute-start.26 = (f32[512,512]{1,0:T(8,128)S(1)}, f32[512,512]{1,0:T(8,128)S(1)}, u32[]{:S(2)}, u32[]{:S(2)}) collective-permute-start(f32[512,512]{1,0:T(8,128)S(1)} %shard_map.39.mine), channel_id=1, source_target_pairs={{0,2},{2,0},{1,3},{3,1},{4,6},{6,4},{5,7},{7,5},{8,10},{10,8},{9,1... | collective-permute-start | bytes 3145736 | tf_op jit(solution)/shard_map/ppermute | solution.py:17

commit v5 on v4

--- a/solution.py
+++ b/solution.py
@@ -154,8 +154,8 @@
 
 def finish_kernel(order, mine, other, weight, out, scaled):
     n_out = out.shape[1]
-    for i in range(0, out.shape[0], 64):
-        rows = slice(i, i + 64)
+    for i in range(0, out.shape[0], 128):
+        rows = slice(i, i + 128)
         both = mine[rows, :] + other[rows, :]
         norm = jnp.sum(both[:, n_out:], axis=1, keepdims=True)
         scaled[rows, :] = both[:, :n_out] * weight[...] * lax.rsqrt(norm + 1e-06)

time: 126 us -> 126 us (level)
  no operation moved by 1% of the time
where the time goes in v5:
time: 126 us; the launch traced here: 125 us
  waiting for transfers between devices  58.7 us (47%)
  starting transfers between devices  46.4 us (37%)
  Pallas kernels  17.4 us (14%)
  local copies, waits for them, and re-layouts  1.73 us (1%)
    ppermute x27, waiting for transfers between devices, shift(): return lax.ppermute(v, axis, [(i, (i + by) % size) for i in range(size)])  58.7 us
    ppermute x27, starting transfers between devices, shift(): return lax.ppermute(v, axis, [(i, (i + by) % size) for i in range(size)])  46.4 us
    pallas_call x2, Pallas kernels, add_blocks(): pl.pallas_call(functools.partial(add_kernel, offsets, len(a_parts) // len...  13.5 us
  transfers between devices with their start and end apart: 27, of which 12 were waited for; matrix products, arithmetic and copies ran while one was open for 1% of the time, Pallas kernels for 11%

profile of v5, /device:TPU:1, one launch (start us, length us, event | category | flops | bytes accessed | tf_op | source)
XLA Modules:
  0.0 124.7 jit_solution(13728260818175404038)
XLA Ops:
  0.0 1.0 fusion.5
  1.0 6.5 %collective-permute-start.15 = (bf16[1,8,8192]{2,1,0:T(8,128)(2,1)S(1)}, bf16[1,8,8192]{2,1,0:T(8,128)(2,1)S(1)}, u32[]{:S(2)}, u32[]{:S(2)}) collective-permute-start(bf16[1,8,8192]{2,1,0:T(8,128)(2,1)S(1)} %get-tuple-element.11), channel_id=1, source_target_pairs={{0,193},{1,0},{64,1},{65,64},{128,65},{129,128},{192,129},{193,192... | collective-permute-start | bytes 393224 | tf_op jit(solution)/shard_map/ppermute | solution.py:17
  7.5 2.7 %collective-permute-start.2 = (bf16[1,8,8192]{2,1,0:T(8,128)(2,1)S(1)}, bf16[1,8,8192]{2,1,0:T(8,128)(2,1)S(1)}, u32[]{:S(2)}, u32[]{:S(2)}) collective-permute-start(bf16[1,8,8192]{2,1,0:T(8,128)(2,1)S(1)} %get-tuple-element.14), channel_id=1, source_target_pairs={{0,193},{1,0},{64,1},{65,64},{128,65},{129,128},{192,129},{193,192... | collective-permute-start | bytes 393224 | tf_op jit(solution)/shard_map/ppermute | solution.py:17
  10.2 2.9 %collective-permute-start.16 = (bf16[1,8,8192]{2,1,0:T(8,128)(2,1)S(1)}, bf16[1,8,8192]{2,1,0:T(8,128)(2,1)S(1)}, u32[]{:S(2)}, u32[]{:S(2)}) collective-permute-start(bf16[1,8,8192]{2,1,0:T(8,128)(2,1)S(1)} %collective-permute-done.15), channel_id=1, source_target_pairs={{0,193},{1,0},{64,1},{65,64},{128,65},{129,128},{192,129},{193,192... | collective-permute-start | bytes 393224 | tf_op jit(solution)/shard_map/ppermute | solution.py:17
  13.1 2.5 %collective-permute-done = bf16[1,8,8192]{2,1,0:T(8,128)(2,1)S(1)} collective-permute-done((bf16[1,8,8192]{2,1,0:T(8,128)(2,1)S(1)}, bf16[1,8,8192]{2,1,0:T(8,128)(2,1)S(1)}, u32[]{:S(2)}, u32[]{:S(2)}) %collective-permute-start) | collective-permute-done | bytes 131104 | tf_op jit(solution)/shard_map/ppermute | solution.py:17
  15.6 2.7 %collective-permute-start.3 = (bf16[1,8,8192]{2,1,0:T(8,128)(2,1)S(1)}, bf16[1,8,8192]{2,1,0:T(8,128)(2,1)S(1)}, u32[]{:S(2)}, u32[]{:S(2)}) collective-permute-start(bf16[1,8,8192]{2,1,0:T(8,128)(2,1)S(1)} %collective-permute-done.2), channel_id=1, source_target_pairs={{0,193},{1,0},{64,1},{65,64},{128,65},{129,128},{192,129},{193,192... | collective-permute-start | bytes 393224 | tf_op jit(solution)/shard_map/ppermute | solution.py:17
  18.3 3.1 %collective-permute-done.1 = bf16[1,8,8192]{2,1,0:T(8,128)(2,1)S(1)} collective-permute-done((bf16[1,8,8192]{2,1,0:T(8,128)(2,1)S(1)}, bf16[1,8,8192]{2,1,0:T(8,128)(2,1)S(1)}, u32[]{:S(2)}, u32[]{:S(2)}) %collective-permute-start.1) | collective-permute-done | bytes 131104 | tf_op jit(solution)/shard_map/ppermute | solution.py:17
  21.4 2.4 %collective-permute-done.17 = bf16[1,8,8192]{2,1,0:T(8,128)(2,1)S(1)} collective-permute-done((bf16[1,8,8192]{2,1,0:T(8,128)(2,1)S(1)}, bf16[1,8,8192]{2,1,0:T(8,128)(2,1)S(1)}, u32[]{:S(2)}, u32[]{:S(2)}) %collective-permute-start.17) | collective-permute-done | bytes 131104 | tf_op jit(solution)/shard_map/ppermute | solution.py:17
  23.9 1.4 %collective-permute-start.18 = (bf16[4,8,8192]{2,1,0:T(8,128)(2,1)S(1)}, bf16[4,8,8192]{2,1,0:T(8,128)(2,1)S(1)}, u32[]{:S(2)}, u32[]{:S(2)}) collective-permute-start(bf16[4,8,8192]{2,1,0:T(8,128)(2,1)S(1)} %pad_maximum_fusion.1), channel_id=1, source_target_pairs={{0,4},{4,8},{8,12},{12,0},{1,5},{5,9},{9,13},{13,1},{2,6},{6,10},{... | collective-permute-start | bytes 1572872 | tf_op jit(solution)/shard_map/ppermute | solution.py:17
  25.2 1.5 %collective-permute-start.19 = (bf16[4,8,8192]{2,1,0:T(8,128)(2,1)S(1)}, bf16[4,8,8192]{2,1,0:T(8,128)(2,1)S(1)}, u32[]{:S(2)}, u32[]{:S(2)}) collective-permute-start(bf16[4,8,8192]{2,1,0:T(8,128)(2,1)S(1)} %pad_maximum_fusion.1), channel_id=1, source_target_pairs={{0,12},{4,0},{8,4},{12,8},{1,13},{5,1},{9,5},{13,9},{2,14},{6,2},{... | collective-permute-start | bytes 1572872 | tf_op jit(solution)/shard_map/ppermute | solution.py:17
  26.8 1.2 collective-permute-done.4
  28.1 1.3 %collective-permute-start.5 = (bf16[4,8,8192]{2,1,0:T(8,128)(2,1)S(1)}, bf16[4,8,8192]{2,1,0:T(8,128)(2,1)S(1)}, u32[]{:S(2)}, u32[]{:S(2)}) collective-permute-start(bf16[4,8,8192]{2,1,0:T(8,128)(2,1)S(1)} %pad_maximum_fusion), channel_id=1, source_target_pairs={{0,16},{16,32},{32,48},{48,0},{1,17},{17,33},{33,49},{49,1},{2,18}... | collective-permute-start | bytes 1572872 | tf_op jit(solution)/shard_map/ppermute | solution.py:17
  29.4 1.5 %collective-permute-start.6 = (bf16[4,8,8192]{2,1,0:T(8,128)(2,1)S(1)}, bf16[4,8,8192]{2,1,0:T(8,128)(2,1)S(1)}, u32[]{:S(2)}, u32[]{:S(2)}) collective-permute-start(bf16[4,8,8192]{2,1,0:T(8,128)(2,1)S(1)} %pad_maximum_fusion), channel_id=1, source_target_pairs={{0,48},{16,0},{32,16},{48,32},{1,49},{17,1},{33,17},{49,33},{2,50}... | collective-permute-start | bytes 1572872 | tf_op jit(solution)/shard_map/ppermute | solution.py:17
  30.9 4.0 %collective-permute-done.18 = bf16[4,8,8192]{2,1,0:T(8,128)(2,1)S(1)} collective-permute-done((bf16[4,8,8192]{2,1,0:T(8,128)(2,1)S(1)}, bf16[4,8,8192]{2,1,0:T(8,128)(2,1)S(1)}, u32[]{:S(2)}, u32[]{:S(2)}) %collective-permute-start.18) | collective-permute-done | bytes 524320 | tf_op jit(solution)/shard_map/ppermute | solution.py:17
  35.0 2.9 %collective-permute-start.21 = (bf16[2,8,8192]{2,1,0:T(8,128)(2,1)S(1)}, bf16[2,8,8192]{2,1,0:T(8,128)(2,1)S(1)}, u32[]{:S(2)}, u32[]{:S(2)}) collective-permute-start(bf16[2,8,8192]{2,1,0:T(8,128)(2,1)S(1)} %slice.47), channel_id=1, source_target_pairs={{0,12},{4,0},{8,4},{12,8},{1,13},{5,1},{9,5},{13,9},{2,14},{6,2},{... | collective-permute-start | bytes 786440 | tf_op jit(solution)/shard_map/ppermute | solution.py:17
  39.3 2.0 %collective-permute-start.8 = (bf16[2,8,8192]{2,1,0:T(8,128)(2,1)S(1)}, bf16[2,8,8192]{2,1,0:T(8,128)(2,1)S(1)}, u32[]{:S(2)}, u32[]{:S(2)}) collective-permute-start(bf16[2,8,8192]{2,1,0:T(8,128)(2,1)S(1)} %slice.42), channel_id=1, source_target_pairs={{0,48},{16,0},{32,16},{48,32},{1,49},{17,1},{33,17},{49,33},{2,50}... | collective-permute-start | bytes 786440 | tf_op jit(solution)/shard_map/ppermute | solution.py:17
  42.0 1.3 %collective-permute-start.22 = (bf16[16,8,8192]{2,1,0:T(8,128)(2,1)S(1)}, bf16[16,8,8192]{2,1,0:T(8,128)(2,1)S(1)}, u32[]{:S(2)}, u32[]{:S(2)}) collective-permute-start(bf16[16,8,8192]{2,1,0:T(8,128)(2,1)S(1)} %constant_dynamic-update-slice_fusion.8), channel_id=1, source_target_pairs={{0,16},{16,32},{32,48},{48,0},{1,17},{17,33},{33,49},{49,1},{2,18}... | collective-permute-start | bytes 6291464 | tf_op jit(solution)/shard_map/ppermute | solution.py:17
  43.3 1.5 %collective-permute-start.24 = (bf16[16,8,8192]{2,1,0:T(8,128)(2,1)S(1)}, bf16[16,8,8192]{2,1,0:T(8,128)(2,1)S(1)}, u32[]{:S(2)}, u32[]{:S(2)}) collective-permute-start(bf16[16,8,8192]{2,1,0:T(8,128)(2,1)S(1)} %constant_dynamic-update-slice_fusion.8), channel_id=1, source_target_pairs={{0,48},{16,0},{32,16},{48,32},{1,49},{17,1},{33,17},{49,33},{2,50}... | collective-permute-start | bytes 6291464 | tf_op jit(solution)/shard_map/ppermute | solution.py:17
  44.8 1.3 %collective-permute-done.7 = bf16[2,8,8192]{2,1,0:T(8,128)(2,1)S(1)} collective-permute-done((bf16[2,8,8192]{2,1,0:T(8,128)(2,1)S(1)}, bf16[2,8,8192]{2,1,0:T(8,128)(2,1)S(1)}, u32[]{:S(2)}, u32[]{:S(2)}) %collective-permute-start.7) | collective-permute-done | bytes 262176 | tf_op jit(solution)/shard_map/ppermute | solution.py:17
  46.2 1.3 %collective-permute-start.9 = (bf16[16,8,8192]{2,1,0:T(8,128)(2,1)S(1)}, bf16[16,8,8192]{2,1,0:T(8,128)(2,1)S(1)}, u32[]{:S(2)}, u32[]{:S(2)}) collective-permute-start(bf16[16,8,8192]{2,1,0:T(8,128)(2,1)S(1)} %constant_dynamic-update-slice_fusion), channel_id=1, source_target_pairs={{0,4},{4,8},{8,12},{12,0},{1,5},{5,9},{9,13},{13,1},{2,6},{6,10},{... | collective-permute-start | bytes 6291464 | tf_op jit(solution)/shard_map/ppermute | solution.py:17
  47.5 1.6 %collective-permute-start.11 = (bf16[16,8,8192]{2,1,0:T(8,128)(2,1)S(1)}, bf16[16,8,8192]{2,1,0:T(8,128)(2,1)S(1)}, u32[]{:S(2)}, u32[]{:S(2)}) collective-permute-start(bf16[16,8,8192]{2,1,0:T(8,128)(2,1)S(1)} %constant_dynamic-update-slice_fusion), channel_id=1, source_target_pairs={{0,12},{4,0},{8,4},{12,8},{1,13},{5,1},{9,5},{13,9},{2,14},{6,2},{... | collective-permute-start | bytes 6291464 | tf_op jit(solution)/shard_map/ppermute | solution.py:17
  49.1 39.0 %collective-permute-done.22 = bf16[16,8,8192]{2,1,0:T(8,128)(2,1)S(1)} collective-permute-done((bf16[16,8,8192]{2,1,0:T(8,128)(2,1)S(1)}, bf16[16,8,8192]{2,1,0:T(8,128)(2,1)S(1)}, u32[]{:S(2)}, u32[]{:S(2)}) %collective-permute-start.22) | collective-permute-done | bytes 2097184 | tf_op jit(solution)/shard_map/ppermute | solution.py:17
  89.1 2.0 %collective-permute-start.25 = (bf16[8,8,8192]{2,1,0:T(8,128)(2,1)S(1)}, bf16[8,8,8192]{2,1,0:T(8,128)(2,1)S(1)}, u32[]{:S(2)}, u32[]{:S(2)}) collective-permute-start(bf16[8,8,8192]{2,1,0:T(8,128)(2,1)S(1)} %slice.49), channel_id=1, source_target_pairs={{0,48},{16,0},{32,16},{48,32},{1,49},{17,1},{33,17},{49,33},{2,50}... | collective-permute-start | bytes 3145736 | tf_op jit(solution)/shard_map/ppermute | solution.py:17
  91.2 1.4 %collective-permute-start.10 = (bf16[8,8,8192]{2,1,0:T(8,128)(2,1)S(1)}, bf16[8,8,8192]{2,1,0:T(8,128)(2,1)S(1)}, u32[]{:S(2)}, u32[]{:S(2)}) collective-permute-start(bf16[8,8,8192]{2,1,0:T(8,128)(2,1)S(1)} %slice.43), channel_id=1, source_target_pairs={{0,4},{4,8},{8,12},{12,0},{1,5},{5,9},{9,13},{13,1},{2,6},{6,10},{... | collective-permute-start | bytes 3145736 | tf_op jit(solution)/shard_map/ppermute | solution.py:17
  92.6 1.8 %collective-permute-start.12 = (bf16[8,8,8192]{2,1,0:T(8,128)(2,1)S(1)}, bf16[8,8,8192]{2,1,0:T(8,128)(2,1)S(1)}, u32[]{:S(2)}, u32[]{:S(2)}) collective-permute-start(bf16[8,8,8192]{2,1,0:T(8,128)(2,1)S(1)} %slice.44), channel_id=1, source_target_pairs={{0,12},{4,0},{8,4},{12,8},{1,13},{5,1},{9,5},{13,9},{2,14},{6,2},{... | collective-permute-start | bytes 3145736 | tf_op jit(solution)/shard_map/ppermute | solution.py:17
  94.4 7.7 %shard_map.37 = (f32[512,512]{1,0:T(8,128)S(1)}, bf16[8192,384]{1,0:T(8,128)(2,1)S(1)}, bf16[8192,384]{1,0:T(8,128)(2,1)S(1)}) custom-call(bf16[128,8192]{1,0:T(8,128)(2,1)S(1)} %bitcast.17, bf16[128,8192]{1,0:T(8,128)(2,1)S(1)} %bitcast.18, bf16[384,16384]{1,0:T(8,128)(2,1)} %bitcast.23, bf16[384,16384]{1,0:T(8,128)(2,1)} %bitcast.24), custom_call_target="tpu_custom_call" | custom-call | flops 1610612736 | bytes 16777216 | tf_op jit(solution)/shard_map/pallas_call | solution.py:126
  102.2 5.8 %shard_map.38.refs_6_ = f32[512,512]{1,0:T(8,128)S(1)} custom-call(bf16[128,8192]{1,0:T(8,128)(2,1)S(1)} %bitcast.15, bf16[128,8192]{1,0:T(8,128)(2,1)S(1)} %bitcast.16, bf16[128,8192]{1,0:T(8,128)(2,1)S(1)} %bitcast.13, bf16[128,8192]{1,0:T(8,128)(2,1)S(1)} %bitcast.14, bf16[8192,384]{1,0:T(8,128)(2,1)S(1)} %get-tuple-element.8.refs_4_, ...), custom_call_target="tpu_custom_call" | custom-call | flops 3221225472 | bytes 20971520 | tf_op jit(solution)/shard_map/pallas_call | solution.py:126
  107.9 1.8 %collective-permute-done.23 = bf16[8,8,8192]{2,1,0:T(8,128)(2,1)S(1)} collective-permute-done((bf16[8,8,8192]{2,1,0:T(8,128)(2,1)S(1)}, bf16[8,8,8192]{2,1,0:T(8,128)(2,1)S(1)}, u32[]{:S(2)}, u32[]{:S(2)}) %collective-permute-start.23) | collective-permute-done | bytes 1048608 | tf_op jit(solution)/shard_map/ppermute | solution.py:17
  110.1 2.4 %shard_map.39.mine = f32[512,512]{1,0:T(8,128)S(1)} custom-call(bf16[64,8192]{1,0:T(8,128)(2,1)S(1)} %bitcast.21, bf16[64,8192]{1,0:T(8,128)(2,1)S(1)} %bitcast.22, bf16[64,8192]{1,0:T(8,128)(2,1)S(1)} %bitcast.19, bf16[64,8192]{1,0:T(8,128)(2,1)S(1)} %bitcast.20, bf16[8192,384]{1,0:T(8,128)(2,1)S(1)} %get-tuple-element.8.refs_4_, ...), custom_call_target="tpu_custom_call", output_to_operand_aliasing={{}: (6, {})} | custom-call | tf_op jit(solution)/shard_map/pallas_call | solution.py:145
  112.4 8.5 %collective-permute-start.26 = (f32[512,512]{1,0:T(8,128)S(1)}, f32[512,512]{1,0:T(8,128)S(1)}, u32[]{:S(2)}, u32[]{:S(2)}) collective-permute-start(f32[512,512]{1,0:T(8,128)S(1)} %shard_map.39.mine), channel_id=1, source_target_pairs={{0,2},{2,0},{1,3},{3,1},{4,6},{6,4},{5,7},{7,5},{8,10},{10,8},{9,1... | collective-permute-start | bytes 3145736 | tf_op jit(solution)/shard_map/ppermute | solution.py:17
  121.2 2.0 %collective-permute-done.26.other = f32[512,512]{1,0:T(8,128)S(1)} collective-permute-done((f32[512,512]{1,0:T(8,128)S(1)}, f32[512,512]{1,0:T(8,128)S(1)}, u32[]{:S(2)}, u32[]{:S(2)}) %collective-permute-start.26) | collective-permute-done | bytes 1048608 | tf_op jit(solution)/shard_map/ppermute | solution.py:17
  123.2 1.5 %shard_map.40 = bf16[512,384]{1,0:T(8,128)(2,1)} custom-call(s32[64]{0:T(128)S(1)} %add.94.order, f32[512,512]{1,0:T(8,128)S(1)} %shard_map.39.mine, f32[512,512]{1,0:T(8,128)S(1)} %collective-permute-done.26.other, f32[1,384]{1,0:T(1,128)S(1)} %broadcast_in_dim.19.weight), custom_call_target="tpu_custom_call" | custom-call | tf_op jit(solution)/shard_map/pallas_call | solution.py:195
  (59 shorter events, 4.2 us)
Async XLA Ops:
  1.0 9.2 %collective-permute-start.15 = (bf16[1,8,8192]{2,1,0:T(8,128)(2,1)S(1)}, bf16[1,8,8192]{2,1,0:T(8,128)(2,1)S(1)}, u32[]{:S(2)}, u32[]{:S(2)}) collective-permute-start(bf16[1,8,8192]{2,1,0:T(8,128)(2,1)S(1)} %get-tuple-element.11), channel_id=1, source_target_pairs={{0,193},{1,0},{64,1},{65,64},{128,65},{129,128},{192,129},{193,192... | collective-permute-start | bytes 393224 | tf_op jit(solution)/shard_map/ppermute | solution.py:17
  7.5 5.6 %collective-permute-start.13 = (bf16[1,8,8192]{2,1,0:T(8,128)(2,1)S(1)}, bf16[1,8,8192]{2,1,0:T(8,128)(2,1)S(1)}, u32[]{:S(2)}, u32[]{:S(2)}) collective-permute-start(bf16[1,8,8192]{2,1,0:T(8,128)(2,1)S(1)} %get-tuple-element.11), channel_id=1, source_target_pairs={{0,1},{1,64},{64,65},{65,128},{128,129},{129,192},{192,193},{193,0... | collective-permute-start | bytes 393224 | tf_op jit(solution)/shard_map/ppermute | solution.py:17
  7.5 8.1 %collective-permute-start = (bf16[1,8,8192]{2,1,0:T(8,128)(2,1)S(1)}, bf16[1,8,8192]{2,1,0:T(8,128)(2,1)S(1)}, u32[]{:S(2)}, u32[]{:S(2)}) collective-permute-start(bf16[1,8,8192]{2,1,0:T(8,128)(2,1)S(1)} %get-tuple-element.14), channel_id=1, source_target_pairs={{0,1},{1,64},{64,65},{65,128},{128,129},{129,192},{192,193},{193,0... | collective-permute-start | bytes 393224 | tf_op jit(solution)/shard_map/ppermute | solution.py:17
  7.5 8.1 %collective-permute-start.2 = (bf16[1,8,8192]{2,1,0:T(8,128)(2,1)S(1)}, bf16[1,8,8192]{2,1,0:T(8,128)(2,1)S(1)}, u32[]{:S(2)}, u32[]{:S(2)}) collective-permute-start(bf16[1,8,8192]{2,1,0:T(8,128)(2,1)S(1)} %get-tuple-element.14), channel_id=1, source_target_pairs={{0,193},{1,0},{64,1},{65,64},{128,65},{129,128},{192,129},{193,192... | collective-permute-start | bytes 393224 | tf_op jit(solution)/shard_map/ppermute | solution.py:17
  10.2 8.0 %collective-permute-start.16 = (bf16[1,8,8192]{2,1,0:T(8,128)(2,1)S(1)}, bf16[1,8,8192]{2,1,0:T(8,128)(2,1)S(1)}, u32[]{:S(2)}, u32[]{:S(2)}) collective-permute-start(bf16[1,8,8192]{2,1,0:T(8,128)(2,1)S(1)} %collective-permute-done.15), channel_id=1, source_target_pairs={{0,193},{1,0},{64,1},{65,64},{128,65},{129,128},{192,129},{193,192... | collective-permute-start | bytes 393224 | tf_op jit(solution)/shard_map/ppermute | solution.py:17
  13.1 5.2 %collective-permute-start.14 = (bf16[1,8,8192]{2,1,0:T(8,128)(2,1)S(1)}, bf16[1,8,8192]{2,1,0:T(8,128)(2,1)S(1)}, u32[]{:S(2)}, u32[]{:S(2)}) collective-permute-start(bf16[1,8,8192]{2,1,0:T(8,128)(2,1)S(1)} %collective-permute-done.13), channel_id=1, source_target_pairs={{0,1},{1,64},{64,65},{65,128},{128,129},{129,192},{192,193},{193,0... | collective-permute-start | bytes 393224 | tf_op jit(solution)/shard_map/ppermute | solution.py:17
  15.6 5.8 %collective-permute-start.1 = (bf16[1,8,8192]{2,1,0:T(8,128)(2,1)S(1)}, bf16[1,8,8192]{2,1,0:T(8,128)(2,1)S(1)}, u32[]{:S(2)}, u32[]{:S(2)}) collective-permute-start(bf16[1,8,8192]{2,1,0:T(8,128)(2,1)S(1)} %collective-permute-done), channel_id=1, source_target_pairs={{0,1},{1,64},{64,65},{65,128},{128,129},{129,192},{192,193},{193,0... | collective-permute-start | bytes 393224 | tf_op jit(solution)/shard_map/ppermute | solution.py:17
  15.6 5.8 %collective-permute-start.3 = (bf16[1,8,8192]{2,1,0:T(8,128)(2,1)S(1)}, bf16[1,8,8192]{2,1,0:T(8,128)(2,1)S(1)}, u32[]{:S(2)}, u32[]{:S(2)}) collective-permute-start(bf16[1,8,8192]{2,1,0:T(8,128)(2,1)S(1)} %collective-permute-done.2), channel_id=1, source_target_pairs={{0,193},{1,0},{64,1},{65,64},{128,65},{129,128},{192,129},{193,192... | collective-permute-start | bytes 393224 | tf_op jit(solution)/shard_map/ppermute | solution.py:17
  18.2 5.5 %collective-permute-start.17 = (bf16[1,8,8192]{2,1,0:T(8,128)(2,1)S(1)}, bf16[1,8,8192]{2,1,0:T(8,128)(2,1)S(1)}, u32[]{:S(2)}, u32[]{:S(2)}) collective-permute-start(bf16[1,8,8192]{2,1,0:T(8,128)(2,1)S(1)} %collective-permute-done.16), channel_id=1, source_target_pairs={{0,192},{64,0},{128,64},{192,128},{1,193},{65,1},{129,65},{193,129... | collective-permute-start | bytes 393224 | tf_op jit(solution)/shard_map/ppermute | solution.py:17
  21.4 6.6 %collective-permute-start.4 = (bf16[1,8,8192]{2,1,0:T(8,128)(2,1)S(1)}, bf16[1,8,8192]{2,1,0:T(8,128)(2,1)S(1)}, u32[]{:S(2)}, u32[]{:S(2)}) collective-permute-start(bf16[1,8,8192]{2,1,0:T(8,128)(2,1)S(1)} %collective-permute-done.1), channel_id=1, source_target_pairs={{0,64},{64,128},{128,192},{192,0},{1,65},{65,129},{129,193},{193,1... | collective-permute-start | bytes 393224 | tf_op jit(solution)/shard_map/ppermute | solution.py:17
  23.9 11.0 %collective-permute-start.18 = (bf16[4,8,8192]{2,1,0:T(8,128)(2,1)S(1)}, bf16[4,8,8192]{2,1,0:T(8,128)(2,1)S(1)}, u32[]{:S(2)}, u32[]{:S(2)}) collective-permute-start(bf16[4,8,8192]{2,1,0:T(8,128)(2,1)S(1)} %pad_maximum_fusion.1), channel_id=1, source_target_pairs={{0,4},{4,8},{8,12},{12,0},{1,5},{5,9},{9,13},{13,1},{2,6},{6,10},{... | collective-permute-start | bytes 1572872 | tf_op jit(solution)/shard_map/ppermute | solution.py:17
  25.2 9.8 %collective-permute-start.19 = (bf16[4,8,8192]{2,1,0:T(8,128)(2,1)S(1)}, bf16[4,8,8192]{2,1,0:T(8,128)(2,1)S(1)}, u32[]{:S(2)}, u32[]{:S(2)}) collective-permute-start(bf16[4,8,8192]{2,1,0:T(8,128)(2,1)S(1)} %pad_maximum_fusion.1), channel_id=1, source_target_pairs={{0,12},{4,0},{8,4},{12,8},{1,13},{5,1},{9,5},{13,9},{2,14},{6,2},{... | collective-permute-start | bytes 1572872 | tf_op jit(solution)/shard_map/ppermute | solution.py:17
  28.1 10.3 %collective-permute-start.5 = (bf16[4,8,8192]{2,1,0:T(8,128)(2,1)S(1)}, bf16[4,8,8192]{2,1,0:T(8,128)(2,1)S(1)}, u32[]{:S(2)}, u32[]{:S(2)}) collective-permute-start(bf16[4,8,8192]{2,1,0:T(8,128)(2,1)S(1)} %pad_maximum_fusion), channel_id=1, source_target_pairs={{0,16},{16,32},{32,48},{48,0},{1,17},{17,33},{33,49},{49,1},{2,18}... | collective-permute-start | bytes 1572872 | tf_op jit(solution)/shard_map/ppermute | solution.py:17
  29.4 9.9 %collective-permute-start.6 = (bf16[4,8,8192]{2,1,0:T(8,128)(2,1)S(1)}, bf16[4,8,8192]{2,1,0:T(8,128)(2,1)S(1)}, u32[]{:S(2)}, u32[]{:S(2)}) collective-permute-start(bf16[4,8,8192]{2,1,0:T(8,128)(2,1)S(1)} %pad_maximum_fusion), channel_id=1, source_target_pairs={{0,48},{16,0},{32,16},{48,32},{1,49},{17,1},{33,17},{49,33},{2,50}... | collective-permute-start | bytes 1572872 | tf_op jit(solution)/shard_map/ppermute | solution.py:17
  34.9 7.1 %collective-permute-start.20 = (bf16[2,8,8192]{2,1,0:T(8,128)(2,1)S(1)}, bf16[2,8,8192]{2,1,0:T(8,128)(2,1)S(1)}, u32[]{:S(2)}, u32[]{:S(2)}) collective-permute-start(bf16[2,8,8192]{2,1,0:T(8,128)(2,1)S(1)} %slice.46), channel_id=1, source_target_pairs={{0,4},{4,8},{8,12},{12,0},{1,5},{5,9},{9,13},{13,1},{2,6},{6,10},{... | collective-permute-start | bytes 786440 | tf_op jit(solution)/shard_map/ppermute | solution.py:17
  35.0 7.0 %collective-permute-start.21 = (bf16[2,8,8192]{2,1,0:T(8,128)(2,1)S(1)}, bf16[2,8,8192]{2,1,0:T(8,128)(2,1)S(1)}, u32[]{:S(2)}, u32[]{:S(2)}) collective-permute-start(bf16[2,8,8192]{2,1,0:T(8,128)(2,1)S(1)} %slice.47), channel_id=1, source_target_pairs={{0,12},{4,0},{8,4},{12,8},{1,13},{5,1},{9,5},{13,9},{2,14},{6,2},{... | collective-permute-start | bytes 786440 | tf_op jit(solution)/shard_map/ppermute | solution.py:17
  38.4 7.7 %collective-permute-start.7 = (bf16[2,8,8192]{2,1,0:T(8,128)(2,1)S(1)}, bf16[2,8,8192]{2,1,0:T(8,128)(2,1)S(1)}, u32[]{:S(2)}, u32[]{:S(2)}) collective-permute-start(bf16[2,8,8192]{2,1,0:T(8,128)(2,1)S(1)} %slice.41), channel_id=1, source_target_pairs={{0,16},{16,32},{32,48},{48,0},{1,17},{17,33},{33,49},{49,1},{2,18}... | collective-permute-start | bytes 786440 | tf_op jit(solution)/shard_map/ppermute | solution.py:17
  39.3 6.9 %collective-permute-start.8 = (bf16[2,8,8192]{2,1,0:T(8,128)(2,1)S(1)}, bf16[2,8,8192]{2,1,0:T(8,128)(2,1)S(1)}, u32[]{:S(2)}, u32[]{:S(2)}) collective-permute-start(bf16[2,8,8192]{2,1,0:T(8,128)(2,1)S(1)} %slice.42), channel_id=1, source_target_pairs={{0,48},{16,0},{32,16},{48,32},{1,49},{17,1},{33,17},{49,33},{2,50}... | collective-permute-start | bytes 786440 | tf_op jit(solution)/shard_map/ppermute | solution.py:17
  42.0 46.1 %collective-permute-start.22 = (bf16[16,8,8192]{2,1,0:T(8,128)(2,1)S(1)}, bf16[16,8,8192]{2,1,0:T(8,128)(2,1)S(1)}, u32[]{:S(2)}, u32[]{:S(2)}) collective-permute-start(bf16[16,8,8192]{2,1,0:T(8,128)(2,1)S(1)} %constant_dynamic-update-slice_fusion.8), channel_id=1, source_target_pairs={{0,16},{16,32},{32,48},{48,0},{1,17},{17,33},{33,49},{49,1},{2,18}... | collective-permute-start | bytes 6291464 | tf_op jit(solution)/shard_map/ppermute | solution.py:17
  43.3 45.7 %collective-permute-start.24 = (bf16[16,8,8192]{2,1,0:T(8,128)(2,1)S(1)}, bf16[16,8,8192]{2,1,0:T(8,128)(2,1)S(1)}, u32[]{:S(2)}, u32[]{:S(2)}) collective-permute-start(bf16[16,8,8192]{2,1,0:T(8,128)(2,1)S(1)} %constant_dynamic-update-slice_fusion.8), channel_id=1, source_target_pairs={{0,48},{16,0},{32,16},{48,32},{1,49},{17,1},{33,17},{49,33},{2,50}... | collective-permute-start | bytes 6291464 | tf_op jit(solution)/shard_map/ppermute | solution.py:17
  46.2 44.9 %collective-permute-start.9 = (bf16[16,8,8192]{2,1,0:T(8,128)(2,1)S(1)}, bf16[16,8,8192]{2,1,0:T(8,128)(2,1)S(1)}, u32[]{:S(2)}, u32[]{:S(2)}) collective-permute-start(bf16[16,8,8192]{2,1,0:T(8,128)(2,1)S(1)} %constant_dynamic-update-slice_fusion), channel_id=1, source_target_pairs={{0,4},{4,8},{8,12},{12,0},{1,5},{5,9},{9,13},{13,1},{2,6},{6,10},{... | collective-permute-start | bytes 6291464 | tf_op jit(solution)/shard_map/ppermute | solution.py:17
  47.5 45.0 %collective-permute-start.11 = (bf16[16,8,8192]{2,1,0:T(8,128)(2,1)S(1)}, bf16[16,8,8192]{2,1,0:T(8,128)(2,1)S(1)}, u32[]{:S(2)}, u32[]{:S(2)}) collective-permute-start(bf16[16,8,8192]{2,1,0:T(8,128)(2,1)S(1)} %constant_dynamic-update-slice_fusion), channel_id=1, source_target_pairs={{0,12},{4,0},{8,4},{12,8},{1,13},{5,1},{9,5},{13,9},{2,14},{6,2},{... | collective-permute-start | bytes 6291464 | tf_op jit(solution)/shard_map/ppermute | solution.py:17
  88.2 21.5 %collective-permute-start.23 = (bf16[8,8,8192]{2,1,0:T(8,128)(2,1)S(1)}, bf16[8,8,8192]{2,1,0:T(8,128)(2,1)S(1)}, u32[]{:S(2)}, u32[]{:S(2)}) collective-permute-start(bf16[8,8,8192]{2,1,0:T(8,128)(2,1)S(1)} %slice.48), channel_id=1, source_target_pairs={{0,16},{16,32},{32,48},{48,0},{1,17},{17,33},{33,49},{49,1},{2,18}... | collective-permute-start | bytes 3145736 | tf_op jit(solution)/shard_map/ppermute | solution.py:17
  89.1 21.0 %collective-permute-start.25 = (bf16[8,8,8192]{2,1,0:T(8,128)(2,1)S(1)}, bf16[8,8,8192]{2,1,0:T(8,128)(2,1)S(1)}, u32[]{:S(2)}, u32[]{:S(2)}) collective-permute-start(bf16[8,8,8192]{2,1,0:T(8,128)(2,1)S(1)} %slice.49), channel_id=1, source_target_pairs={{0,48},{16,0},{32,16},{48,32},{1,49},{17,1},{33,17},{49,33},{2,50}... | collective-permute-start | bytes 3145736 | tf_op jit(solution)/shard_map/ppermute | solution.py:17
  91.2 18.9 %collective-permute-start.10 = (bf16[8,8,8192]{2,1,0:T(8,128)(2,1)S(1)}, bf16[8,8,8192]{2,1,0:T(8,128)(2,1)S(1)}, u32[]{:S(2)}, u32[]{:S(2)}) collective-permute-start(bf16[8,8,8192]{2,1,0:T(8,128)(2,1)S(1)} %slice.43), channel_id=1, source_target_pairs={{0,4},{4,8},{8,12},{12,0},{1,5},{5,9},{9,13},{13,1},{2,6},{6,10},{... | collective-permute-start | bytes 3145736 | tf_op jit(solution)/shard_map/ppermute | solution.py:17
  92.6 17.4 %collective-permute-start.12 = (bf16[8,8,8192]{2,1,0:T(8,128)(2,1)S(1)}, bf16[8,8,8192]{2,1,0:T(8,128)(2,1)S(1)}, u32[]{:S(2)}, u32[]{:S(2)}) collective-permute-start(bf16[8,8,8192]{2,1,0:T(8,128)(2,1)S(1)} %slice.44), channel_id=1, source_target_pairs={{0,12},{4,0},{8,4},{12,8},{1,13},{5,1},{9,5},{13,9},{2,14},{6,2},{... | collective-permute-start | bytes 3145736 | tf_op jit(solution)/shard_map/ppermute | solution.py:17
  110.0 11.2 %copy-start = (f32[384]{0:T(512)S(1)}, f32[384]{0:T(512)}, u32[]{:S(2)}) copy-start(f32[384]{0:T(512)} %param.5) | copy-start | bytes 4612
  112.4 10.8 %collective-permute-start.26 = (f32[512,512]{1,0:T(8,128)S(1)}, f32[512,512]{1,0:T(8,128)S(1)}, u32[]{:S(2)}, u32[]{:S(2)}) collective-permute-start(f32[512,512]{1,0:T(8,128)S(1)} %shard_map.39.mine), channel_id=1, source_target_pairs={{0,2},{2,0},{1,3},{3,1},{4,6},{6,4},{5,7},{7,5},{8,10},{10,8},{9,1... | collective-permute-start | bytes 3145736 | tf_op jit(solution)/shard_map/ppermute | solution.py:17
